TPU v7x, 32 devices: a whole 2x2x4 slice. The times are simulated.
32 devices in a mesh: dp: 16 (over z, y, core), grp: 2 (over x).
Axes of the slice: x: 2, y: 2, z: 4, core: 2. Of those that a mesh axis runs over, the one named last changes fastest.
Arguments:
- activations: bfloat16 [8192, 3072], P('dp', 'grp'), may hold values from -125 to 125
- cotangents: bfloat16 [8192, 3072], P('dp', 'grp'), may hold values from -125 to 125
Outputs:
- update: float32 [3072, 3072], P('dp', 'grp')
All inputs are finite; a program needn't handle non-finite values.
Results may differ from a plain program's by a relative error of at most 0.009.
Values may be sent and summed in bfloat16 or wider, within the bound.
A program may use at most 192 MiB of HBM per device.

v0:
```python
import jax
import jax.numpy as jnp
from jax import lax
from jax.sharding import PartitionSpec as P

D = 3072
ITERS = 3


damping = 0.05
epsilon = 1e-06


def row_panel(stacked_tiles):
    return lax.all_gather(stacked_tiles, "grp", axis=2, tiled=True)


def times_columns(panel_rows, stacked_tiles):
    return jnp.einsum(
        "fri,fic->frc",
        panel_rows,
        lax.all_gather(stacked_tiles, "dp", axis=1, tiled=True),
        preferred_element_type=jnp.float32,
    )


def shards(activations, cotangents):
    dp_count = lax.axis_size("dp")
    grp_count = lax.axis_size("grp")
    tile_rows = D // dp_count
    tile_cols = D // grp_count
    dp_index = lax.axis_index("dp")
    grp_index = lax.axis_index("grp")
    whole_inputs, whole_grads = (
        lax.all_gather(activations, "grp", axis=1, tiled=True),
        lax.all_gather(cotangents, "grp", axis=1, tiled=True),
    )
    contract = (((0,), (0,)), ((), ()))
    row_ids = dp_index * tile_rows + lax.iota(jnp.int32, tile_rows)[:, None]
    col_ids = grp_index * tile_cols + lax.iota(jnp.int32, tile_cols)[None, :]
    diag_tile = (row_ids == col_ids).astype(jnp.float32)
    diag_rows = (row_ids == lax.iota(jnp.int32, D)[None, :]).astype(jnp.float32)
    gradient_tile = None
    grads_part = whole_grads
    input_cov = lax.dot_general(
        whole_inputs, activations, contract, preferred_element_type=jnp.float32
    )
    grad_cov = lax.dot_general(grads_part, cotangents, contract, preferred_element_type=jnp.float32)
    input_cov, grad_cov = (input_cov, grad_cov)
    grads_part = whole_grads
    weight_grad = lax.dot_general(
        grads_part, activations, contract, preferred_element_type=jnp.float32
    )
    sum_tiles = lax.psum_scatter(
        jnp.concatenate([input_cov, grad_cov, weight_grad], axis=1),
        "dp",
        scatter_dimension=0,
        tiled=True,
    )
    gradient_tile = sum_tiles[:, 2 * tile_cols :]
    factor_tiles = jnp.stack([sum_tiles[:, :tile_cols], sum_tiles[:, tile_cols : 2 * tile_cols]])
    trace_parts = jnp.sum(factor_tiles * diag_tile[None], axis=(1, 2))
    square_parts = jnp.sum(factor_tiles * factor_tiles, axis=(1, 2))
    trace_sums, square_sums = lax.psum((trace_parts, square_parts), ("dp", "grp"))
    damp_terms = damping * trace_sums / D
    norm_square = square_sums + 2.0 * damp_terms * trace_sums + D * damp_terms * damp_terms
    scale_factors = lax.rsqrt(norm_square)[:, None, None]
    base_tiles = (
        scale_factors * (factor_tiles + damp_terms[:, None, None] * diag_tile[None])
    ).astype(jnp.bfloat16)
    base_rows = row_panel(base_tiles)
    iterate_tiles = (2.0 * diag_tile[None] - base_tiles.astype(jnp.float32)).astype(jnp.bfloat16)
    iterate_rows = (2.0 * diag_rows[None] - base_rows.astype(jnp.float32)).astype(jnp.bfloat16)
    for sweep_index in range(ITERS - 1):
        product = times_columns(base_rows, iterate_tiles)
        product_tiles = product.astype(jnp.bfloat16)
        updated = 2.0 * iterate_tiles.astype(jnp.float32) - times_columns(
            iterate_rows, product_tiles
        )
        iterate_tiles = updated.astype(jnp.bfloat16)
        if sweep_index + 2 < ITERS:
            iterate_rows = row_panel(iterate_tiles)
    inverse_rows = row_panel(iterate_tiles[1:2])
    left_side = times_columns(inverse_rows, gradient_tile.astype(jnp.bfloat16)[None])
    left_tiles = left_side.astype(jnp.bfloat16)
    left_rows = row_panel(left_tiles)
    preconditioned = times_columns(left_rows, iterate_tiles[0:1])[0]
    square_total = lax.psum(jnp.sum(preconditioned * preconditioned), ("dp", "grp"))
    return preconditioned * lax.rsqrt(square_total / (D * D) + epsilon)


def solution(mesh):
    in_specs = (P("dp", "grp"), P("dp", "grp"))
    out_specs = P("dp", "grp")
    return jax.shard_map(shards, mesh=mesh, in_specs=in_specs, out_specs=out_specs, check_vma=False)
```

profile of v0, /device:TPU:0, one launch (start us, length us, event | category | flops | bytes accessed | tf_op | source)
XLA Modules:
  0.0 1544.2 jit_solution(1684799033130425431)
XLA Ops:
  6.5 0.7 all-gather.17.cloned.1.call-update
  7.3 0.0 all-gather.15.cloned.1.call-start
  7.3 0.7 all-gather.15.cloned.1.call-update
  8.0 0.0 reduce-scatter.4.cloned.1.call-start
  8.1 48.5 %all-gather.17.cloned.1.call-done = bf16[512,3072]{1,0:T(8,128)(2,1)} async-done(((bf16[512,1536]{1,0:T(8,128)(2,1)}), bf16[512,3072]{1,0:T(8,128)(2,1)}) %all-gather.17.cloned.1.call-update) | async-done | bytes 3145744 | tf_op jit(solution)/shard_map/all_gather | solution.py:36
  56.6 12.1 fusion.23
  68.7 9.2 fusion.22
  77.9 25.2 %all-gather.15.cloned.1.call-done = bf16[512,3072]{1,0:T(8,128)(2,1)} async-done(((bf16[512,1536]{1,0:T(8,128)(2,1)}), bf16[512,3072]{1,0:T(8,128)(2,1)}) %all-gather.15.cloned.1.call-update) | async-done | bytes 3145744 | tf_op jit(solution)/shard_map/all_gather | solution.py:35
  103.1 10.9 fusion.21
  114.0 36.9 %pad_maximum_fusion = f32[3072,4608]{0,1:T(8,128)} fusion(f32[3072,1536]{0,1:T(8,128)} %fusion.23, f32[3072,1536]{0,1:T(8,128)} %fusion.22, f32[3072,1536]{0,1:T(8,128)} %fusion.21), kind=kLoop, calls=%fused_computation | loop fusion | flops 28311552 | bytes 113246208 | tf_op jit(solution)/shard_map/concatenate | solution.py:55
  150.8 54.9 %copy.14 = f32[3072,4608]{1,0:T(8,128)} copy(f32[3072,4608]{0,1:T(8,128)} %pad_maximum_fusion) | data formatting | bytes 113246208
  205.8 0.0 reduce-scatter.4.cloned.1.call-update
  205.8 0.0 all-gather.19.cloned.1.call-start
  205.9 1.2 compare_select_fusion
  207.0 0.1 compare_convert_fusion
  207.2 518.7 %reduce-scatter.4.cloned.1.call-done = f32[192,4608]{1,0:T(8,128)} async-done(((f32[3072,4608]{1,0:T(8,128)}), f32[192,4608]{1,0:T(8,128)}) %reduce-scatter.4.cloned.1.call-update) | async-done | bytes 3538960 | tf_op jit(solution)/shard_map/reduce_scatter | solution.py:54
  725.8 1.8 slice_bitcast_fusion.1
  727.6 1.0 copy-done.4
  728.7 0.5 multiply_reduce_fusion.1
  729.2 39.3 %all-reduce = (f32[2]{0:T(128)S(1)}, f32[2]{0:T(128)S(1)}) all-reduce(f32[2]{0:T(128)S(1)} %get-tuple-element.6, f32[2]{0:T(128)S(1)} %get-tuple-element.5), channel_id=1, replica_groups=mesh['dp'=16,'grp'=2] {'dp','grp'}, use_global_device_ids=true, to_apply=%region_4.0 | all-reduce | flops 4 | bytes 32 | tf_op jit(solution)/shard_map/psum | solution.py:64
  768.5 3.3 subtract_convert_fusion.2
  771.8 0.0 all-gather.19.cloned.1.call-update
  771.8 0.2 all-gather.21.cloned.1.call-start
  772.0 2.2 copy.9
  774.2 0.0 all-gather.21.cloned.1.call-update
  774.3 0.0 all-gather.23.cloned.1.call-start
  774.3 33.5 %all-gather.19.cloned.1.call-done = bf16[2,192,3072]{2,1,0:T(8,128)(2,1)} async-done(((bf16[2,192,1536]{2,1,0:T(8,128)(2,1)}), bf16[2,192,3072]{2,1,0:T(8,128)(2,1)}) %all-gather.19.cloned.1.call-update) | async-done | bytes 2359312 | tf_op jit(solution)/shard_map/all_gather | solution.py:15
  807.8 100.5 %all-gather.21.cloned.1.call-done = bf16[2,3072,1536]{2,0,1:T(2,128)(2,1)} async-done(((bf16[2,192,1536]{2,0,1:T(2,128)(2,1)}), bf16[2,3072,1536]{2,0,1:T(2,128)(2,1)}) %all-gather.21.cloned.1.call-update) | async-done | bytes 18874384 | tf_op jit(solution)/shard_map/all_gather | solution.py:22
  908.3 11.9 fusion.8
  920.3 0.0 all-gather.23.cloned.1.call-update
  920.3 0.0 all-gather.27.cloned.1.call-start
  920.3 0.3 fusion.15
  920.6 98.8 %all-gather.23.cloned.1.call-done = bf16[2,3072,1536]{2,1,0:T(8,128)(2,1)} async-done(((bf16[2,192,1536]{2,1,0:T(8,128)(2,1)}), bf16[2,3072,1536]{2,1,0:T(8,128)(2,1)}) %all-gather.23.cloned.1.call-update) | async-done | bytes 18874384 | tf_op jit(solution)/shard_map/all_gather | solution.py:22
  1019.4 11.1 fusion.6
  1030.6 2.3 copy.10
  1032.9 0.0 all-gather.27.cloned.1.call-update
  1032.9 0.0 all-gather.25.cloned.1.call-start
  1033.0 0.7 all-gather.25.cloned.1.call-update
  1033.7 0.3 all-gather.29.cloned.1.call-start
  1033.9 98.1 %all-gather.27.cloned.1.call-done = bf16[2,3072,1536]{2,0,1:T(2,128)(2,1)} async-done(((bf16[2,192,1536]{2,0,1:T(2,128)(2,1)}), bf16[2,3072,1536]{2,0,1:T(2,128)(2,1)}) %all-gather.27.cloned.1.call-update) | async-done | bytes 18874384 | tf_op jit(solution)/shard_map/all_gather | solution.py:22
  1132.0 11.2 fusion.11
  1143.2 0.0 all-gather.29.cloned.1.call-update
  1143.2 0.0 all-gather.35.cloned.1.call-start
  1143.3 1.5 slice.24
  1144.8 0.3 copy.16
  1145.0 1.1 copy.11
  1146.1 0.0 all-gather.35.cloned.1.call-update
  1146.1 0.0 all-gather.31.cloned.1.call-start
  1146.2 23.5 %all-gather.25.cloned.1.call-done = bf16[2,192,3072]{2,1,0:T(8,128)(2,1)} async-done(((bf16[2,192,1536]{2,1,0:T(8,128)(2,1)}), bf16[2,192,3072]{2,1,0:T(8,128)(2,1)}) %all-gather.25.cloned.1.call-update) | async-done | bytes 2359312 | tf_op jit(solution)/shard_map/all_gather | solution.py:15
  1169.7 100.6 %all-gather.29.cloned.1.call-done = bf16[2,3072,1536]{2,1,0:T(8,128)(2,1)} async-done(((bf16[2,192,1536]{2,1,0:T(8,128)(2,1)}), bf16[2,3072,1536]{2,1,0:T(8,128)(2,1)}) %all-gather.29.cloned.1.call-update) | async-done | bytes 18874384 | tf_op jit(solution)/shard_map/all_gather | solution.py:22
  1270.4 10.9 fusion.7
  1281.3 1.1 fusion.20
  1282.4 0.0 all-gather.31.cloned.1.call-update
  1282.4 0.0 all-gather.37.cloned.1.call-start
  1282.4 71.8 %all-gather.35.cloned.1.call-done = bf16[3072,1536]{1,0:T(8,128)(2,1)} async-done(((bf16[192,1536]{1,0:T(8,128)(2,1)}), bf16[3072,1536]{1,0:T(8,128)(2,1)}) %all-gather.35.cloned.1.call-update) | async-done | bytes 9437200 | tf_op jit(solution)/shard_map/all_gather | solution.py:22
  1354.2 22.6 %all-gather.31.cloned.1.call-done = bf16[1,192,3072]{2,1,0:T(8,128)(2,1)} async-done(((bf16[1,192,1536]{2,1,0:T(8,128)(2,1)}), bf16[1,192,3072]{2,1,0:T(8,128)(2,1)}) %all-gather.31.cloned.1.call-update) | async-done | bytes 1179664 | tf_op jit(solution)/shard_map/all_gather | solution.py:15
  1376.8 6.9 convolution_convert_fusion
  1383.6 0.0 all-gather.33.cloned.1.call-start
  1383.7 0.7 all-gather.33.cloned.1.call-update
  1384.4 22.2 %all-gather.37.cloned.1.call-done = bf16[192,3072]{1,0:T(8,128)(2,1)} async-done(((bf16[192,1536]{1,0:T(8,128)(2,1)}), bf16[192,3072]{1,0:T(8,128)(2,1)}) %all-gather.37.cloned.1.call-update) | async-done | bytes 1179664 | tf_op jit(solution)/shard_map/all_gather | solution.py:15
  1406.6 84.0 %all-gather.33.cloned.1.call-done = bf16[1,3072,1536]{2,1,0:T(8,128)(2,1)} async-done(((bf16[1,192,1536]{2,1,0:T(8,128)(2,1)}), bf16[1,3072,1536]{2,1,0:T(8,128)(2,1)}) %all-gather.33.cloned.1.call-update) | async-done | bytes 9437200 | tf_op jit(solution)/shard_map/all_gather | solution.py:22
  1490.6 6.7 multiply_reduce_fusion.2
  1497.3 38.5 %psum.23 = f32[]{:T(128)} all-reduce(f32[]{:T(128)} %get-tuple-element.17), channel_id=1, replica_groups=mesh['dp'=16,'grp'=2] {'dp','grp'}, use_global_device_ids=true, to_apply=%region_6.0 | all-reduce | flops 1 | bytes 8 | tf_op jit(solution)/shard_map/psum | solution.py:88
  1536.6 1.1 broadcast_multiply_fusion
  (20 shorter events, 0.1 us)
Async XLA Ops:
  6.5 50.0 %copy-start.6 = (bf16[512,1536]{1,0:T(8,128)(2,1)S(1)}, bf16[512,1536]{1,0:T(8,128)(2,1)}, u32[]{:S(2)}) copy-start(bf16[512,1536]{1,0:T(8,128)(2,1)} %param.2) | copy-start | bytes 4718596
  6.5 50.0 %all-gather.17.cloned.1.call-start = ((), (), s32[]{:S(2)}) async-start(), calls=%async_computation.2 | async-start | bytes 4718592 | tf_op jit(solution)/shard_map/all_gather | solution.py:36
  7.3 95.8 %all-gather.15.cloned.1.call-start = ((), (), s32[]{:S(2)}) async-start(), calls=%async_computation.1 | async-start | bytes 4718592 | tf_op jit(solution)/shard_map/all_gather | solution.py:35
  8.0 60.7 %copy-start.5 = (bf16[512,1536]{1,0:T(8,128)(2,1)S(1)}, bf16[512,1536]{1,0:T(8,128)(2,1)}, u32[]{:S(2)}) copy-start(bf16[512,1536]{1,0:T(8,128)(2,1)} %param.3) | copy-start | bytes 4718596
  8.0 717.8 %reduce-scatter.4.cloned.1.call-start = ((), (), s32[]{:S(2)}) async-start(), calls=%async_computation.13 | async-start | bytes 60162048 | tf_op jit(solution)/shard_map/reduce_scatter | solution.py:54
  56.6 12.1 copy-start.7
  205.8 602.0 %all-gather.19.cloned.1.call-start = ((), (), s32[]{:S(2)}) async-start(), calls=%async_computation.3 | async-start | bytes 3538944 | tf_op jit(solution)/shard_map/all_gather | solution.py:15
  727.6 1.0 copy-start.4
  771.8 2.5 copy-start.3
  771.8 136.5 %all-gather.21.cloned.1.call-start = ((), (), s32[]{:S(2)}) async-start(), calls=%async_computation.4 | async-start | bytes 20054016 | tf_op jit(solution)/shard_map/all_gather | solution.py:22
  774.3 245.1 %all-gather.23.cloned.1.call-start = ((), (), s32[]{:S(2)}) async-start(), calls=%async_computation.5 | async-start | bytes 20054016 | tf_op jit(solution)/shard_map/all_gather | solution.py:22
  920.3 211.7 %all-gather.27.cloned.1.call-start = ((), (), s32[]{:S(2)}) async-start(), calls=%async_computation.7 | async-start | bytes 20054016 | tf_op jit(solution)/shard_map/all_gather | solution.py:22
  1030.5 2.4 copy-start.1
  1030.5 101.5 %copy-start = (bf16[2,192,3072]{2,1,0:T(8,128)(2,1)S(1)}, bf16[2,192,3072]{2,1,0:T(8,128)(2,1)}, u32[]{:S(2)}) copy-start(bf16[2,192,3072]{2,1,0:T(8,128)(2,1)} %all-gather.19.cloned.1.call-done) | copy-start | bytes 7077892
  1032.9 136.8 %all-gather.25.cloned.1.call-start = ((), (), s32[]{:S(2)}) async-start(), calls=%async_computation.6 | async-start | bytes 3538944 | tf_op jit(solution)/shard_map/all_gather | solution.py:15
  1033.7 236.7 %all-gather.29.cloned.1.call-start = ((), (), s32[]{:S(2)}) async-start(), calls=%async_computation.8 | async-start | bytes 20054016 | tf_op jit(solution)/shard_map/all_gather | solution.py:22
  1143.2 127.1 %copy-start.2 = (bf16[2,192,1536]{2,1,0:T(8,128)(2,1)S(1)}, bf16[2,192,1536]{2,1,0:T(8,128)(2,1)}, u32[]{:S(2)}) copy-start(bf16[2,192,1536]{2,1,0:T(8,128)(2,1)} %copy-done.1) | copy-start | bytes 3538948
  1143.2 211.0 %all-gather.35.cloned.1.call-start = ((), (), s32[]{:S(2)}) async-start(), calls=%async_computation.11 | async-start | bytes 10027008 | tf_op jit(solution)/shard_map/all_gather | solution.py:22
  1146.1 230.6 %all-gather.31.cloned.1.call-start = ((), (), s32[]{:S(2)}) async-start(), calls=%async_computation.9 | async-start | bytes 1769472 | tf_op jit(solution)/shard_map/all_gather | solution.py:15
  1282.4 124.2 %all-gather.37.cloned.1.call-start = ((), (), s32[]{:S(2)}) async-start(), calls=%async_computation.12 | async-start | bytes 1769472 | tf_op jit(solution)/shard_map/all_gather | solution.py:15
  1383.6 107.0 %all-gather.33.cloned.1.call-start = ((), (), s32[]{:S(2)}) async-start(), calls=%async_computation.10 | async-start | bytes 10027008 | tf_op jit(solution)/shard_map/all_gather | solution.py:22
Sparse Core Ops, SparseCore 0:
  8.9 47.6 all-gather.16
  58.1 44.9 all-gather.14
  205.9 519.8 reduce-scatter.3
  771.9 35.8 all-gather.18
  809.3 98.9 all-gather.20
  920.4 98.9 all-gather.22
  1033.0 98.9 all-gather.26
  1133.6 36.0 all-gather.24
  1171.3 98.9 all-gather.28
  1272.7 81.4 all-gather.34
  1355.8 20.8 all-gather.30
  1383.8 22.7 all-gather.36
  1409.1 81.4 all-gather.32
where the time goes:
time: 1550 us; the launch traced here: 1540 us
  waiting for transfers between devices  1250 us (81%)
  matrix products  90.9 us (6%)
  blocking collectives  77.8 us (5%)
  local copies, waits for them, and re-layouts  66.2 us (4%)
  other arithmetic  43.4 us (3%)
    all_gather x6, waiting for transfers between devices, times_columns(): lax.all_gather(stacked_tiles, 'dp', axis=1, tiled=True)  554 us
    reduce_scatter x1, waiting for transfers between devices, shards(): lax.psum_scatter(jnp.concatenate([input_cov, grad_cov, weight_grad], axis...  519 us
    all_gather x4, waiting for transfers between devices, row_panel(): return lax.all_gather(stacked_tiles, 'grp', axis=2, tiled=True)  102 us
    dot_general x6, matrix products, times_columns(): jnp.einsum('fri,fic->frc', panel_rows, lax.all_gather(stacked_tiles, 'dp'...  58.7 us
    unnamed x18, local copies, waits for them, and re-layouts  56.2 us
    all_gather x1, waiting for transfers between devices, shards(): lax.all_gather(cotangents, 'grp', axis=1, tiled=True)  48.5 us
    psum x1, blocking collectives, shards(): lax.psum((trace_parts, square_parts), ('dp', 'grp'))  39.3 us
    psum x1, blocking collectives, shards(): lax.psum(jnp.sum(preconditioned * preconditioned), ('dp', 'grp'))  38.5 us
  transfers between devices with their start and end apart: 13, of which 13 were waited for; matrix products, arithmetic and copies ran while one was open for 3% of the time, Pallas kernels for 0%

commit v1 on v0

v1 whole, which is shorter than its diff:
```python
import jax
import jax.numpy as jnp
from jax import lax
from jax.sharding import PartitionSpec as P

damping = 0.05
epsilon = 1e-06
f32 = jnp.float32
bf16 = jnp.bfloat16


def dot_rows(left, right):
    return lax.dot_general(left, right, (((0,), (0,)), ((), ())), preferred_element_type=f32)


def matmul(left, right):
    return jnp.dot(left, right, preferred_element_type=f32)


def shards(activations, cotangents):
    n = lax.axis_size("dp")
    c = lax.axis_size("grp")
    chips = n // 2
    part = c // 2
    cols = activations.shape[1]
    D = cols * c
    rows = D // n
    half = D // 2
    dp_index = lax.axis_index("dp")
    grp_index = lax.axis_index("grp")
    core = dp_index % 2
    on_g = grp_index >= part
    pairs = [(i, i ^ 1) for i in range(n)]
    same_core = [list(range(0, n, 2)), list(range(1, n, 2))]

    def other_core(x):
        return lax.ppermute(x, "dp", pairs)

    def core_halves(mine):
        theirs = other_core(mine)
        return jnp.where(
            core == 0,
            jnp.concatenate([mine, theirs], axis=0),
            jnp.concatenate([theirs, mine], axis=0),
        )

    def reduce_rows(x):
        return lax.psum_scatter(
            x, "dp", scatter_dimension=0, tiled=True, axis_index_groups=same_core
        )

    if c == 2:
        theirs = lax.ppermute(jnp.where(on_g, activations, cotangents), "grp", [(0, 1), (1, 0)])
        mine = jnp.where(
            on_g,
            jnp.concatenate([theirs, cotangents], axis=1),
            jnp.concatenate([activations, theirs], axis=1),
        )
    else:
        mine = jnp.where(
            on_g,
            lax.all_gather(cotangents, "grp", axis=1, tiled=True),
            lax.all_gather(activations, "grp", axis=1, tiled=True),
        )
    mine = jnp.concatenate([mine, other_core(mine)], axis=0)
    my_half = lax.dynamic_slice_in_dim(mine, core * half, half, 1)
    cov_rows = reduce_rows(dot_rows(my_half, mine).astype(bf16))

    all_grads = lax.all_gather(cotangents, "grp", axis=1, tiled=True)
    all_grads = jnp.concatenate([all_grads, other_core(all_grads)], axis=0)
    acts = jnp.concatenate([activations, other_core(activations)], axis=0)
    acts = lax.dynamic_slice_in_dim(acts, core * (cols // 2), cols // 2, 1)
    grad_rows = reduce_rows(dot_rows(acts, all_grads).astype(bf16))
    grad_rows = lax.all_gather(grad_rows, "grp", axis=0, tiled=True)

    cov = lax.all_gather(cov_rows, "dp", axis=0, tiled=True)
    cov = cov.reshape(chips, 2, rows, D).transpose(1, 0, 2, 3).reshape(D, D)
    wide = cov.astype(f32)
    diag = lax.iota(jnp.int32, D)[:, None] == lax.iota(jnp.int32, D)[None, :]
    trace = jnp.sum(jnp.where(diag, wide, 0.0))
    square = jnp.sum(wide * wide)
    damp = damping * trace / D
    scale = lax.rsqrt(square + 2.0 * damp * trace + D * damp * damp)
    base = (scale * (wide + jnp.where(diag, damp, 0.0))).astype(bf16)

    def my_rows(x):
        return lax.dynamic_slice_in_dim(x, core * half, half, 0)

    base_half = my_rows(base)
    base_wide = base_half.astype(f32)
    second_wide = 2.0 * base_wide - matmul(base_half, base)
    second_half = second_wide.astype(bf16)
    second = core_halves(second_half)
    second_wide = second_half.astype(f32)
    fourth_half = (2.0 * second_wide - matmul(second_half, second)).astype(bf16)
    fourth = core_halves(fourth_half)
    mixed_half = (2.0 * (base_wide + second_wide) - matmul(base_half, second)).astype(bf16)
    tail_half = (
        4.0 * fourth_half.astype(f32) + 2.0 * mixed_half.astype(f32) - matmul(mixed_half, fourth)
    ).astype(bf16)
    tail = core_halves(tail_half)

    left = (8.0 * grad_rows.astype(f32) - matmul(grad_rows, tail)).astype(bf16)
    left = lax.all_to_all(left, "dp", split_axis=1, concat_axis=0, tiled=True)
    left = lax.ppermute(left, "grp", [(part + j, j) for j in range(part)])
    left = left.reshape(chips, 2, c, D // c // n, rows).transpose(2, 1, 0, 3, 4).reshape(D, rows)
    precond = 8.0 * left.astype(f32).T - dot_rows(left, tail)

    keep = lax.dynamic_slice_in_dim(precond, (grp_index % part) * cols, cols, 1)
    send = lax.dynamic_slice_in_dim(precond, (grp_index % part + part) * cols, cols, 1)
    sent = lax.ppermute(send.astype(bf16), "grp", [(j, part + j) for j in range(part)])
    precond = jnp.where(on_g, sent.astype(f32), keep)
    total = lax.psum(jnp.sum(precond * precond), ("dp", "grp"))
    return precond * lax.rsqrt(total / (D * D) + epsilon)


def solution(mesh):
    spec = P("dp", "grp")
    return jax.shard_map(shards, mesh=mesh, in_specs=(spec, spec), out_specs=spec, check_vma=False)
```

time: 1550 us -> 853 us (0.55)
  waiting for transfers between devices: 1250 us -> 427 us
  matrix products: 90.9 us -> 207 us
  local copies, waits for them, and re-layouts: 66.2 us -> 44.3 us
  other arithmetic: 43.4 us -> 60.4 us
    all_gather x12 -> x3, waiting for transfers between devices: 729 us -> 166 us  [the longest x1 99.4 us: shards(): cov = lax.all_gather(cov_rows, 'dp', axis=0, tiled=True)]
    reduce_scatter x1 -> x2, waiting for transfers between devices: 519 us -> 178 us  [reduce_rows(): lax.psum_scatter(x, 'dp', scatter_dimension=0, tiled=True, axis_index_gro...]
    dot_general x9 -> x8, matrix products: 90.9 us -> 207 us  [the longest x5 168 us: matmul(): return jnp.dot(left, right, preferred_element_type=f32)]
    ppermute x0 -> x9, waiting for transfers between devices: none -> 82.3 us  [the longest x1 34.4 us: shards(): lax.ppermute(jnp.where(on_g, activations, cotangents), 'grp', [(0, 1), (1...]
    unnamed x18 -> x6, local copies, waits for them, and re-layouts: 56.2 us -> 4.21 us
    all_to_all x0 -> x1, blocking collectives: none -> 41.5 us  [shards(): left = lax.all_to_all(left, 'dp', split_axis=1, concat_axis=0, tiled=True)]
    psum x2 -> x1, blocking collectives: 77.8 us -> 40.7 us  [shards(): total = lax.psum(jnp.sum(precond * precond), ('dp', 'grp'))]
    concatenate x1 -> x0, other arithmetic: 36.9 us -> none  [shards(): jnp.concatenate([input_cov, grad_cov, weight_grad], axis=1)]
  transfers between devices with their start and end apart: 13 -> 14, of which waited for: 13 -> 9; matrix products, arithmetic and copies ran while one was open for 3% -> 15% of each run, Pallas kernels for 0% -> 0%
where the time goes in v1:
time: 853 us; the launch traced here: 847 us
  waiting for transfers between devices  427 us (50%)
  matrix products  207 us (24%)
  blocking collectives  82.2 us (10%)
  other arithmetic  60.4 us (7%)
  local copies, waits for them, and re-layouts  44.3 us (5%)
  between operations  19.1 us (2%)
    reduce_scatter x2, waiting for transfers between devices, reduce_rows(): lax.psum_scatter(x, 'dp', scatter_dimension=0, tiled=True, axis_index_gro...  178 us
    dot_general x5, matrix products, matmul(): return jnp.dot(left, right, preferred_element_type=f32)  168 us
    all_gather x1, waiting for transfers between devices, shards(): cov = lax.all_gather(cov_rows, 'dp', axis=0, tiled=True)  99.4 us
    all_gather x1, waiting for transfers between devices, shards(): all_grads = lax.all_gather(cotangents, 'grp', axis=1, tiled=True)  44.3 us
    all_to_all x1, blocking collectives, shards(): left = lax.all_to_all(left, 'dp', split_axis=1, concat_axis=0, tiled=True)  41.5 us
    psum x1, blocking collectives, shards(): total = lax.psum(jnp.sum(precond * precond), ('dp', 'grp'))  40.7 us
    dot_general x3, matrix products, dot_rows(): lax.dot_general(left, right, (((0,), (0,)), ((), ())), preferred_element_...  38.1 us
    ppermute x1, waiting for transfers between devices, shards(): lax.ppermute(jnp.where(on_g, activations, cotangents), 'grp', [(0, 1), (1...  34.4 us
  transfers between devices with their start and end apart: 14, of which 9 were waited for; matrix products, arithmetic and copies ran while one was open for 15% of the time, Pallas kernels for 0%

profile of v1, /device:TPU:0, one launch (start us, length us, event | category | flops | bytes accessed | tf_op | source)
XLA Modules:
  0.0 847.4 jit_solution(1882348261889960127)
XLA Ops:
  7.4 0.0 reduce-scatter.5.cloned.1.call-start
  7.4 1.6 broadcast_select_fusion
  8.9 3.0 collective-permute-start.2
  12.0 34.4 %collective-permute-done.2 = bf16[512,1536]{1,0:T(8,128)(2,1)S(1)} collective-permute-done((bf16[512,1536]{1,0:T(8,128)(2,1)S(1)}, bf16[512,1536]{1,0:T(8,128)(2,1)S(1)}, u32[]{:S(2)}, u32[]{:S(2)}) %collective-permute-start.2) | collective-permute-done | bytes 1572896 | tf_op jit(solution)/shard_map/ppermute | solution.py:53
  46.3 2.3 maximum_select_fusion.10
  48.7 0.1 collective-permute-start.3
  48.8 5.8 collective-permute-done.3
  54.5 14.6 %convolution_convert_fusion = bf16[1536,3072]{1,0:T(8,128)(2,1)} fusion(bf16[512,3072]{1,0:T(8,128)(2,1)} %collective-permute-done.3, bf16[512,3072]{1,0:T(8,128)(2,1)S(1)} %maximum_select_fusion.10, s32[]{:T(128)S(6)} %select_n.77), kind=kOutput, calls=%fused_computation.29 | convolution fusion | flops 9687269376 | bytes 22020100 | tf_op jit(solution)/shard_map/dot_general | solution.py:13
  69.2 0.0 reduce-scatter.5.cloned.1.call-update
  69.2 0.0 all-gather.8.cloned.1.call-start
  69.2 164.9 %reduce-scatter.5.cloned.1.call-done = bf16[192,3072]{1,0:T(8,128)(2,1)} async-done(((bf16[1536,3072]{1,0:T(8,128)(2,1)}), bf16[192,3072]{1,0:T(8,128)(2,1)}) %reduce-scatter.5.cloned.1.call-update) | async-done | bytes 1179664 | tf_op jit(solution)/shard_map/reduce_scatter | solution.py:48
  234.2 0.0 all-gather.8.cloned.1.call-update
  234.2 0.2 all-gather.4.cloned.1.call-start
  234.4 99.4 %all-gather.8.cloned.1.call-done = bf16[3072,3072]{1,0:T(8,128)(2,1)} async-done(((bf16[192,3072]{1,0:T(8,128)(2,1)}), bf16[3072,3072]{1,0:T(8,128)(2,1)}) %all-gather.8.cloned.1.call-update) | async-done | bytes 18874384 | tf_op jit(solution)/shard_map/all_gather | solution.py:76
  333.8 0.0 copy-start
  333.8 21.2 %convert_bitcast_fusion = f32[2,8,192,3072]{3,2,0,1:T(8,128)} fusion(bf16[8,2,192,3072]{3,2,1,0:T(8,128)(2,1)} %bitcast.32), kind=kLoop, calls=%fused_computation.3 | loop fusion | flops 9437184 | bytes 56623104 | tf_op jit(solution)/shard_map/convert_element_type | solution.py:78
  355.0 4.2 copy-done
  359.2 17.0 %multiply_reduce_fusion = (f32[]{:T(128)}, f32[]{:T(128)}) fusion(bf16[8,2,192,3072]{3,2,1,0:T(8,128)(2,1)S(1)} %bitcast.33, s32[2,8,192]{2,0,1:T(2,128)S(1)} %multiply_add_fusion), kind=kLoop, calls=%fused_computation.7 | loop fusion | flops 56623104 | bytes 18886664 | tf_op jit(solution)/shard_map/reduce_sum | solution.py:81
  379.1 28.1 %copy.7 = f32[2,8,192,3072]{3,2,1,0:T(8,128)} copy(f32[2,8,192,3072]{3,2,0,1:T(8,128)} %convert_bitcast_fusion) | data formatting | bytes 75497472 | tf_op jit(solution)/shard_map/convert_element_type | solution.py:78
  407.8 16.2 %fusion.1 = bf16[3072,3072]{1,0:T(8,128)(2,1)S(1)} fusion(f32[2,8,192,3072]{3,2,1,0:T(8,128)} %copy.7, f32[]{:T(128)S(6)} %div.6, f32[]{:T(128)S(6)} %rsqrt.6), kind=kLoop, calls=%fused_computation.2 | loop fusion | flops 47185920 | bytes 56623112 | tf_op jit(solution)/shard_map/convert_element_type | solution.py:84
  424.0 0.0 copy-start.1
  424.0 0.0 copy-start.2
  424.0 31.6 %fusion.3 = bf16[1536,3072]{1,0:T(8,128)(2,1)} fusion(bf16[3072,3072]{1,0:T(8,128)(2,1)S(1)} %fusion.1, s32[]{:T(128)S(6)} %select_n.77), kind=kOutput, calls=%fused_computation.12 | convolution fusion | flops 29009903616 | bytes 47186944 | tf_op jit(solution)/shard_map/dot_general | solution.py:17
  455.6 0.0 copy-done.1
  455.6 0.3 collective-permute-start.4
  455.9 0.0 all-gather.4.cloned.1.call-update
  455.9 0.3 reduce-scatter.3.cloned.1.call-start
  456.2 0.0 copy-done.2
  456.2 0.3 collective-permute-start
  456.5 44.3 %all-gather.4.cloned.1.call-done = bf16[512,3072]{1,0:T(8,128)(2,1)} async-done(((bf16[512,1536]{1,0:T(8,128)(2,1)}), bf16[512,3072]{1,0:T(8,128)(2,1)}) %all-gather.4.cloned.1.call-update) | async-done | bytes 3145744 | tf_op jit(solution)/shard_map/all_gather | solution.py:69
  500.8 0.0 collective-permute-start.1
  500.8 0.0 collective-permute-done.4
  500.8 40.5 %fusion.5 = bf16[1536,3072]{1,0:T(8,128)(2,1)} fusion(bf16[1536,3072]{1,0:T(8,128)(2,1)} %fusion.3, bf16[1536,3072]{1,0:T(8,128)(2,1)} %collective-permute-done.4, pred[]{:T(512)S(6)} %eq.41), kind=kOutput, calls=%fused_computation.14 | convolution fusion | flops 29094838272 | bytes 28311552 | tf_op jit(solution)/shard_map/dot_general | solution.py:17
  541.3 0.5 collective-permute-start.5
  541.8 0.0 collective-permute-done
  541.8 0.0 collective-permute-done.1
  541.8 8.9 %fusion.22 = bf16[768,3072]{1,0:T(8,128)(2,1)} fusion(bf16[512,3072]{1,0:T(8,128)(2,1)} %collective-permute-done.1, bf16[512,3072]{1,0:T(8,128)(2,1)} %all-gather.4.cloned.1.call-done, s32[]{:T(128)S(6)} %select_n.71, bf16[512,1536]{1,0:T(8,128)(2,1)S(1)} %copy-done.2, bf16[512,1536]{1,0:T(8,128)(2,1)} %collective-permute-done), kind=kOutput, calls=%fused_computation.39 | convolution fusion | flops 4849926144 | bytes 14155780 | tf_op jit(solution)/shard_map/dot_general | solution.py:13
  550.7 0.0 reduce-scatter.3.cloned.1.call-update
  550.7 0.4 all-gather.6.cloned.1.call-start
  551.2 40.6 %fusion.8 = bf16[1536,3072]{1,0:T(8,128)(2,1)} fusion(bf16[1536,3072]{1,0:T(8,128)(2,1)} %fusion.3, bf16[3072,3072]{1,0:T(8,128)(2,1)} %copy-done.1, s32[]{:T(128)S(6)} %select_n.77, bf16[1536,3072]{1,0:T(8,128)(2,1)} %collective-permute-done.4, pred[]{:T(512)S(6)} %eq.41), kind=kOutput, calls=%fused_computation.17 | convolution fusion | flops 29104275456 | bytes 56624640 | tf_op jit(solution)/shard_map/dot_general | solution.py:17
  591.8 0.0 collective-permute-done.5
  591.8 40.9 %subtract_convert_fusion = bf16[1536,3072]{1,0:T(8,128)(2,1)} fusion(bf16[1536,3072]{1,0:T(8,128)(2,1)} %fusion.8, bf16[1536,3072]{1,0:T(8,128)(2,1)} %fusion.5, bf16[1536,3072]{1,0:T(8,128)(2,1)} %collective-permute-done.5, pred[]{:T(512)S(6)} %eq.41), kind=kOutput, calls=%fused_computation.27 | convolution fusion | flops 29108994048 | bytes 37748736 | tf_op jit(solution)/shard_map/dot_general | solution.py:17
  632.8 0.1 collective-permute-start.6
  632.8 13.5 %reduce-scatter.3.cloned.1.call-done = bf16[96,3072]{1,0:T(8,128)(2,1)} async-done(((bf16[768,3072]{1,0:T(8,128)(2,1)}), bf16[96,3072]{1,0:T(8,128)(2,1)}) %reduce-scatter.3.cloned.1.call-update) | async-done | bytes 589840 | tf_op jit(solution)/shard_map/reduce_scatter | solution.py:48
  646.3 0.0 all-gather.6.cloned.1.call-update
  646.3 22.5 %all-gather.6.cloned.1.call-done = bf16[192,3072]{1,0:T(8,128)(2,1)} async-done(((bf16[96,3072]{1,0:T(8,128)(2,1)}), bf16[192,3072]{1,0:T(8,128)(2,1)}) %all-gather.6.cloned.1.call-update) | async-done | bytes 1179664 | tf_op jit(solution)/shard_map/all_gather | solution.py:74
  668.8 0.0 collective-permute-done.6
  668.8 14.8 %subtract_convert_fusion.1 = bf16[192,3072]{1,0:T(8,128)(2,1)S(1)} fusion(bf16[192,3072]{1,0:T(8,128)(2,1)} %all-gather.6.cloned.1.call-done, bf16[1536,3072]{1,0:T(8,128)(2,1)} %collective-permute-done.6, bf16[1536,3072]{1,0:T(8,128)(2,1)} %subtract_convert_fusion, pred[]{:T(512)S(6)} %eq.41), kind=kOutput, calls=%fused_computation.46 | convolution fusion | flops 3711172608 | bytes 21233664 | tf_op jit(solution)/shard_map/dot_general | solution.py:17
  683.6 0.7 copy.11
  684.3 41.5 %all_to_all.19 = bf16[192,16,192]{0,2,1:T(8,128)(2,1)S(1)} all-to-all(bf16[192,16,192]{0,2,1:T(8,128)(2,1)S(1)} %bitcast.35), channel_id=1, replica_groups=mesh['dp'=16,'grp'=2] {'dp'}, dimensions={1} | all-to-all | bytes 2359296 | tf_op jit(solution)/shard_map/all_to_all | solution.py:104
  725.8 0.9 copy.9
  726.6 1.7 all_to_all.17
  728.4 1.3 collective-permute-start.7
  729.7 29.3 %collective-permute-done.7 = bf16[3072,192]{0,1:T(8,128)(2,1)} collective-permute-done((bf16[3072,192]{0,1:T(8,128)(2,1)S(1)}, bf16[3072,192]{0,1:T(8,128)(2,1)}, u32[]{:S(2)}, u32[]{:S(2)}) %collective-permute-start.7) | collective-permute-done | bytes 1179680 | tf_op jit(solution)/shard_map/ppermute | solution.py:105
  759.0 5.5 reshape.33
  764.5 0.3 copy.10
  764.8 3.0 reshape.34
  767.7 14.6 %convolution_subtract_fusion = f32[192,3072]{1,0:T(8,128)S(1)} fusion(bf16[3072,192]{0,1:T(8,128)(2,1)} %reshape.34, bf16[1536,3072]{1,0:T(8,128)(2,1)} %collective-permute-done.6, bf16[1536,3072]{1,0:T(8,128)(2,1)} %subtract_convert_fusion, pred[]{:T(512)S(6)} %eq.41), kind=kOutput, calls=%fused_computation.40 | convolution fusion | flops 3710582784 | bytes 22413312 | tf_op jit(solution)/shard_map/dot_general | solution.py:13
  782.3 0.1 dynamic_slice.52
  782.4 1.4 collective-permute-start.8
  783.8 12.8 %collective-permute-done.8 = bf16[192,1536]{1,0:T(8,128)(2,1)S(1)} collective-permute-done((bf16[192,1536]{1,0:T(8,128)(2,1)S(1)}, bf16[192,1536]{1,0:T(8,128)(2,1)S(1)}, u32[]{:S(2)}, u32[]{:S(2)}) %collective-permute-start.8) | collective-permute-done | bytes 589856 | tf_op jit(solution)/shard_map/ppermute | solution.py:111
  796.6 0.9 multiply_reduce_fusion.1
  797.5 40.7 %psum.7 = f32[]{:T(128)} all-reduce(f32[]{:T(128)} %multiply_reduce_fusion.1), channel_id=1, replica_groups=mesh['dp'=16,'grp'=2] {'dp','grp'}, use_global_device_ids=true, to_apply=%region_5.6 | all-reduce | flops 1 | bytes 8 | tf_op jit(solution)/shard_map/psum | solution.py:113
  838.9 1.2 fusion.30
  (1 shorter events, 0.0 us)
Async XLA Ops:
  7.4 226.8 %reduce-scatter.5.cloned.1.call-start = ((), (), s32[]{:S(2)}) async-start(), calls=%async_computation.6 | async-start | bytes 10616832 | tf_op jit(solution)/shard_map/reduce_scatter | solution.py:48
  8.9 37.4 %collective-permute-start.2 = (bf16[512,1536]{1,0:T(8,128)(2,1)S(1)}, bf16[512,1536]{1,0:T(8,128)(2,1)S(1)}, u32[]{:S(2)}, u32[]{:S(2)}) collective-permute-start(bf16[512,1536]{1,0:T(8,128)(2,1)S(1)} %broadcast_select_fusion), channel_id=1, source_target_pairs={{0,1},{1,0},{2,3},{3,2},{4,5},{5,4},{6,7},{7,6},{8,9},{9,8},{10,11... | collective-permute-start | bytes 4718600 | tf_op jit(solution)/shard_map/ppermute | solution.py:53
  48.7 5.9 collective-permute-start.3
  69.2 264.6 %all-gather.8.cloned.1.call-start = ((), (), s32[]{:S(2)}) async-start(), calls=%async_computation.7 | async-start | bytes 20054016 | tf_op jit(solution)/shard_map/all_gather | solution.py:76
  234.2 266.6 %all-gather.4.cloned.1.call-start = ((), (), s32[]{:S(2)}) async-start(), calls=%async_computation.3 | async-start | bytes 4718592 | tf_op jit(solution)/shard_map/all_gather | solution.py:69
  333.8 25.4 %copy-start = (bf16[3072,3072]{1,0:T(8,128)(2,1)S(1)}, bf16[3072,3072]{1,0:T(8,128)(2,1)}, u32[]{:S(2)}) copy-start(bf16[3072,3072]{1,0:T(8,128)(2,1)} %all-gather.8.cloned.1.call-done) | copy-start | bytes 56623108
  424.0 31.6 %copy-start.1 = (bf16[3072,3072]{1,0:T(8,128)(2,1)}, bf16[3072,3072]{1,0:T(8,128)(2,1)S(1)}, u32[]{:S(2)}) copy-start(bf16[3072,3072]{1,0:T(8,128)(2,1)S(1)} %fusion.1) | copy-start | bytes 56623108
  424.0 32.1 %copy-start.2 = (bf16[512,1536]{1,0:T(8,128)(2,1)S(1)}, bf16[512,1536]{1,0:T(8,128)(2,1)}, u32[]{:S(2)}) copy-start(bf16[512,1536]{1,0:T(8,128)(2,1)} %param.2) | copy-start | bytes 4718596
  455.6 45.2 %collective-permute-start.4 = (bf16[1536,3072]{1,0:T(8,128)(2,1)}, bf16[1536,3072]{1,0:T(8,128)(2,1)}, u32[]{:S(2)}, u32[]{:S(2)}) collective-permute-start(bf16[1536,3072]{1,0:T(8,128)(2,1)} %fusion.3), channel_id=1, source_target_pairs={{0,2},{2,0},{4,6},{6,4},{8,10},{10,8},{12,14},{14,12},{16,18},{18,... | collective-permute-start | bytes 28311560 | tf_op jit(solution)/shard_map/ppermute | solution.py:37
  455.9 190.4 %reduce-scatter.3.cloned.1.call-start = ((), (), s32[]{:S(2)}) async-start(), calls=%async_computation.4 | async-start | bytes 5308416 | tf_op jit(solution)/shard_map/reduce_scatter | solution.py:48
  456.2 85.7 %collective-permute-start = (bf16[512,1536]{1,0:T(8,128)(2,1)S(1)}, bf16[512,1536]{1,0:T(8,128)(2,1)}, u32[]{:S(2)}, u32[]{:S(2)}) collective-permute-start(bf16[512,1536]{1,0:T(8,128)(2,1)S(1)} %copy-done.2), channel_id=1, source_target_pairs={{0,2},{2,0},{4,6},{6,4},{8,10},{10,8},{12,14},{14,12},{16,18},{18,... | collective-permute-start | bytes 4718600 | tf_op jit(solution)/shard_map/ppermute | solution.py:37
  500.8 41.1 %collective-permute-start.1 = (bf16[512,3072]{1,0:T(8,128)(2,1)}, bf16[512,3072]{1,0:T(8,128)(2,1)}, u32[]{:S(2)}, u32[]{:S(2)}) collective-permute-start(bf16[512,3072]{1,0:T(8,128)(2,1)} %all-gather.4.cloned.1.call-done), channel_id=1, source_target_pairs={{0,2},{2,0},{4,6},{6,4},{8,10},{10,8},{12,14},{14,12},{16,18},{18,... | collective-permute-start | bytes 9437192 | tf_op jit(solution)/shard_map/ppermute | solution.py:37
  541.3 50.5 %collective-permute-start.5 = (bf16[1536,3072]{1,0:T(8,128)(2,1)}, bf16[1536,3072]{1,0:T(8,128)(2,1)}, u32[]{:S(2)}, u32[]{:S(2)}) collective-permute-start(bf16[1536,3072]{1,0:T(8,128)(2,1)} %fusion.5), channel_id=1, source_target_pairs={{0,2},{2,0},{4,6},{6,4},{8,10},{10,8},{12,14},{14,12},{16,18},{18,... | collective-permute-start | bytes 28311560 | tf_op jit(solution)/shard_map/ppermute | solution.py:37
  550.7 118.1 %all-gather.6.cloned.1.call-start = ((), (), s32[]{:S(2)}) async-start(), calls=%async_computation.5 | async-start | bytes 1769472 | tf_op jit(solution)/shard_map/all_gather | solution.py:74
  632.8 36.1 %collective-permute-start.6 = (bf16[1536,3072]{1,0:T(8,128)(2,1)}, bf16[1536,3072]{1,0:T(8,128)(2,1)}, u32[]{:S(2)}, u32[]{:S(2)}) collective-permute-start(bf16[1536,3072]{1,0:T(8,128)(2,1)} %subtract_convert_fusion), channel_id=1, source_target_pairs={{0,2},{2,0},{4,6},{6,4},{8,10},{10,8},{12,14},{14,12},{16,18},{18,... | collective-permute-start | bytes 28311560 | tf_op jit(solution)/shard_map/ppermute | solution.py:37
  728.4 30.6 %collective-permute-start.7 = (bf16[3072,192]{0,1:T(8,128)(2,1)S(1)}, bf16[3072,192]{0,1:T(8,128)(2,1)}, u32[]{:S(2)}, u32[]{:S(2)}) collective-permute-start(bf16[3072,192]{0,1:T(8,128)(2,1)S(1)} %all_to_all.17), channel_id=1, source_target_pairs={{1,0},{3,2},{5,4},{7,6},{9,8},{11,10},{13,12},{15,14},{17,16},{19,... | collective-permute-start | bytes 3538952 | tf_op jit(solution)/shard_map/ppermute | solution.py:105
  782.4 14.2 %collective-permute-start.8 = (bf16[192,1536]{1,0:T(8,128)(2,1)S(1)}, bf16[192,1536]{1,0:T(8,128)(2,1)S(1)}, u32[]{:S(2)}, u32[]{:S(2)}) collective-permute-start(bf16[192,1536]{1,0:T(8,128)(2,1)S(1)} %dynamic_slice.52), channel_id=1, source_target_pairs={{0,1},{2,3},{4,5},{6,7},{8,9},{10,11},{12,13},{14,15},{16,17},{18,... | collective-permute-start | bytes 1769480 | tf_op jit(solution)/shard_map/ppermute | solution.py:111
Sparse Core Ops, SparseCore 0:
  69.3 164.8 reduce-scatter.4
  235.7 98.0 all-gather.7
  550.8 95.4 reduce-scatter.2
Sparse Core Ops, SparseCore 1:
  456.0 44.7 all-gather.3
  646.4 22.3 all-gather.5

commit v2 on v1

--- a/solution.py
+++ b/solution.py
@@ -49,6 +49,41 @@
             x, "dp", scatter_dimension=0, tiled=True, axis_index_groups=same_core
         )
 
+    ring = list(range(0, chips, 2)) + list(range(chips - 1, 0, -2))
+    chip = dp_index // 2
+    place = jnp.where(chip % 2 == 0, chip // 2, chips - 1 - chip // 2)
+
+    def ring_reduce(x, lanes):
+        width = x.shape[1] // (2 * lanes)
+
+        def block(lane, spot):
+            spot = (spot + 2 * chips) % chips
+            owner = jnp.where(spot < chips // 2, 2 * spot, 2 * (chips - 1 - spot) + 1)
+            piece = lax.dynamic_slice(x, (owner * rows, lane * width), (rows, width))
+            return piece.astype(f32)
+
+        totals = [None] * (2 * lanes)
+        for lane in range(2 * lanes):
+            totals[lane] = block(lane, place + (1 if lane % 2 else -1))
+        for step in range(chips - 1):
+            for lane in range(2 * lanes):
+                way = -1 if lane % 2 else 1
+                moves = [
+                    (ring[p] * 2 + k, ring[(p + way) % chips] * 2 + k)
+                    for p in range(chips)
+                    for k in range(2)
+                ]
+                got = lax.ppermute(totals[lane].astype(bf16), "dp", moves)
+                totals[lane] = got.astype(f32) + block(lane, place - way * (step + 2))
+        return jnp.concatenate(totals, axis=1)
+
+    def sum_dp(x):
+        hop = 1
+        while hop < n:
+            x = x + lax.ppermute(x, "dp", [(i, i ^ hop) for i in range(n)])
+            hop *= 2
+        return x
+
     if c == 2:
         theirs = lax.ppermute(jnp.where(on_g, activations, cotangents), "grp", [(0, 1), (1, 0)])
         mine = jnp.where(
@@ -57,44 +92,60 @@
             jnp.concatenate([activations, theirs], axis=1),
         )
     else:
+        all_grads = lax.all_gather(cotangents, "grp", axis=1, tiled=True)
         mine = jnp.where(
-            on_g,
-            lax.all_gather(cotangents, "grp", axis=1, tiled=True),
-            lax.all_gather(activations, "grp", axis=1, tiled=True),
+            on_g, all_grads, lax.all_gather(activations, "grp", axis=1, tiled=True)
         )
     mine = jnp.concatenate([mine, other_core(mine)], axis=0)
-    my_half = lax.dynamic_slice_in_dim(mine, core * half, half, 1)
-    cov_rows = reduce_rows(dot_rows(my_half, mine).astype(bf16))
+    my_half = lax.dynamic_index_in_dim(
+        mine.reshape(mine.shape[0], chips, 2, rows), core, 2, keepdims=False
+    ).reshape(mine.shape[0], half)
+    cov_rows = ring_reduce(dot_rows(my_half, mine).astype(bf16), 2)
 
-    all_grads = lax.all_gather(cotangents, "grp", axis=1, tiled=True)
+    if c == 2:
+        rest = lax.ppermute(cotangents, "grp", [(1, 0)])
+        all_grads = jnp.concatenate([cotangents, rest], axis=1)
     all_grads = jnp.concatenate([all_grads, other_core(all_grads)], axis=0)
+    if c == 2:
+        all_grads = jnp.where(on_g, mine, all_grads)
     acts = jnp.concatenate([activations, other_core(activations)], axis=0)
     acts = lax.dynamic_slice_in_dim(acts, core * (cols // 2), cols // 2, 1)
     grad_rows = reduce_rows(dot_rows(acts, all_grads).astype(bf16))
-    grad_rows = lax.all_gather(grad_rows, "grp", axis=0, tiled=True)
+    if c == 2:
+        first = lax.ppermute(grad_rows, "grp", [(0, 1)])
+        grad_rows = jnp.concatenate([first, grad_rows], axis=0)
+    else:
+        grad_rows = lax.all_gather(grad_rows, "grp", axis=0, tiled=True)
 
-    cov = lax.all_gather(cov_rows, "dp", axis=0, tiled=True)
-    cov = cov.reshape(chips, 2, rows, D).transpose(1, 0, 2, 3).reshape(D, D)
-    wide = cov.astype(f32)
-    diag = lax.iota(jnp.int32, D)[:, None] == lax.iota(jnp.int32, D)[None, :]
-    trace = jnp.sum(jnp.where(diag, wide, 0.0))
-    square = jnp.sum(wide * wide)
+    cov = lax.all_gather(cov_rows.astype(bf16), "dp", axis=0, tiled=True)
+
+    def diag_mask(start, count):
+        return start + lax.iota(jnp.int32, count)[:, None] == lax.iota(jnp.int32, D)[None, :]
+
+    trace_part = jnp.sum(jnp.where(diag_mask(dp_index * rows, rows), cov_rows, 0.0))
+    trace, square = sum_dp(jnp.stack([trace_part, jnp.sum(cov_rows * cov_rows)]))
     damp = damping * trace / D
     scale = lax.rsqrt(square + 2.0 * damp * trace + D * damp * damp)
-    base = (scale * (wide + jnp.where(diag, damp, 0.0))).astype(bf16)
 
     def my_rows(x):
         return lax.dynamic_slice_in_dim(x, core * half, half, 0)
 
-    base_half = my_rows(base)
-    base_wide = base_half.astype(f32)
-    second_wide = 2.0 * base_wide - matmul(base_half, base)
-    second_half = second_wide.astype(bf16)
+    cov_half = my_rows(cov)
+    cov_wide = cov_half.astype(f32)
+    damp_half = jnp.where(diag_mask(core * half, half), damp, 0.0)
+    base_wide = scale * (cov_wide + damp_half)
+    base_square = scale * scale * (
+        matmul(cov_half, cov) + 2.0 * damp * cov_wide + damp * damp_half
+    )
+    second_half = (2.0 * base_wide - base_square).astype(bf16)
     second = core_halves(second_half)
     second_wide = second_half.astype(f32)
     fourth_half = (2.0 * second_wide - matmul(second_half, second)).astype(bf16)
     fourth = core_halves(fourth_half)
-    mixed_half = (2.0 * (base_wide + second_wide) - matmul(base_half, second)).astype(bf16)
+    mixed_half = (
+        2.0 * (base_wide + second_wide)
+        - scale * (matmul(cov_half, second) + damp * second_wide)
+    ).astype(bf16)
     tail_half = (
         4.0 * fourth_half.astype(f32) + 2.0 * mixed_half.astype(f32) - matmul(mixed_half, fourth)
     ).astype(bf16)
@@ -106,11 +157,15 @@
     left = left.reshape(chips, 2, c, D // c // n, rows).transpose(2, 1, 0, 3, 4).reshape(D, rows)
     precond = 8.0 * left.astype(f32).T - dot_rows(left, tail)
 
+    total = sum_dp(jnp.sum(precond * precond))
+
     keep = lax.dynamic_slice_in_dim(precond, (grp_index % part) * cols, cols, 1)
     send = lax.dynamic_slice_in_dim(precond, (grp_index % part + part) * cols, cols, 1)
     sent = lax.ppermute(send.astype(bf16), "grp", [(j, part + j) for j in range(part)])
     precond = jnp.where(on_g, sent.astype(f32), keep)
-    total = lax.psum(jnp.sum(precond * precond), ("dp", "grp"))
+    total = lax.ppermute(total, "grp", [(j, part + j) for j in range(part)]) + jnp.where(
+        on_g, 0.0, total
+    )
     return precond * lax.rsqrt(total / (D * D) + epsilon)
 
 

time: 853 us -> 699 us (0.82)
  waiting for transfers between devices: 427 us -> 293 us
  starting transfers between devices: 7.86 us -> 54.6 us
  blocking collectives: 82.2 us -> 40.7 us
  other arithmetic: 60.4 us -> 25.7 us
  matrix products: 207 us -> 232 us
  local copies, waits for them, and re-layouts: 44.3 us -> 21.8 us
    reduce_scatter x2 -> x1, waiting for transfers between devices: 178 us -> 7.98 us  [reduce_rows(): lax.psum_scatter(x, 'dp', scatter_dimension=0, tiled=True, axis_index_gro...]
    ppermute x0 -> x39, waiting for transfers between devices: none -> 127 us  [the longest x28 66.3 us: ring_reduce(): got = lax.ppermute(totals[lane].astype(bf16), 'dp', moves)]
    all_gather x3 -> x1, waiting for transfers between devices: 166 us -> 74.6 us  [shards(): cov = lax.all_gather(cov_rows.astype(bf16), 'dp', axis=0, tiled=True)]
    ppermute x0 -> x39, starting transfers between devices: none -> 47.9 us  [the longest x28 29.2 us: ring_reduce(): got = lax.ppermute(totals[lane].astype(bf16), 'dp', moves)]
    psum x1 -> x0, blocking collectives: 40.7 us -> none  [shards(): total = lax.psum(jnp.sum(precond * precond), ('dp', 'grp'))]
    convert_element_type x1 -> x0, local copies, waits for them, and re-layouts: 28.1 us -> none  [shards(): wide = cov.astype(f32)]
    convert_element_type x2 -> x7, other arithmetic: 37.4 us -> 10.2 us  [the longest x6 9.03 us: ring_reduce(): got = lax.ppermute(totals[lane].astype(bf16), 'dp', moves)]
    dot_general x5, matrix products: 168 us -> 185 us  [matmul(): return jnp.dot(left, right, preferred_element_type=f32)]
  transfers between devices with their start and end apart: 14 -> 50, of which waited for: 9 -> 44; matrix products, arithmetic and copies ran while one was open for 15% -> 22% of each run, Pallas kernels for 0% -> 0%
where the time goes in v2:
time: 699 us; the launch traced here: 690 us
  waiting for transfers between devices  293 us (42%)
  matrix products  232 us (33%)
  starting transfers between devices  54.6 us (8%)
  blocking collectives  40.7 us (6%)
  other arithmetic  25.7 us (4%)
  between operations  22.6 us (3%)
  local copies, waits for them, and re-layouts  21.8 us (3%)
    dot_general x5, matrix products, matmul(): return jnp.dot(left, right, preferred_element_type=f32)  185 us
    all_gather x1, waiting for transfers between devices, shards(): cov = lax.all_gather(cov_rows.astype(bf16), 'dp', axis=0, tiled=True)  74.6 us
    ppermute x28, waiting for transfers between devices, ring_reduce(): got = lax.ppermute(totals[lane].astype(bf16), 'dp', moves)  66.3 us
    dot_general x3, matrix products, dot_rows(): lax.dot_general(left, right, (((0,), (0,)), ((), ())), preferred_element_...  46.9 us
    all_to_all x1, blocking collectives, shards(): left = lax.all_to_all(left, 'dp', split_axis=1, concat_axis=0, tiled=True)  40.7 us
    ppermute x1, waiting for transfers between devices, shards(): lax.ppermute(jnp.where(on_g, activations, cotangents), 'grp', [(0, 1), (1...  33.9 us
    ppermute x1, waiting for transfers between devices, shards(): rest = lax.ppermute(cotangents, 'grp', [(1, 0)])  32.9 us
    ppermute x1, waiting for transfers between devices, shards(): left = lax.ppermute(left, 'grp', [(part + j, j) for j in range(part)])  29.4 us
  transfers between devices with their start and end apart: 50, of which 44 were waited for; matrix products, arithmetic and copies ran while one was open for 22% of the time, Pallas kernels for 0%

profile of v2, /device:TPU:0, one launch (start us, length us, event | category | flops | bytes accessed | tf_op | source)
XLA Modules:
  0.0 690.2 jit_solution(17928989823888154691)
XLA Ops:
  7.4 1.7 copy.12
  9.1 2.3 copy.11
  11.6 3.0 collective-permute-start.1
  15.9 33.9 %collective-permute-done.1 = bf16[512,1536]{0,1:T(8,128)(2,1)S(1)} collective-permute-done((bf16[512,1536]{0,1:T(8,128)(2,1)S(1)}, bf16[512,1536]{0,1:T(8,128)(2,1)S(1)}, u32[]{:S(2)}, u32[]{:S(2)}) %collective-permute-start.1) | collective-permute-done | bytes 1572896 | tf_op jit(solution)/shard_map/ppermute | solution.py:88
  49.8 32.9 %collective-permute-done.3 = bf16[512,1536]{0,1:T(8,128)(2,1)S(1)} collective-permute-done((bf16[512,1536]{0,1:T(8,128)(2,1)S(1)}, bf16[512,1536]{0,1:T(8,128)(2,1)S(1)}, u32[]{:S(2)}, u32[]{:S(2)}) %collective-permute-start.3) | collective-permute-done | bytes 1572896 | tf_op jit(solution)/shard_map/ppermute | solution.py:106
  82.7 3.3 maximum_select_fusion.14
  86.2 5.7 collective-permute-done.2
  91.9 4.0 pad_maximum_fusion
  96.3 12.1 %convolution_convert_fusion = bf16[1536,3072]{1,0:T(8,128)(2,1)S(1)} fusion(bf16[1024,1536]{0,1:T(8,128)(2,1)S(1)} %bitcast.29, bf16[512,3072]{0,1:T(8,128)(2,1)} %copy-done.3, bf16[512,3072]{0,1:T(8,128)(2,1)} %get-tuple-element.39), kind=kOutput, calls=%fused_computation.31 | convolution fusion | flops 9680977920 | bytes 18874368 | tf_op jit(solution)/shard_map/dot_general | solution.py:13
  108.5 3.7 copy-done.2
  112.2 1.9 collective-permute-start.6
  114.3 1.8 collective-permute-start.20
  116.3 5.8 collective-permute-done.6
  122.1 1.9 collective-permute-done.27
  124.0 3.7 collective-permute-done.20
  127.6 1.5 collective-permute-done.13
  129.2 1.5 add_convert_fusion.23
  130.7 1.6 collective-permute-start.7
  132.7 1.6 collective-permute-start.21
  134.8 5.9 collective-permute-done.7
  140.7 1.6 collective-permute-done.28
  142.2 2.7 collective-permute-done.21
  146.2 1.5 add_convert_fusion.22
  147.7 1.6 collective-permute-start.8
  149.8 1.6 collective-permute-start.22
  151.8 5.8 collective-permute-done.8
  159.0 1.8 collective-permute-done.22
  162.1 1.5 add_convert_fusion.21
  163.6 1.5 collective-permute-start.9
  167.7 4.6 collective-permute-done.9
  173.6 2.0 collective-permute-done.23
  176.7 1.5 add_convert_fusion.20
  182.3 3.4 collective-permute-done.10
  186.5 3.0 collective-permute-done.24
  190.5 1.5 add_convert_fusion.19
  194.9 1.7 collective-permute-start.18
  196.6 2.2 collective-permute-done.11
  199.6 4.0 collective-permute-done.25
  210.3 2.7 collective-permute-done.12
  213.6 2.5 collective-permute-done.26
  226.1 2.2 collective-permute-done.35
  230.1 3.0 collective-permute-done.36
  233.7 3.9 collective-permute-done.37
  241.9 74.6 %all-gather.2.cloned.1.call-done = bf16[3072,3072]{1,0:T(8,128)(2,1)} async-done(((bf16[192,3072]{1,0:T(8,128)(2,1)}), bf16[3072,3072]{1,0:T(8,128)(2,1)}) %all-gather.2.cloned.1.call-update) | async-done | bytes 18874384 | tf_op jit(solution)/shard_map/all_gather | solution.py:120
  316.4 43.7 %fusion.4 = bf16[1536,3072]{1,0:T(8,128)(2,1)} fusion(f32[]{:T(128)S(6)} %mul.341, f32[]{:T(128)S(6)} %mul.349, f32[]{:T(128)S(6)} %div.28, s32[1536]{0:T(1024)S(1)} %iota_add_fusion, f32[]{:T(128)S(6)} %rsqrt.6, bf16[3072,3072]{1,0:T(8,128)(2,1)} %all-gather.2.cloned.1.call-done, s32[]{:T(128)S(6)} %select_n.386), kind=kOutput, calls=%fused_computation.10 | convolution fusion | flops 29052370944 | bytes 47195136 | tf_op jit(solution)/shard_map/dot_general | solution.py:17
  360.8 14.3 %collective-permute-done.38 = bf16[1536,3072]{1,0:T(8,128)(2,1)} collective-permute-done((bf16[1536,3072]{1,0:T(8,128)(2,1)}, bf16[1536,3072]{1,0:T(8,128)(2,1)}, u32[]{:S(2)}, u32[]{:S(2)}) %collective-permute-start.38) | collective-permute-done | bytes 9437216 | tf_op jit(solution)/shard_map/ppermute | solution.py:37
  375.1 40.3 %fusion.7 = bf16[1536,3072]{1,0:T(8,128)(2,1)} fusion(bf16[1536,3072]{1,0:T(8,128)(2,1)} %fusion.4, bf16[1536,3072]{1,0:T(8,128)(2,1)} %collective-permute-done.38, pred[]{:T(512)S(6)} %eq.71), kind=kOutput, calls=%fused_computation.13 | convolution fusion | flops 29094838272 | bytes 28311552 | tf_op jit(solution)/shard_map/dot_general | solution.py:17
  415.6 19.5 %fusion.31 = bf16[768,3072]{1,0:T(8,128)(2,1)} fusion(bf16[512,3072]{0,1:T(8,128)(2,1)} %collective-permute-done.4, bf16[512,1536]{0,1:T(8,128)(2,1)S(1)} %copy-done.5, bf16[512,1536]{0,1:T(8,128)(2,1)S(1)} %copy-done.1, pred[]{:T(512)S(6)} %ge.3, s32[]{:T(128)S(6)} %select_n.324, bf16[512,1536]{1,0:T(8,128)(2,1)} %param.2, ...), kind=kOutput, calls=%fused_computation.43 | convolution fusion | flops 4871946240 | bytes 20447236 | tf_op jit(solution)/shard_map/dot_general | solution.py:13
  435.1 46.2 %fusion.10 = bf16[1536,3072]{1,0:T(8,128)(2,1)} fusion(bf16[1536,3072]{1,0:T(8,128)(2,1)} %fusion.4, f32[]{:T(128)S(6)} %div.28, s32[1536]{0:T(1024)S(1)} %iota_add_fusion, f32[]{:T(128)S(6)} %rsqrt.6, bf16[1536,3072]{1,0:T(8,128)(2,1)} %collective-permute-done.38, pred[]{:T(512)S(6)} %eq.71, bf16[3072,3072]{1,0:T(8,128)(2,1)} %all-gather.2.cloned.1.call-done, ...), kind=kOutput, calls=%fused_computation.16 | convolution fusion | flops 29137305600 | bytes 56631808 | tf_op jit(solution)/shard_map/dot_general | solution.py:17
  481.3 41.1 %subtract_convert_fusion = bf16[1536,3072]{1,0:T(8,128)(2,1)} fusion(bf16[1536,3072]{1,0:T(8,128)(2,1)} %fusion.10, bf16[1536,3072]{1,0:T(8,128)(2,1)} %fusion.7, bf16[1536,3072]{1,0:T(8,128)(2,1)} %collective-permute-done.39, pred[]{:T(512)S(6)} %eq.71), kind=kOutput, calls=%fused_computation.28 | convolution fusion | flops 29108994048 | bytes 37748736 | tf_op jit(solution)/shard_map/dot_general | solution.py:17
  522.4 8.0 %reduce-scatter.2.cloned.1.call-done = bf16[96,3072]{1,0:T(8,128)(2,1)} async-done(((bf16[768,3072]{1,0:T(8,128)(2,1)}), bf16[96,3072]{1,0:T(8,128)(2,1)}) %reduce-scatter.2.cloned.1.call-update) | async-done | bytes 589840 | tf_op jit(solution)/shard_map/reduce_scatter | solution.py:48
  530.3 3.4 collective-permute-start.5
  533.7 12.6 %collective-permute-done.5 = bf16[96,3072]{1,0:T(8,128)(2,1)S(1)} collective-permute-done((bf16[96,3072]{1,0:T(8,128)(2,1)}, bf16[96,3072]{1,0:T(8,128)(2,1)S(1)}, u32[]{:S(2)}, u32[]{:S(2)}) %collective-permute-start.5) | collective-permute-done | bytes 589856 | tf_op jit(solution)/shard_map/ppermute | solution.py:115
  547.5 14.3 %subtract_convert_fusion.1 = bf16[192,3072]{1,0:T(8,128)(2,1)S(1)} fusion(bf16[192,3072]{1,0:T(8,128)(2,1)S(1)} %constant_dynamic-update-slice_fusion, bf16[1536,3072]{1,0:T(8,128)(2,1)} %collective-permute-done.40, bf16[1536,3072]{1,0:T(8,128)(2,1)} %subtract_convert_fusion, pred[]{:T(512)S(6)} %eq.71), kind=kOutput, calls=%fused_computation.52 | convolution fusion | flops 3711172608 | bytes 21233664 | tf_op jit(solution)/shard_map/dot_general | solution.py:17
  562.5 40.7 %all_to_all.19 = bf16[192,16,192]{0,2,1:T(8,128)(2,1)S(1)} all-to-all(bf16[192,16,192]{0,2,1:T(8,128)(2,1)S(1)} %bitcast.27), channel_id=1, replica_groups=mesh['dp'=16,'grp'=2] {'dp'}, dimensions={1} | all-to-all | bytes 2359296 | tf_op jit(solution)/shard_map/all_to_all | solution.py:155
  604.0 1.7 all_to_all.17
  607.0 29.4 %collective-permute-done.41 = bf16[3072,192]{0,1:T(8,128)(2,1)} collective-permute-done((bf16[3072,192]{0,1:T(8,128)(2,1)S(1)}, bf16[3072,192]{0,1:T(8,128)(2,1)}, u32[]{:S(2)}, u32[]{:S(2)}) %collective-permute-start.41) | collective-permute-done | bytes 1179680 | tf_op jit(solution)/shard_map/ppermute | solution.py:156
  636.4 5.5 reshape.28
  642.2 3.0 reshape.29
  645.1 15.3 %multiply_reduce_fusion = (f32[]{:T(128)}, f32[192,3072]{1,0:T(8,128)S(1)}) fusion(bf16[3072,192]{0,1:T(8,128)(2,1)} %reshape.29, bf16[1536,3072]{1,0:T(8,128)(2,1)} %collective-permute-done.40, bf16[1536,3072]{1,0:T(8,128)(2,1)} %subtract_convert_fusion, pred[]{:T(512)S(6)} %eq.71), kind=kOutput, calls=%fused_computation.51 | convolution fusion | flops 3711762432 | bytes 22413316 | tf_op jit(solution)/shard_map/dot_general | solution.py:13
  664.6 2.6 collective-permute-start.44
  668.8 3.2 collective-permute-start.45
  673.1 3.1 collective-permute-start.46
  678.2 2.6 collective-permute-start.47
  (93 shorter events, 55.2 us)
Async XLA Ops:
  7.4 309.1 %all-gather.2.cloned.1.call-start = ((), (), s32[]{:S(2)}) async-start(), calls=%async_computation.3 | async-start | bytes 20054016 | tf_op jit(solution)/shard_map/all_gather | solution.py:120
  9.1 76.9 %copy-start = (bf16[512,1536]{0,1:T(8,128)(2,1)}, bf16[512,1536]{0,1:T(8,128)(2,1)S(1)}, u32[]{:S(2)}) copy-start(bf16[512,1536]{0,1:T(8,128)(2,1)S(1)} %copy.12) | copy-start | bytes 4718596
  11.6 38.2 %collective-permute-start.1 = (bf16[512,1536]{0,1:T(8,128)(2,1)S(1)}, bf16[512,1536]{0,1:T(8,128)(2,1)S(1)}, u32[]{:S(2)}, u32[]{:S(2)}) collective-permute-start(bf16[512,1536]{0,1:T(8,128)(2,1)S(1)} %broadcast_select_fusion), channel_id=1, source_target_pairs={{0,1},{1,0},{2,3},{3,2},{4,5},{5,4},{6,7},{7,6},{8,9},{9,8},{10,11... | collective-permute-start | bytes 4718600 | tf_op jit(solution)/shard_map/ppermute | solution.py:88
  14.6 68.1 %collective-permute-start.3 = (bf16[512,1536]{0,1:T(8,128)(2,1)S(1)}, bf16[512,1536]{0,1:T(8,128)(2,1)S(1)}, u32[]{:S(2)}, u32[]{:S(2)}) collective-permute-start(bf16[512,1536]{0,1:T(8,128)(2,1)S(1)} %copy.12), channel_id=1, source_target_pairs={{1,0},{3,2},{5,4},{7,6},{9,8},{11,10},{13,12},{15,14},{17,16},{19,... | collective-permute-start | bytes 4718600 | tf_op jit(solution)/shard_map/ppermute | solution.py:106
  82.7 3.3 copy-start.4
  86.0 5.9 collective-permute-start.2
  91.9 4.0 copy-start.3
  108.4 3.7 copy-start.2
  112.2 9.9 %collective-permute-start.6 = (bf16[192,768]{1,0:T(8,128)(2,1)S(1)}, bf16[192,768]{1,0:T(8,128)(2,1)S(1)}, u32[]{:S(2)}, u32[]{:S(2)}) collective-permute-start(bf16[192,768]{1,0:T(8,128)(2,1)S(1)} %get-tuple-element.35), channel_id=1, source_target_pairs={{0,8},{2,10},{8,16},{10,18},{16,24},{18,26},{24,28},{26,30},{28,20... | collective-permute-start | bytes 884744 | tf_op jit(solution)/shard_map/ppermute | solution.py:76
  114.1 9.9 %collective-permute-start.27 = (bf16[192,768]{1,0:T(8,128)(2,1)S(1)}, bf16[192,768]{1,0:T(8,128)(2,1)S(1)}, u32[]{:S(2)}, u32[]{:S(2)}) collective-permute-start(bf16[192,768]{1,0:T(8,128)(2,1)S(1)} %get-tuple-element.36), channel_id=1, source_target_pairs={{0,4},{2,6},{8,0},{10,2},{16,8},{18,10},{24,16},{26,18},{28,24},{3... | collective-permute-start | bytes 884744 | tf_op jit(solution)/shard_map/ppermute | solution.py:76
  114.3 13.4 %collective-permute-start.20 = (bf16[192,768]{1,0:T(8,128)(2,1)S(1)}, bf16[192,768]{1,0:T(8,128)(2,1)S(1)}, u32[]{:S(2)}, u32[]{:S(2)}) collective-permute-start(bf16[192,768]{1,0:T(8,128)(2,1)S(1)} %get-tuple-element.37), channel_id=1, source_target_pairs={{0,8},{2,10},{8,16},{10,18},{16,24},{18,26},{24,28},{26,30},{28,20... | collective-permute-start | bytes 884744 | tf_op jit(solution)/shard_map/ppermute | solution.py:76
  116.1 13.1 %collective-permute-start.13 = (bf16[192,768]{1,0:T(8,128)(2,1)S(1)}, bf16[192,768]{1,0:T(8,128)(2,1)S(1)}, u32[]{:S(2)}, u32[]{:S(2)}) collective-permute-start(bf16[192,768]{1,0:T(8,128)(2,1)S(1)} %get-tuple-element.38), channel_id=1, source_target_pairs={{0,4},{2,6},{8,0},{10,2},{16,8},{18,10},{24,16},{26,18},{28,24},{3... | collective-permute-start | bytes 884744 | tf_op jit(solution)/shard_map/ppermute | solution.py:76
  130.7 10.0 %collective-permute-start.7 = (bf16[192,768]{1,0:T(8,128)(2,1)S(1)}, bf16[192,768]{1,0:T(8,128)(2,1)S(1)}, u32[]{:S(2)}, u32[]{:S(2)}) collective-permute-start(bf16[192,768]{1,0:T(8,128)(2,1)S(1)} %get-tuple-element.31), channel_id=1, source_target_pairs={{0,8},{2,10},{8,16},{10,18},{16,24},{18,26},{24,28},{26,30},{28,20... | collective-permute-start | bytes 884744 | tf_op jit(solution)/shard_map/ppermute | solution.py:76
  132.3 9.9 %collective-permute-start.28 = (bf16[192,768]{1,0:T(8,128)(2,1)S(1)}, bf16[192,768]{1,0:T(8,128)(2,1)S(1)}, u32[]{:S(2)}, u32[]{:S(2)}) collective-permute-start(bf16[192,768]{1,0:T(8,128)(2,1)S(1)} %get-tuple-element.32), channel_id=1, source_target_pairs={{0,4},{2,6},{8,0},{10,2},{16,8},{18,10},{24,16},{26,18},{28,24},{3... | collective-permute-start | bytes 884744 | tf_op jit(solution)/shard_map/ppermute | solution.py:76
  132.7 12.2 %collective-permute-start.21 = (bf16[192,768]{1,0:T(8,128)(2,1)S(1)}, bf16[192,768]{1,0:T(8,128)(2,1)S(1)}, u32[]{:S(2)}, u32[]{:S(2)}) collective-permute-start(bf16[192,768]{1,0:T(8,128)(2,1)S(1)} %get-tuple-element.33), channel_id=1, source_target_pairs={{0,8},{2,10},{8,16},{10,18},{16,24},{18,26},{24,28},{26,30},{28,20... | collective-permute-start | bytes 884744 | tf_op jit(solution)/shard_map/ppermute | solution.py:76
  134.3 11.9 %collective-permute-start.14 = (bf16[192,768]{1,0:T(8,128)(2,1)S(1)}, bf16[192,768]{1,0:T(8,128)(2,1)S(1)}, u32[]{:S(2)}, u32[]{:S(2)}) collective-permute-start(bf16[192,768]{1,0:T(8,128)(2,1)S(1)} %get-tuple-element.34), channel_id=1, source_target_pairs={{0,4},{2,6},{8,0},{10,2},{16,8},{18,10},{24,16},{26,18},{28,24},{3... | collective-permute-start | bytes 884744 | tf_op jit(solution)/shard_map/ppermute | solution.py:76
  147.7 9.9 %collective-permute-start.8 = (bf16[192,768]{1,0:T(8,128)(2,1)S(1)}, bf16[192,768]{1,0:T(8,128)(2,1)S(1)}, u32[]{:S(2)}, u32[]{:S(2)}) collective-permute-start(bf16[192,768]{1,0:T(8,128)(2,1)S(1)} %get-tuple-element.27), channel_id=1, source_target_pairs={{0,8},{2,10},{8,16},{10,18},{16,24},{18,26},{24,28},{26,30},{28,20... | collective-permute-start | bytes 884744 | tf_op jit(solution)/shard_map/ppermute | solution.py:76
  149.4 9.6 %collective-permute-start.29 = (bf16[192,768]{1,0:T(8,128)(2,1)S(1)}, bf16[192,768]{1,0:T(8,128)(2,1)S(1)}, u32[]{:S(2)}, u32[]{:S(2)}) collective-permute-start(bf16[192,768]{1,0:T(8,128)(2,1)S(1)} %get-tuple-element.28), channel_id=1, source_target_pairs={{0,4},{2,6},{8,0},{10,2},{16,8},{18,10},{24,16},{26,18},{28,24},{3... | collective-permute-start | bytes 884744 | tf_op jit(solution)/shard_map/ppermute | solution.py:76
  149.8 11.0 %collective-permute-start.22 = (bf16[192,768]{1,0:T(8,128)(2,1)S(1)}, bf16[192,768]{1,0:T(8,128)(2,1)S(1)}, u32[]{:S(2)}, u32[]{:S(2)}) collective-permute-start(bf16[192,768]{1,0:T(8,128)(2,1)S(1)} %get-tuple-element.29), channel_id=1, source_target_pairs={{0,8},{2,10},{8,16},{10,18},{16,24},{18,26},{24,28},{26,30},{28,20... | collective-permute-start | bytes 884744 | tf_op jit(solution)/shard_map/ppermute | solution.py:76
  151.4 10.7 %collective-permute-start.15 = (bf16[192,768]{1,0:T(8,128)(2,1)S(1)}, bf16[192,768]{1,0:T(8,128)(2,1)S(1)}, u32[]{:S(2)}, u32[]{:S(2)}) collective-permute-start(bf16[192,768]{1,0:T(8,128)(2,1)S(1)} %get-tuple-element.30), channel_id=1, source_target_pairs={{0,4},{2,6},{8,0},{10,2},{16,8},{18,10},{24,16},{26,18},{28,24},{3... | collective-permute-start | bytes 884744 | tf_op jit(solution)/shard_map/ppermute | solution.py:76
  163.6 8.7 %collective-permute-start.9 = (bf16[192,768]{1,0:T(8,128)(2,1)S(1)}, bf16[192,768]{1,0:T(8,128)(2,1)S(1)}, u32[]{:S(2)}, u32[]{:S(2)}) collective-permute-start(bf16[192,768]{1,0:T(8,128)(2,1)S(1)} %get-tuple-element.23), channel_id=1, source_target_pairs={{0,8},{2,10},{8,16},{10,18},{16,24},{18,26},{24,28},{26,30},{28,20... | collective-permute-start | bytes 884744 | tf_op jit(solution)/shard_map/ppermute | solution.py:76
  165.2 8.4 %collective-permute-start.30 = (bf16[192,768]{1,0:T(8,128)(2,1)S(1)}, bf16[192,768]{1,0:T(8,128)(2,1)S(1)}, u32[]{:S(2)}, u32[]{:S(2)}) collective-permute-start(bf16[192,768]{1,0:T(8,128)(2,1)S(1)} %get-tuple-element.24), channel_id=1, source_target_pairs={{0,4},{2,6},{8,0},{10,2},{16,8},{18,10},{24,16},{26,18},{28,24},{3... | collective-permute-start | bytes 884744 | tf_op jit(solution)/shard_map/ppermute | solution.py:76
  165.7 9.8 %collective-permute-start.23 = (bf16[192,768]{1,0:T(8,128)(2,1)S(1)}, bf16[192,768]{1,0:T(8,128)(2,1)S(1)}, u32[]{:S(2)}, u32[]{:S(2)}) collective-permute-start(bf16[192,768]{1,0:T(8,128)(2,1)S(1)} %get-tuple-element.25), channel_id=1, source_target_pairs={{0,8},{2,10},{8,16},{10,18},{16,24},{18,26},{24,28},{26,30},{28,20... | collective-permute-start | bytes 884744 | tf_op jit(solution)/shard_map/ppermute | solution.py:76
  167.2 9.5 %collective-permute-start.16 = (bf16[192,768]{1,0:T(8,128)(2,1)S(1)}, bf16[192,768]{1,0:T(8,128)(2,1)S(1)}, u32[]{:S(2)}, u32[]{:S(2)}) collective-permute-start(bf16[192,768]{1,0:T(8,128)(2,1)S(1)} %get-tuple-element.26), channel_id=1, source_target_pairs={{0,4},{2,6},{8,0},{10,2},{16,8},{18,10},{24,16},{26,18},{28,24},{3... | collective-permute-start | bytes 884744 | tf_op jit(solution)/shard_map/ppermute | solution.py:76
  178.2 7.5 %collective-permute-start.10 = (bf16[192,768]{1,0:T(8,128)(2,1)S(1)}, bf16[192,768]{1,0:T(8,128)(2,1)S(1)}, u32[]{:S(2)}, u32[]{:S(2)}) collective-permute-start(bf16[192,768]{1,0:T(8,128)(2,1)S(1)} %get-tuple-element.19), channel_id=1, source_target_pairs={{0,8},{2,10},{8,16},{10,18},{16,24},{18,26},{24,28},{26,30},{28,20... | collective-permute-start | bytes 884744 | tf_op jit(solution)/shard_map/ppermute | solution.py:76
  179.2 7.3 %collective-permute-start.31 = (bf16[192,768]{1,0:T(8,128)(2,1)S(1)}, bf16[192,768]{1,0:T(8,128)(2,1)S(1)}, u32[]{:S(2)}, u32[]{:S(2)}) collective-permute-start(bf16[192,768]{1,0:T(8,128)(2,1)S(1)} %get-tuple-element.20), channel_id=1, source_target_pairs={{0,4},{2,6},{8,0},{10,2},{16,8},{18,10},{24,16},{26,18},{28,24},{3... | collective-permute-start | bytes 884744 | tf_op jit(solution)/shard_map/ppermute | solution.py:76
  180.3 9.2 %collective-permute-start.24 = (bf16[192,768]{1,0:T(8,128)(2,1)S(1)}, bf16[192,768]{1,0:T(8,128)(2,1)S(1)}, u32[]{:S(2)}, u32[]{:S(2)}) collective-permute-start(bf16[192,768]{1,0:T(8,128)(2,1)S(1)} %get-tuple-element.21), channel_id=1, source_target_pairs={{0,8},{2,10},{8,16},{10,18},{16,24},{18,26},{24,28},{26,30},{28,20... | collective-permute-start | bytes 884744 | tf_op jit(solution)/shard_map/ppermute | solution.py:76
  181.2 9.3 %collective-permute-start.17 = (bf16[192,768]{1,0:T(8,128)(2,1)S(1)}, bf16[192,768]{1,0:T(8,128)(2,1)S(1)}, u32[]{:S(2)}, u32[]{:S(2)}) collective-permute-start(bf16[192,768]{1,0:T(8,128)(2,1)S(1)} %get-tuple-element.22), channel_id=1, source_target_pairs={{0,4},{2,6},{8,0},{10,2},{16,8},{18,10},{24,16},{26,18},{28,24},{3... | collective-permute-start | bytes 884744 | tf_op jit(solution)/shard_map/ppermute | solution.py:76
  192.0 6.8 collective-permute-start.11
  192.9 6.7 collective-permute-start.32
  194.1 9.5 %collective-permute-start.25 = (bf16[192,768]{1,0:T(8,128)(2,1)S(1)}, bf16[192,768]{1,0:T(8,128)(2,1)S(1)}, u32[]{:S(2)}, u32[]{:S(2)}) collective-permute-start(bf16[192,768]{1,0:T(8,128)(2,1)S(1)} %get-tuple-element.17), channel_id=1, source_target_pairs={{0,8},{2,10},{8,16},{10,18},{16,24},{18,26},{24,28},{26,30},{28,20... | collective-permute-start | bytes 884744 | tf_op jit(solution)/shard_map/ppermute | solution.py:76
  194.9 9.8 %collective-permute-start.18 = (bf16[192,768]{1,0:T(8,128)(2,1)S(1)}, bf16[192,768]{1,0:T(8,128)(2,1)S(1)}, u32[]{:S(2)}, u32[]{:S(2)}) collective-permute-start(bf16[192,768]{1,0:T(8,128)(2,1)S(1)} %get-tuple-element.18), channel_id=1, source_target_pairs={{0,4},{2,6},{8,0},{10,2},{16,8},{18,10},{24,16},{26,18},{28,24},{3... | collective-permute-start | bytes 884744 | tf_op jit(solution)/shard_map/ppermute | solution.py:76
  206.2 6.8 collective-permute-start.12
  206.9 6.7 collective-permute-start.33
  208.2 7.9 %collective-permute-start.26 = (bf16[192,768]{1,0:T(8,128)(2,1)S(1)}, bf16[192,768]{1,0:T(8,128)(2,1)S(1)}, u32[]{:S(2)}, u32[]{:S(2)}) collective-permute-start(bf16[192,768]{1,0:T(8,128)(2,1)S(1)} %get-tuple-element.13), channel_id=1, source_target_pairs={{0,8},{2,10},{8,16},{10,18},{16,24},{18,26},{24,28},{26,30},{28,20... | collective-permute-start | bytes 884744 | tf_op jit(solution)/shard_map/ppermute | solution.py:76
  208.9 7.9 %collective-permute-start.19 = (bf16[192,768]{1,0:T(8,128)(2,1)S(1)}, bf16[192,768]{1,0:T(8,128)(2,1)S(1)}, u32[]{:S(2)}, u32[]{:S(2)}) collective-permute-start(bf16[192,768]{1,0:T(8,128)(2,1)S(1)} %get-tuple-element.14), channel_id=1, source_target_pairs={{0,4},{2,6},{8,0},{10,2},{16,8},{18,10},{24,16},{26,18},{28,24},{3... | collective-permute-start | bytes 884744 | tf_op jit(solution)/shard_map/ppermute | solution.py:76
  219.5 310.9 %reduce-scatter.2.cloned.1.call-start = ((), (), s32[]{:S(2)}) async-start(), calls=%async_computation.2 | async-start | bytes 5308416 | tf_op jit(solution)/shard_map/reduce_scatter | solution.py:48
  222.3 1.1 collective-permute-start.34
  224.7 3.5 collective-permute-start.35
  229.5 3.5 collective-permute-start.36
  233.1 4.4 collective-permute-start.37
  360.1 15.0 %collective-permute-start.38 = (bf16[1536,3072]{1,0:T(8,128)(2,1)}, bf16[1536,3072]{1,0:T(8,128)(2,1)}, u32[]{:S(2)}, u32[]{:S(2)}) collective-permute-start(bf16[1536,3072]{1,0:T(8,128)(2,1)} %fusion.4), channel_id=1, source_target_pairs={{0,2},{2,0},{4,6},{6,4},{8,10},{10,8},{12,14},{14,12},{16,18},{18,... | collective-permute-start | bytes 28311560 | tf_op jit(solution)/shard_map/ppermute | solution.py:37
  360.3 55.3 %collective-permute-start = (bf16[512,1536]{1,0:T(8,128)(2,1)}, bf16[512,1536]{1,0:T(8,128)(2,1)}, u32[]{:S(2)}, u32[]{:S(2)}) collective-permute-start(bf16[512,1536]{1,0:T(8,128)(2,1)} %param.2), channel_id=1, source_target_pairs={{0,2},{2,0},{4,6},{6,4},{8,10},{10,8},{12,14},{14,12},{16,18},{18,... | collective-permute-start | bytes 4718600 | tf_op jit(solution)/shard_map/ppermute | solution.py:37
  360.6 55.0 %copy-start.1 = (bf16[512,1536]{0,1:T(8,128)(2,1)S(1)}, bf16[512,1536]{0,1:T(8,128)(2,1)}, u32[]{:S(2)}) copy-start(bf16[512,1536]{0,1:T(8,128)(2,1)} %copy-done) | copy-start | bytes 4718596
  360.6 55.0 %copy-start.5 = (bf16[512,1536]{0,1:T(8,128)(2,1)S(1)}, bf16[512,1536]{0,1:T(8,128)(2,1)}, u32[]{:S(2)}) copy-start(bf16[512,1536]{0,1:T(8,128)(2,1)} %copy-done.4) | copy-start | bytes 4718596
  360.6 55.0 %collective-permute-start.4 = (bf16[512,3072]{0,1:T(8,128)(2,1)}, bf16[512,3072]{0,1:T(8,128)(2,1)}, u32[]{:S(2)}, u32[]{:S(2)}) collective-permute-start(bf16[512,3072]{0,1:T(8,128)(2,1)} %get-tuple-element.40), channel_id=1, source_target_pairs={{0,2},{2,0},{4,6},{6,4},{8,10},{10,8},{12,14},{14,12},{16,18},{18,... | collective-permute-start | bytes 9437192 | tf_op jit(solution)/shard_map/ppermute | solution.py:37
  415.4 65.8 %collective-permute-start.39 = (bf16[1536,3072]{1,0:T(8,128)(2,1)}, bf16[1536,3072]{1,0:T(8,128)(2,1)}, u32[]{:S(2)}, u32[]{:S(2)}) collective-permute-start(bf16[1536,3072]{1,0:T(8,128)(2,1)} %fusion.7), channel_id=1, source_target_pairs={{0,2},{2,0},{4,6},{6,4},{8,10},{10,8},{12,14},{14,12},{16,18},{18,... | collective-permute-start | bytes 28311560 | tf_op jit(solution)/shard_map/ppermute | solution.py:37
  522.3 25.2 %collective-permute-start.40 = (bf16[1536,3072]{1,0:T(8,128)(2,1)}, bf16[1536,3072]{1,0:T(8,128)(2,1)}, u32[]{:S(2)}, u32[]{:S(2)}) collective-permute-start(bf16[1536,3072]{1,0:T(8,128)(2,1)} %subtract_convert_fusion), channel_id=1, source_target_pairs={{0,2},{2,0},{4,6},{6,4},{8,10},{10,8},{12,14},{14,12},{16,18},{18,... | collective-permute-start | bytes 28311560 | tf_op jit(solution)/shard_map/ppermute | solution.py:37
  530.3 16.0 %collective-permute-start.5 = (bf16[96,3072]{1,0:T(8,128)(2,1)}, bf16[96,3072]{1,0:T(8,128)(2,1)S(1)}, u32[]{:S(2)}, u32[]{:S(2)}) collective-permute-start(bf16[96,3072]{1,0:T(8,128)(2,1)} %reduce-scatter.2.cloned.1.call-done), channel_id=1, source_target_pairs={{0,1},{2,3},{4,5},{6,7},{8,9},{10,11},{12,13},{14,15},{16,17},{18,... | collective-permute-start | bytes 1769480 | tf_op jit(solution)/shard_map/ppermute | solution.py:115
  605.7 30.7 %collective-permute-start.41 = (bf16[3072,192]{0,1:T(8,128)(2,1)S(1)}, bf16[3072,192]{0,1:T(8,128)(2,1)}, u32[]{:S(2)}, u32[]{:S(2)}) collective-permute-start(bf16[3072,192]{0,1:T(8,128)(2,1)S(1)} %all_to_all.17), channel_id=1, source_target_pairs={{1,0},{3,2},{5,4},{7,6},{9,8},{11,10},{13,12},{15,14},{17,16},{19,... | collective-permute-start | bytes 3538952 | tf_op jit(solution)/shard_map/ppermute | solution.py:156
  660.5 21.0 %collective-permute-start.42 = (bf16[192,1536]{1,0:T(8,128)(2,1)S(1)}, bf16[192,1536]{1,0:T(8,128)(2,1)S(1)}, u32[]{:S(2)}, u32[]{:S(2)}) collective-permute-start(bf16[192,1536]{1,0:T(8,128)(2,1)S(1)} %dynamic_slice.205), channel_id=1, source_target_pairs={{0,1},{2,3},{4,5},{6,7},{8,9},{10,11},{12,13},{14,15},{16,17},{18,... | collective-permute-start | bytes 1769480 | tf_op jit(solution)/shard_map/ppermute | solution.py:164
  661.9 1.5 collective-permute-start.43
  664.6 3.7 collective-permute-start.44
  668.8 3.7 collective-permute-start.45
  673.1 4.6 collective-permute-start.46
  678.2 2.6 collective-permute-start.47
Sparse Core Ops, SparseCore 0:
  219.6 96.7 all-gather.1
Sparse Core Ops, SparseCore 1:
  435.2 95.1 reduce-scatter.1

commit v3 on v2

--- a/solution.py
+++ b/solution.py
@@ -1,8 +1,13 @@
+import math
+
 import jax
 import jax.numpy as jnp
 from jax import lax
+from jax.experimental import pallas as pl
+from jax.experimental.pallas import tpu as pltpu
 from jax.sharding import PartitionSpec as P
 
+ITERS = 3
 damping = 0.05
 epsilon = 1e-06
 f32 = jnp.float32
@@ -13,8 +18,42 @@
     return lax.dot_general(left, right, (((0,), (0,)), ((), ())), preferred_element_type=f32)
 
 
-def matmul(left, right):
-    return jnp.dot(left, right, preferred_element_type=f32)
+def series(start, cov, scale, damp):
+    rows, D = start.shape
+    width = math.gcd(D, 512)
+    terms = 2**ITERS - 1
+
+    def kernel(scalar_ref, start_ref, cov_ref, out_ref, narrow_ref):
+        scale = scalar_ref[0]
+        damp = scalar_ref[1]
+        out_ref[...] = start_ref[...]
+
+        @pl.loop(0, terms)
+        def _(term):
+            narrow_ref[...] = out_ref[...].astype(bf16)
+
+            @pl.loop(0, D // width)
+            def _(block):
+                at = pl.ds(pl.multiple_of(block * width, width), width)
+                product = jnp.dot(narrow_ref[...], cov_ref[:, at], preferred_element_type=f32)
+                total = out_ref[:, at]
+                out_ref[:, at] = start_ref[:, at] + total - scale * (product + damp * total)
+
+    vmem = pl.BlockSpec(memory_space=pltpu.VMEM)
+    return pl.pallas_call(
+        kernel,
+        out_shape=jax.ShapeDtypeStruct((rows, D), f32),
+        in_specs=[pl.BlockSpec(memory_space=pltpu.SMEM), vmem, vmem],
+        out_specs=vmem,
+        scratch_shapes=[pltpu.VMEM((rows, D), bf16)],
+        compiler_params=pltpu.CompilerParams(vmem_limit_bytes=D * D * 2 + 24 * 1024 * 1024),
+        cost_estimate=pl.CostEstimate(
+            flops=2 * terms * rows * D * D,
+            bytes_accessed=2 * D * D + 8 * rows * D,
+            transcendentals=0,
+        ),
+        name="series",
+    )(jnp.stack([scale, damp]), start, cov)
 
 
 def shards(activations, cotangents):
@@ -31,23 +70,9 @@
     core = dp_index % 2
     on_g = grp_index >= part
     pairs = [(i, i ^ 1) for i in range(n)]
-    same_core = [list(range(0, n, 2)), list(range(1, n, 2))]
 
     def other_core(x):
         return lax.ppermute(x, "dp", pairs)
-
-    def core_halves(mine):
-        theirs = other_core(mine)
-        return jnp.where(
-            core == 0,
-            jnp.concatenate([mine, theirs], axis=0),
-            jnp.concatenate([theirs, mine], axis=0),
-        )
-
-    def reduce_rows(x):
-        return lax.psum_scatter(
-            x, "dp", scatter_dimension=0, tiled=True, axis_index_groups=same_core
-        )
 
     ring = list(range(0, chips, 2)) + list(range(chips - 1, 0, -2))
     chip = dp_index // 2
@@ -55,11 +80,12 @@
 
     def ring_reduce(x, lanes):
         width = x.shape[1] // (2 * lanes)
+        count = x.shape[0] // chips
 
         def block(lane, spot):
             spot = (spot + 2 * chips) % chips
             owner = jnp.where(spot < chips // 2, 2 * spot, 2 * (chips - 1 - spot) + 1)
-            piece = lax.dynamic_slice(x, (owner * rows, lane * width), (rows, width))
+            piece = lax.dynamic_slice(x, (owner * count, lane * width), (count, width))
             return piece.astype(f32)
 
         totals = [None] * (2 * lanes)
@@ -100,7 +126,10 @@
     my_half = lax.dynamic_index_in_dim(
         mine.reshape(mine.shape[0], chips, 2, rows), core, 2, keepdims=False
     ).reshape(mine.shape[0], half)
-    cov_rows = ring_reduce(dot_rows(my_half, mine).astype(bf16), 2)
+    cov_part, cotangents = lax.optimization_barrier(
+        (dot_rows(my_half, mine).astype(bf16), cotangents)
+    )
+    cov_rows = ring_reduce(cov_part, 2)
 
     if c == 2:
         rest = lax.ppermute(cotangents, "grp", [(1, 0)])
@@ -110,7 +139,7 @@
         all_grads = jnp.where(on_g, mine, all_grads)
     acts = jnp.concatenate([activations, other_core(activations)], axis=0)
     acts = lax.dynamic_slice_in_dim(acts, core * (cols // 2), cols // 2, 1)
-    grad_rows = reduce_rows(dot_rows(acts, all_grads).astype(bf16))
+    grad_rows = ring_reduce(dot_rows(acts, all_grads).astype(bf16), 1).astype(bf16)
     if c == 2:
         first = lax.ppermute(grad_rows, "grp", [(0, 1)])
         grad_rows = jnp.concatenate([first, grad_rows], axis=0)
@@ -127,35 +156,11 @@
     damp = damping * trace / D
     scale = lax.rsqrt(square + 2.0 * damp * trace + D * damp * damp)
 
-    def my_rows(x):
-        return lax.dynamic_slice_in_dim(x, core * half, half, 0)
-
-    cov_half = my_rows(cov)
-    cov_wide = cov_half.astype(f32)
-    damp_half = jnp.where(diag_mask(core * half, half), damp, 0.0)
-    base_wide = scale * (cov_wide + damp_half)
-    base_square = scale * scale * (
-        matmul(cov_half, cov) + 2.0 * damp * cov_wide + damp * damp_half
-    )
-    second_half = (2.0 * base_wide - base_square).astype(bf16)
-    second = core_halves(second_half)
-    second_wide = second_half.astype(f32)
-    fourth_half = (2.0 * second_wide - matmul(second_half, second)).astype(bf16)
-    fourth = core_halves(fourth_half)
-    mixed_half = (
-        2.0 * (base_wide + second_wide)
-        - scale * (matmul(cov_half, second) + damp * second_wide)
-    ).astype(bf16)
-    tail_half = (
-        4.0 * fourth_half.astype(f32) + 2.0 * mixed_half.astype(f32) - matmul(mixed_half, fourth)
-    ).astype(bf16)
-    tail = core_halves(tail_half)
-
-    left = (8.0 * grad_rows.astype(f32) - matmul(grad_rows, tail)).astype(bf16)
+    left = series(grad_rows.astype(f32), cov, scale, damp).astype(bf16)
     left = lax.all_to_all(left, "dp", split_axis=1, concat_axis=0, tiled=True)
     left = lax.ppermute(left, "grp", [(part + j, j) for j in range(part)])
     left = left.reshape(chips, 2, c, D // c // n, rows).transpose(2, 1, 0, 3, 4).reshape(D, rows)
-    precond = 8.0 * left.astype(f32).T - dot_rows(left, tail)
+    precond = series(left.T.astype(f32), cov, scale, damp)
 
     total = sum_dp(jnp.sum(precond * precond))
 

time: 699 us -> 561 us (0.80); the launches traced: 690 us -> 560 us
  matrix products: 232 us -> 24.9 us
  Pallas kernels: 0 us -> 82.4 us
  waiting for transfers between devices: 293 us -> 254 us
  starting transfers between devices: 54.6 us -> 69.8 us
  other arithmetic: 25.7 us -> 36.8 us
  local copies, waits for them, and re-layouts: 21.8 us -> 31.7 us
    dot_general x5 -> x0, matrix products: 185 us -> none  [matmul(): return jnp.dot(left, right, preferred_element_type=f32)]
    pallas_call x0 -> x2, Pallas kernels: none -> 82.4 us  [series(): pl.pallas_call(kernel, out_shape=jax.ShapeDtypeStruct((rows, D), f32), in...]
    all_gather x1, waiting for transfers between devices: 74.6 us -> 0.02 us  [shards(): cov = lax.all_gather(cov_rows.astype(bf16), 'dp', axis=0, tiled=True)]
    ppermute x28 -> x42, waiting for transfers between devices: 66.3 us -> 135 us  [ring_reduce(): got = lax.ppermute(totals[lane].astype(bf16), 'dp', moves)]
    dot_general x3 -> x2, matrix products: 46.9 us -> 24.9 us  [dot_rows(): lax.dot_general(left, right, (((0,), (0,)), ((), ())), preferred_element_...]
    ppermute x28 -> x42, starting transfers between devices: 29.2 us -> 43.3 us  [ring_reduce(): got = lax.ppermute(totals[lane].astype(bf16), 'dp', moves)]
    convert_element_type x0 -> x3, local copies, waits for them, and re-layouts: none -> 14.1 us  [shards(): precond = series(left.T.astype(f32), cov, scale, damp)]
    ppermute x1, waiting for transfers between devices: 12.6 us -> 0.01 us  [shards(): first = lax.ppermute(grad_rows, 'grp', [(0, 1)])]
  transfers between devices with their start and end apart: 50 -> 60, of which waited for: 44 -> 54; matrix products, arithmetic and copies ran while one was open for 22% -> 6% of each run, Pallas kernels for 0% -> 0%
where the time goes in v3:
time: 561 us; the launch traced here: 560 us
  waiting for transfers between devices  254 us (45%)
  Pallas kernels  82.4 us (15%)
  starting transfers between devices  69.8 us (12%)
  blocking collectives  39.8 us (7%)
  other arithmetic  36.8 us (7%)
  local copies, waits for them, and re-layouts  31.7 us (6%)
  matrix products  24.9 us (4%)
  between operations  21.4 us (4%)
    ppermute x42, waiting for transfers between devices, ring_reduce(): got = lax.ppermute(totals[lane].astype(bf16), 'dp', moves)  135 us
    pallas_call x2, Pallas kernels, series(): pl.pallas_call(kernel, out_shape=jax.ShapeDtypeStruct((rows, D), f32), in...  82.4 us
    ppermute x42, starting transfers between devices, ring_reduce(): got = lax.ppermute(totals[lane].astype(bf16), 'dp', moves)  43.3 us
    all_to_all x1, blocking collectives, shards(): left = lax.all_to_all(left, 'dp', split_axis=1, concat_axis=0, tiled=True)  39.8 us
    ppermute x1, waiting for transfers between devices, shards(): lax.ppermute(jnp.where(on_g, activations, cotangents), 'grp', [(0, 1), (1...  34.4 us
    ppermute x1, waiting for transfers between devices, shards(): left = lax.ppermute(left, 'grp', [(part + j, j) for j in range(part)])  29.2 us
    ppermute x1, waiting for transfers between devices, shards(): rest = lax.ppermute(cotangents, 'grp', [(1, 0)])  29.1 us
    dot_general x2, matrix products, dot_rows(): lax.dot_general(left, right, (((0,), (0,)), ((), ())), preferred_element_...  24.9 us
  transfers between devices with their start and end apart: 60, of which 54 were waited for; matrix products, arithmetic and copies ran while one was open for 6% of the time, Pallas kernels for 0%

profile of v3, /device:TPU:0, one launch (start us, length us, event | category | flops | bytes accessed | tf_op | source)
XLA Modules:
  0.0 560.4 jit_solution(9793350817403452831)
XLA Ops:
  6.5 1.7 copy.12
  8.3 1.7 copy.11
  10.2 3.0 collective-permute-start
  13.2 34.4 %collective-permute-done = bf16[512,1536]{0,1:T(8,128)(2,1)S(1)} collective-permute-done((bf16[512,1536]{0,1:T(8,128)(2,1)S(1)}, bf16[512,1536]{0,1:T(8,128)(2,1)S(1)}, u32[]{:S(2)}, u32[]{:S(2)}) %collective-permute-start) | collective-permute-done | bytes 1572896 | tf_op jit(solution)/shard_map/ppermute | solution.py:114
  47.6 2.2 maximum_select_fusion.4
  49.7 5.9 %collective-permute-done.1 = bf16[512,3072]{0,1:T(8,128)(2,1)S(1)} collective-permute-done((bf16[512,3072]{0,1:T(8,128)(2,1)}, bf16[512,3072]{0,1:T(8,128)(2,1)S(1)}, u32[]{:S(2)}, u32[]{:S(2)}) %collective-permute-start.1) | collective-permute-done | bytes 3145760 | tf_op jit(solution)/shard_map/ppermute | solution.py:75
  55.6 4.0 pad_maximum_fusion
  60.0 12.1 %convolution_convert_fusion = bf16[1536,3072]{1,0:T(8,128)(2,1)S(1)} fusion(bf16[1024,1536]{0,1:T(8,128)(2,1)S(1)} %bitcast.26, bf16[512,3072]{0,1:T(8,128)(2,1)} %copy-done.12, bf16[512,3072]{0,1:T(8,128)(2,1)} %maximum_select_fusion.4), kind=kOutput, calls=%fused_computation | convolution fusion | flops 9680977920 | bytes 18874368 | tf_op jit(solution)/shard_map/dot_general | solution.py:18
  72.1 3.7 copy-done.1
  75.9 1.9 collective-permute-start.2
  78.0 1.8 collective-permute-start.16
  80.0 5.8 %collective-permute-done.2 = bf16[192,768]{1,0:T(8,128)(2,1)S(1)} collective-permute-done((bf16[192,768]{1,0:T(8,128)(2,1)S(1)}, bf16[192,768]{1,0:T(8,128)(2,1)S(1)}, u32[]{:S(2)}, u32[]{:S(2)}) %collective-permute-start.2) | collective-permute-done | bytes 294944 | tf_op jit(solution)/shard_map/ppermute | solution.py:102
  85.8 1.9 collective-permute-done.23
  87.7 3.7 collective-permute-done.16
  94.4 1.6 collective-permute-start.3
  96.4 1.6 collective-permute-start.17
  98.5 5.9 %collective-permute-done.3 = bf16[192,768]{1,0:T(8,128)(2,1)S(1)} collective-permute-done((bf16[192,768]{1,0:T(8,128)(2,1)S(1)}, bf16[192,768]{1,0:T(8,128)(2,1)S(1)}, u32[]{:S(2)}, u32[]{:S(2)}) %collective-permute-start.3) | collective-permute-done | bytes 294944 | tf_op jit(solution)/shard_map/ppermute | solution.py:102
  104.4 1.6 collective-permute-done.24
  105.9 2.7 collective-permute-done.17
  111.4 1.6 collective-permute-start.4
  113.5 1.6 collective-permute-start.18
  115.5 5.8 %collective-permute-done.4 = bf16[192,768]{1,0:T(8,128)(2,1)S(1)} collective-permute-done((bf16[192,768]{1,0:T(8,128)(2,1)S(1)}, bf16[192,768]{1,0:T(8,128)(2,1)S(1)}, u32[]{:S(2)}, u32[]{:S(2)}) %collective-permute-start.4) | collective-permute-done | bytes 294944 | tf_op jit(solution)/shard_map/ppermute | solution.py:102
  122.6 1.9 collective-permute-done.18
  127.3 1.6 collective-permute-start.5
  131.4 4.6 collective-permute-done.5
  137.3 1.9 collective-permute-done.19
  146.0 3.4 collective-permute-done.6
  150.2 3.0 collective-permute-done.20
  159.8 2.7 collective-permute-done.7
  163.3 4.0 collective-permute-done.21
  173.9 2.7 collective-permute-done.8
  177.2 2.5 collective-permute-done.22
  186.7 29.1 %collective-permute-done.35 = bf16[512,1536]{0,1:T(8,128)(2,1)S(1)} collective-permute-done((bf16[512,1536]{0,1:T(8,128)(2,1)S(1)}, bf16[512,1536]{0,1:T(8,128)(2,1)S(1)}, u32[]{:S(2)}, u32[]{:S(2)}) %collective-permute-start.35) | collective-permute-done | bytes 1572896 | tf_op jit(solution)/shard_map/ppermute | solution.py:135
  215.8 2.0 pad_maximum_fusion.1
  218.5 5.8 %collective-permute-done.34 = bf16[512,1536]{1,0:T(8,128)(2,1)} collective-permute-done((bf16[512,1536]{1,0:T(8,128)(2,1)S(1)}, bf16[512,1536]{1,0:T(8,128)(2,1)}, u32[]{:S(2)}, u32[]{:S(2)}) %collective-permute-start.34) | collective-permute-done | bytes 1572896 | tf_op jit(solution)/shard_map/ppermute | solution.py:75
  224.3 2.4 collective-permute-done.36
  226.7 12.7 %fusion.6 = bf16[768,3072]{1,0:T(8,128)(2,1)S(1)} fusion(bf16[512,3072]{0,1:T(8,128)(2,1)} %collective-permute-done.36, bf16[512,1536]{0,1:T(8,128)(2,1)} %copy-done.14, bf16[512,1536]{0,1:T(8,128)(2,1)S(1)} %copy.16, pred[]{:T(512)S(6)} %ge.3, s32[]{:T(128)S(6)} %select_n.455, bf16[512,1536]{1,0:T(8,128)(2,1)S(1)} %copy-done.13, ...), kind=kOutput, calls=%fused_computation.9 | convolution fusion | flops 4871946240 | bytes 20447236 | tf_op jit(solution)/shard_map/dot_general | solution.py:18
  239.5 2.1 copy-done.11
  243.7 13.9 %collective-permute-done.37 = bf16[96,1536]{1,0:T(8,128)(2,1)S(1)} collective-permute-done((bf16[96,1536]{1,0:T(8,128)(2,1)S(1)}, bf16[96,1536]{1,0:T(8,128)(2,1)S(1)}, u32[]{:S(2)}, u32[]{:S(2)}) %collective-permute-start.37) | collective-permute-done | bytes 294944 | tf_op jit(solution)/shard_map/ppermute | solution.py:102
  261.7 13.5 %collective-permute-done.38 = bf16[96,1536]{1,0:T(8,128)(2,1)S(1)} collective-permute-done((bf16[96,1536]{1,0:T(8,128)(2,1)S(1)}, bf16[96,1536]{1,0:T(8,128)(2,1)S(1)}, u32[]{:S(2)}, u32[]{:S(2)}) %collective-permute-start.38) | collective-permute-done | bytes 294944 | tf_op jit(solution)/shard_map/ppermute | solution.py:102
  278.9 13.2 %collective-permute-done.39 = bf16[96,1536]{1,0:T(8,128)(2,1)S(1)} collective-permute-done((bf16[96,1536]{1,0:T(8,128)(2,1)S(1)}, bf16[96,1536]{1,0:T(8,128)(2,1)S(1)}, u32[]{:S(2)}, u32[]{:S(2)}) %collective-permute-start.39) | collective-permute-done | bytes 294944 | tf_op jit(solution)/shard_map/ppermute | solution.py:102
  295.7 10.1 %collective-permute-done.40 = bf16[96,1536]{1,0:T(8,128)(2,1)S(1)} collective-permute-done((bf16[96,1536]{1,0:T(8,128)(2,1)S(1)}, bf16[96,1536]{1,0:T(8,128)(2,1)S(1)}, u32[]{:S(2)}, u32[]{:S(2)}) %collective-permute-start.40) | collective-permute-done | bytes 294944 | tf_op jit(solution)/shard_map/ppermute | solution.py:102
  309.1 5.7 %collective-permute-done.41 = bf16[96,1536]{1,0:T(8,128)(2,1)S(1)} collective-permute-done((bf16[96,1536]{1,0:T(8,128)(2,1)S(1)}, bf16[96,1536]{1,0:T(8,128)(2,1)S(1)}, u32[]{:S(2)}, u32[]{:S(2)}) %collective-permute-start.41) | collective-permute-done | bytes 294944 | tf_op jit(solution)/shard_map/ppermute | solution.py:102
  317.1 1.5 collective-permute-start.42
  319.2 4.7 collective-permute-done.42
  331.6 1.8 collective-permute-done.43
  336.0 3.3 collective-permute-start.51
  341.0 3.3 collective-permute-done.31
  346.7 2.4 collective-permute-done.32
  349.2 2.6 collective-permute-start.33
  351.7 1.9 collective-permute-done.33
  358.1 41.2 %series.2 = f32[192,3072]{1,0:T(8,128)S(1)} custom-call(f32[2]{0:T(128)S(1)} %pad_maximum_fusion.5.scalar_ref, f32[192,3072]{1,0:T(8,128)S(1)} %maximum_convert_fusion.start_ref, bf16[3072,3072]{1,0:T(8,128)(2,1)} %all-gather.2.cloned.1.call-done.cov_ref), custom_call_target="tpu_custom_call" | custom-call | flops 25367150592 | bytes 23592960 | tf_op jit(solution)/shard_map/series/pallas_call | solution.py:43
  400.2 39.8 %all_to_all.19 = bf16[192,16,192]{0,2,1:T(8,128)(2,1)S(1)} all-to-all(bf16[192,16,192]{0,2,1:T(8,128)(2,1)S(1)} %bitcast.25), channel_id=1, replica_groups=mesh['dp'=16,'grp'=2] {'dp'}, dimensions={1} | all-to-all | bytes 2359296 | tf_op jit(solution)/shard_map/all_to_all | solution.py:160
  440.9 1.7 all_to_all.17
  443.9 29.2 %collective-permute-done.52 = bf16[3072,192]{0,1:T(8,128)(2,1)S(1)} collective-permute-done((bf16[3072,192]{0,1:T(8,128)(2,1)S(1)}, bf16[3072,192]{0,1:T(8,128)(2,1)S(1)}, u32[]{:S(2)}, u32[]{:S(2)}) %collective-permute-start.52) | collective-permute-done | bytes 1179680 | tf_op jit(solution)/shard_map/ppermute | solution.py:161
  473.1 5.7 %reshape.24 = f32[8,2,2,96,192]{3,2,1,0,4:T(2,128)} reshape(bf16[3072,192]{0,1:T(8,128)(2,1)S(1)} %collective-permute-done.52) | data formatting | bytes 3538944 | tf_op jit(solution)/shard_map/convert_element_type | solution.py:163
  478.8 3.9 copy.19
  482.7 4.5 reshape.23
  487.2 1.7 copy-done
  488.9 41.2 %series.3 = f32[192,3072]{1,0:T(8,128)S(1)} custom-call(f32[2]{0:T(128)S(1)} %pad_maximum_fusion.5.scalar_ref, f32[192,3072]{1,0:T(8,128)S(1)} %bitcast.21, bf16[3072,3072]{1,0:T(8,128)(2,1)} %all-gather.2.cloned.1.call-done.cov_ref), custom_call_target="tpu_custom_call" | custom-call | flops 25367150592 | bytes 23592960 | tf_op jit(solution)/shard_map/series/pallas_call | solution.py:43
  535.4 2.6 collective-permute-start.55
  539.7 3.2 collective-permute-start.56
  543.9 3.1 collective-permute-start.57
  549.0 2.6 collective-permute-start.58
  (138 shorter events, 92.1 us)
Async XLA Ops:
  6.5 351.6 %all-gather.2.cloned.1.call-start = ((), (), s32[]{:S(2)}) async-start(), calls=%async_computation.1 | async-start | bytes 20054016 | tf_op jit(solution)/shard_map/all_gather | solution.py:149
  10.2 37.4 %collective-permute-start = (bf16[512,1536]{0,1:T(8,128)(2,1)S(1)}, bf16[512,1536]{0,1:T(8,128)(2,1)S(1)}, u32[]{:S(2)}, u32[]{:S(2)}) collective-permute-start(bf16[512,1536]{0,1:T(8,128)(2,1)S(1)} %broadcast_select_fusion), channel_id=1, source_target_pairs={{0,1},{1,0},{2,3},{3,2},{4,5},{5,4},{6,7},{7,6},{8,9},{9,8},{10,11... | collective-permute-start | bytes 4718600 | tf_op jit(solution)/shard_map/ppermute | solution.py:114
  49.7 5.9 %collective-permute-start.1 = (bf16[512,3072]{0,1:T(8,128)(2,1)}, bf16[512,3072]{0,1:T(8,128)(2,1)S(1)}, u32[]{:S(2)}, u32[]{:S(2)}) collective-permute-start(bf16[512,3072]{0,1:T(8,128)(2,1)} %maximum_select_fusion.4), channel_id=1, source_target_pairs={{0,2},{2,0},{4,6},{6,4},{8,10},{10,8},{12,14},{14,12},{16,18},{18,... | collective-permute-start | bytes 9437192 | tf_op jit(solution)/shard_map/ppermute | solution.py:75
  75.9 9.9 %collective-permute-start.2 = (bf16[192,768]{1,0:T(8,128)(2,1)S(1)}, bf16[192,768]{1,0:T(8,128)(2,1)S(1)}, u32[]{:S(2)}, u32[]{:S(2)}) collective-permute-start(bf16[192,768]{1,0:T(8,128)(2,1)S(1)} %get-tuple-element.39), channel_id=1, source_target_pairs={{0,8},{2,10},{8,16},{10,18},{16,24},{18,26},{24,28},{26,30},{28,20... | collective-permute-start | bytes 884744 | tf_op jit(solution)/shard_map/ppermute | solution.py:102
  77.8 9.9 %collective-permute-start.23 = (bf16[192,768]{1,0:T(8,128)(2,1)S(1)}, bf16[192,768]{1,0:T(8,128)(2,1)S(1)}, u32[]{:S(2)}, u32[]{:S(2)}) collective-permute-start(bf16[192,768]{1,0:T(8,128)(2,1)S(1)} %get-tuple-element.40), channel_id=1, source_target_pairs={{0,4},{2,6},{8,0},{10,2},{16,8},{18,10},{24,16},{26,18},{28,24},{3... | collective-permute-start | bytes 884744 | tf_op jit(solution)/shard_map/ppermute | solution.py:102
  78.0 13.4 %collective-permute-start.16 = (bf16[192,768]{1,0:T(8,128)(2,1)S(1)}, bf16[192,768]{1,0:T(8,128)(2,1)S(1)}, u32[]{:S(2)}, u32[]{:S(2)}) collective-permute-start(bf16[192,768]{1,0:T(8,128)(2,1)S(1)} %get-tuple-element.41), channel_id=1, source_target_pairs={{0,8},{2,10},{8,16},{10,18},{16,24},{18,26},{24,28},{26,30},{28,20... | collective-permute-start | bytes 884744 | tf_op jit(solution)/shard_map/ppermute | solution.py:102
  79.8 13.1 %collective-permute-start.9 = (bf16[192,768]{1,0:T(8,128)(2,1)S(1)}, bf16[192,768]{1,0:T(8,128)(2,1)S(1)}, u32[]{:S(2)}, u32[]{:S(2)}) collective-permute-start(bf16[192,768]{1,0:T(8,128)(2,1)S(1)} %get-tuple-element.42), channel_id=1, source_target_pairs={{0,4},{2,6},{8,0},{10,2},{16,8},{18,10},{24,16},{26,18},{28,24},{3... | collective-permute-start | bytes 884744 | tf_op jit(solution)/shard_map/ppermute | solution.py:102
  94.4 10.0 %collective-permute-start.3 = (bf16[192,768]{1,0:T(8,128)(2,1)S(1)}, bf16[192,768]{1,0:T(8,128)(2,1)S(1)}, u32[]{:S(2)}, u32[]{:S(2)}) collective-permute-start(bf16[192,768]{1,0:T(8,128)(2,1)S(1)} %get-tuple-element.35), channel_id=1, source_target_pairs={{0,8},{2,10},{8,16},{10,18},{16,24},{18,26},{24,28},{26,30},{28,20... | collective-permute-start | bytes 884744 | tf_op jit(solution)/shard_map/ppermute | solution.py:102
  96.0 9.9 %collective-permute-start.24 = (bf16[192,768]{1,0:T(8,128)(2,1)S(1)}, bf16[192,768]{1,0:T(8,128)(2,1)S(1)}, u32[]{:S(2)}, u32[]{:S(2)}) collective-permute-start(bf16[192,768]{1,0:T(8,128)(2,1)S(1)} %get-tuple-element.36), channel_id=1, source_target_pairs={{0,4},{2,6},{8,0},{10,2},{16,8},{18,10},{24,16},{26,18},{28,24},{3... | collective-permute-start | bytes 884744 | tf_op jit(solution)/shard_map/ppermute | solution.py:102
  96.4 12.2 %collective-permute-start.17 = (bf16[192,768]{1,0:T(8,128)(2,1)S(1)}, bf16[192,768]{1,0:T(8,128)(2,1)S(1)}, u32[]{:S(2)}, u32[]{:S(2)}) collective-permute-start(bf16[192,768]{1,0:T(8,128)(2,1)S(1)} %get-tuple-element.37), channel_id=1, source_target_pairs={{0,8},{2,10},{8,16},{10,18},{16,24},{18,26},{24,28},{26,30},{28,20... | collective-permute-start | bytes 884744 | tf_op jit(solution)/shard_map/ppermute | solution.py:102
  98.0 11.9 %collective-permute-start.10 = (bf16[192,768]{1,0:T(8,128)(2,1)S(1)}, bf16[192,768]{1,0:T(8,128)(2,1)S(1)}, u32[]{:S(2)}, u32[]{:S(2)}) collective-permute-start(bf16[192,768]{1,0:T(8,128)(2,1)S(1)} %get-tuple-element.38), channel_id=1, source_target_pairs={{0,4},{2,6},{8,0},{10,2},{16,8},{18,10},{24,16},{26,18},{28,24},{3... | collective-permute-start | bytes 884744 | tf_op jit(solution)/shard_map/ppermute | solution.py:102
  111.4 9.9 %collective-permute-start.4 = (bf16[192,768]{1,0:T(8,128)(2,1)S(1)}, bf16[192,768]{1,0:T(8,128)(2,1)S(1)}, u32[]{:S(2)}, u32[]{:S(2)}) collective-permute-start(bf16[192,768]{1,0:T(8,128)(2,1)S(1)} %get-tuple-element.31), channel_id=1, source_target_pairs={{0,8},{2,10},{8,16},{10,18},{16,24},{18,26},{24,28},{26,30},{28,20... | collective-permute-start | bytes 884744 | tf_op jit(solution)/shard_map/ppermute | solution.py:102
  113.1 9.6 %collective-permute-start.25 = (bf16[192,768]{1,0:T(8,128)(2,1)S(1)}, bf16[192,768]{1,0:T(8,128)(2,1)S(1)}, u32[]{:S(2)}, u32[]{:S(2)}) collective-permute-start(bf16[192,768]{1,0:T(8,128)(2,1)S(1)} %get-tuple-element.32), channel_id=1, source_target_pairs={{0,4},{2,6},{8,0},{10,2},{16,8},{18,10},{24,16},{26,18},{28,24},{3... | collective-permute-start | bytes 884744 | tf_op jit(solution)/shard_map/ppermute | solution.py:102
  113.5 11.0 %collective-permute-start.18 = (bf16[192,768]{1,0:T(8,128)(2,1)S(1)}, bf16[192,768]{1,0:T(8,128)(2,1)S(1)}, u32[]{:S(2)}, u32[]{:S(2)}) collective-permute-start(bf16[192,768]{1,0:T(8,128)(2,1)S(1)} %get-tuple-element.33), channel_id=1, source_target_pairs={{0,8},{2,10},{8,16},{10,18},{16,24},{18,26},{24,28},{26,30},{28,20... | collective-permute-start | bytes 884744 | tf_op jit(solution)/shard_map/ppermute | solution.py:102
  115.1 10.7 %collective-permute-start.11 = (bf16[192,768]{1,0:T(8,128)(2,1)S(1)}, bf16[192,768]{1,0:T(8,128)(2,1)S(1)}, u32[]{:S(2)}, u32[]{:S(2)}) collective-permute-start(bf16[192,768]{1,0:T(8,128)(2,1)S(1)} %get-tuple-element.34), channel_id=1, source_target_pairs={{0,4},{2,6},{8,0},{10,2},{16,8},{18,10},{24,16},{26,18},{28,24},{3... | collective-permute-start | bytes 884744 | tf_op jit(solution)/shard_map/ppermute | solution.py:102
  127.3 8.7 %collective-permute-start.5 = (bf16[192,768]{1,0:T(8,128)(2,1)S(1)}, bf16[192,768]{1,0:T(8,128)(2,1)S(1)}, u32[]{:S(2)}, u32[]{:S(2)}) collective-permute-start(bf16[192,768]{1,0:T(8,128)(2,1)S(1)} %get-tuple-element.27), channel_id=1, source_target_pairs={{0,8},{2,10},{8,16},{10,18},{16,24},{18,26},{24,28},{26,30},{28,20... | collective-permute-start | bytes 884744 | tf_op jit(solution)/shard_map/ppermute | solution.py:102
  128.9 8.4 %collective-permute-start.26 = (bf16[192,768]{1,0:T(8,128)(2,1)S(1)}, bf16[192,768]{1,0:T(8,128)(2,1)S(1)}, u32[]{:S(2)}, u32[]{:S(2)}) collective-permute-start(bf16[192,768]{1,0:T(8,128)(2,1)S(1)} %get-tuple-element.28), channel_id=1, source_target_pairs={{0,4},{2,6},{8,0},{10,2},{16,8},{18,10},{24,16},{26,18},{28,24},{3... | collective-permute-start | bytes 884744 | tf_op jit(solution)/shard_map/ppermute | solution.py:102
  129.4 9.8 %collective-permute-start.19 = (bf16[192,768]{1,0:T(8,128)(2,1)S(1)}, bf16[192,768]{1,0:T(8,128)(2,1)S(1)}, u32[]{:S(2)}, u32[]{:S(2)}) collective-permute-start(bf16[192,768]{1,0:T(8,128)(2,1)S(1)} %get-tuple-element.29), channel_id=1, source_target_pairs={{0,8},{2,10},{8,16},{10,18},{16,24},{18,26},{24,28},{26,30},{28,20... | collective-permute-start | bytes 884744 | tf_op jit(solution)/shard_map/ppermute | solution.py:102
  130.9 9.5 %collective-permute-start.12 = (bf16[192,768]{1,0:T(8,128)(2,1)S(1)}, bf16[192,768]{1,0:T(8,128)(2,1)S(1)}, u32[]{:S(2)}, u32[]{:S(2)}) collective-permute-start(bf16[192,768]{1,0:T(8,128)(2,1)S(1)} %get-tuple-element.30), channel_id=1, source_target_pairs={{0,4},{2,6},{8,0},{10,2},{16,8},{18,10},{24,16},{26,18},{28,24},{3... | collective-permute-start | bytes 884744 | tf_op jit(solution)/shard_map/ppermute | solution.py:102
  141.9 7.5 %collective-permute-start.6 = (bf16[192,768]{1,0:T(8,128)(2,1)S(1)}, bf16[192,768]{1,0:T(8,128)(2,1)S(1)}, u32[]{:S(2)}, u32[]{:S(2)}) collective-permute-start(bf16[192,768]{1,0:T(8,128)(2,1)S(1)} %get-tuple-element.23), channel_id=1, source_target_pairs={{0,8},{2,10},{8,16},{10,18},{16,24},{18,26},{24,28},{26,30},{28,20... | collective-permute-start | bytes 884744 | tf_op jit(solution)/shard_map/ppermute | solution.py:102
  142.9 7.3 %collective-permute-start.27 = (bf16[192,768]{1,0:T(8,128)(2,1)S(1)}, bf16[192,768]{1,0:T(8,128)(2,1)S(1)}, u32[]{:S(2)}, u32[]{:S(2)}) collective-permute-start(bf16[192,768]{1,0:T(8,128)(2,1)S(1)} %get-tuple-element.24), channel_id=1, source_target_pairs={{0,4},{2,6},{8,0},{10,2},{16,8},{18,10},{24,16},{26,18},{28,24},{3... | collective-permute-start | bytes 884744 | tf_op jit(solution)/shard_map/ppermute | solution.py:102
  144.0 9.2 %collective-permute-start.20 = (bf16[192,768]{1,0:T(8,128)(2,1)S(1)}, bf16[192,768]{1,0:T(8,128)(2,1)S(1)}, u32[]{:S(2)}, u32[]{:S(2)}) collective-permute-start(bf16[192,768]{1,0:T(8,128)(2,1)S(1)} %get-tuple-element.25), channel_id=1, source_target_pairs={{0,8},{2,10},{8,16},{10,18},{16,24},{18,26},{24,28},{26,30},{28,20... | collective-permute-start | bytes 884744 | tf_op jit(solution)/shard_map/ppermute | solution.py:102
  144.9 9.3 %collective-permute-start.13 = (bf16[192,768]{1,0:T(8,128)(2,1)S(1)}, bf16[192,768]{1,0:T(8,128)(2,1)S(1)}, u32[]{:S(2)}, u32[]{:S(2)}) collective-permute-start(bf16[192,768]{1,0:T(8,128)(2,1)S(1)} %get-tuple-element.26), channel_id=1, source_target_pairs={{0,4},{2,6},{8,0},{10,2},{16,8},{18,10},{24,16},{26,18},{28,24},{3... | collective-permute-start | bytes 884744 | tf_op jit(solution)/shard_map/ppermute | solution.py:102
  155.7 6.8 %collective-permute-start.7 = (bf16[192,768]{1,0:T(8,128)(2,1)S(1)}, bf16[192,768]{1,0:T(8,128)(2,1)S(1)}, u32[]{:S(2)}, u32[]{:S(2)}) collective-permute-start(bf16[192,768]{1,0:T(8,128)(2,1)S(1)} %get-tuple-element.19), channel_id=1, source_target_pairs={{0,8},{2,10},{8,16},{10,18},{16,24},{18,26},{24,28},{26,30},{28,20... | collective-permute-start | bytes 884744 | tf_op jit(solution)/shard_map/ppermute | solution.py:102
  156.5 6.7 %collective-permute-start.28 = (bf16[192,768]{1,0:T(8,128)(2,1)S(1)}, bf16[192,768]{1,0:T(8,128)(2,1)S(1)}, u32[]{:S(2)}, u32[]{:S(2)}) collective-permute-start(bf16[192,768]{1,0:T(8,128)(2,1)S(1)} %get-tuple-element.20), channel_id=1, source_target_pairs={{0,4},{2,6},{8,0},{10,2},{16,8},{18,10},{24,16},{26,18},{28,24},{3... | collective-permute-start | bytes 884744 | tf_op jit(solution)/shard_map/ppermute | solution.py:102
  157.8 9.4 %collective-permute-start.21 = (bf16[192,768]{1,0:T(8,128)(2,1)S(1)}, bf16[192,768]{1,0:T(8,128)(2,1)S(1)}, u32[]{:S(2)}, u32[]{:S(2)}) collective-permute-start(bf16[192,768]{1,0:T(8,128)(2,1)S(1)} %get-tuple-element.21), channel_id=1, source_target_pairs={{0,8},{2,10},{8,16},{10,18},{16,24},{18,26},{24,28},{26,30},{28,20... | collective-permute-start | bytes 884744 | tf_op jit(solution)/shard_map/ppermute | solution.py:102
  158.6 9.7 %collective-permute-start.14 = (bf16[192,768]{1,0:T(8,128)(2,1)S(1)}, bf16[192,768]{1,0:T(8,128)(2,1)S(1)}, u32[]{:S(2)}, u32[]{:S(2)}) collective-permute-start(bf16[192,768]{1,0:T(8,128)(2,1)S(1)} %get-tuple-element.22), channel_id=1, source_target_pairs={{0,4},{2,6},{8,0},{10,2},{16,8},{18,10},{24,16},{26,18},{28,24},{3... | collective-permute-start | bytes 884744 | tf_op jit(solution)/shard_map/ppermute | solution.py:102
  169.8 6.8 %collective-permute-start.8 = (bf16[192,768]{1,0:T(8,128)(2,1)S(1)}, bf16[192,768]{1,0:T(8,128)(2,1)S(1)}, u32[]{:S(2)}, u32[]{:S(2)}) collective-permute-start(bf16[192,768]{1,0:T(8,128)(2,1)S(1)} %get-tuple-element.15), channel_id=1, source_target_pairs={{0,8},{2,10},{8,16},{10,18},{16,24},{18,26},{24,28},{26,30},{28,20... | collective-permute-start | bytes 884744 | tf_op jit(solution)/shard_map/ppermute | solution.py:102
  170.5 6.7 %collective-permute-start.29 = (bf16[192,768]{1,0:T(8,128)(2,1)S(1)}, bf16[192,768]{1,0:T(8,128)(2,1)S(1)}, u32[]{:S(2)}, u32[]{:S(2)}) collective-permute-start(bf16[192,768]{1,0:T(8,128)(2,1)S(1)} %get-tuple-element.16), channel_id=1, source_target_pairs={{0,4},{2,6},{8,0},{10,2},{16,8},{18,10},{24,16},{26,18},{28,24},{3... | collective-permute-start | bytes 884744 | tf_op jit(solution)/shard_map/ppermute | solution.py:102
  171.9 7.9 %collective-permute-start.22 = (bf16[192,768]{1,0:T(8,128)(2,1)S(1)}, bf16[192,768]{1,0:T(8,128)(2,1)S(1)}, u32[]{:S(2)}, u32[]{:S(2)}) collective-permute-start(bf16[192,768]{1,0:T(8,128)(2,1)S(1)} %get-tuple-element.17), channel_id=1, source_target_pairs={{0,8},{2,10},{8,16},{10,18},{16,24},{18,26},{24,28},{26,30},{28,20... | collective-permute-start | bytes 884744 | tf_op jit(solution)/shard_map/ppermute | solution.py:102
  172.5 7.9 %collective-permute-start.15 = (bf16[192,768]{1,0:T(8,128)(2,1)S(1)}, bf16[192,768]{1,0:T(8,128)(2,1)S(1)}, u32[]{:S(2)}, u32[]{:S(2)}) collective-permute-start(bf16[192,768]{1,0:T(8,128)(2,1)S(1)} %get-tuple-element.18), channel_id=1, source_target_pairs={{0,4},{2,6},{8,0},{10,2},{16,8},{18,10},{24,16},{26,18},{28,24},{3... | collective-permute-start | bytes 884744 | tf_op jit(solution)/shard_map/ppermute | solution.py:102
  185.3 30.5 %collective-permute-start.35 = (bf16[512,1536]{0,1:T(8,128)(2,1)S(1)}, bf16[512,1536]{0,1:T(8,128)(2,1)S(1)}, u32[]{:S(2)}, u32[]{:S(2)}) collective-permute-start(bf16[512,1536]{0,1:T(8,128)(2,1)S(1)} %copy.16), channel_id=1, source_target_pairs={{1,0},{3,2},{5,4},{7,6},{9,8},{11,10},{13,12},{15,14},{17,16},{19,... | collective-permute-start | bytes 4718600 | tf_op jit(solution)/shard_map/ppermute | solution.py:135
  218.0 8.7 %collective-permute-start.36 = (bf16[512,3072]{0,1:T(8,128)(2,1)}, bf16[512,3072]{0,1:T(8,128)(2,1)}, u32[]{:S(2)}, u32[]{:S(2)}) collective-permute-start(bf16[512,3072]{0,1:T(8,128)(2,1)} %pad_maximum_fusion.1), channel_id=1, source_target_pairs={{0,2},{2,0},{4,6},{6,4},{8,10},{10,8},{12,14},{14,12},{16,18},{18,... | collective-permute-start | bytes 9437192 | tf_op jit(solution)/shard_map/ppermute | solution.py:75
  218.0 6.3 %collective-permute-start.34 = (bf16[512,1536]{1,0:T(8,128)(2,1)S(1)}, bf16[512,1536]{1,0:T(8,128)(2,1)}, u32[]{:S(2)}, u32[]{:S(2)}) collective-permute-start(bf16[512,1536]{1,0:T(8,128)(2,1)S(1)} %copy-done.13), channel_id=1, source_target_pairs={{0,2},{2,0},{4,6},{6,4},{8,10},{10,8},{12,14},{14,12},{16,18},{18,... | collective-permute-start | bytes 4718600 | tf_op jit(solution)/shard_map/ppermute | solution.py:75
  241.6 16.0 %collective-permute-start.37 = (bf16[96,1536]{1,0:T(8,128)(2,1)S(1)}, bf16[96,1536]{1,0:T(8,128)(2,1)S(1)}, u32[]{:S(2)}, u32[]{:S(2)}) collective-permute-start(bf16[96,1536]{1,0:T(8,128)(2,1)S(1)} %get-tuple-element.57), channel_id=1, source_target_pairs={{0,8},{2,10},{8,16},{10,18},{16,24},{18,26},{24,28},{26,30},{28,20... | collective-permute-start | bytes 884744 | tf_op jit(solution)/shard_map/ppermute | solution.py:102
  242.6 15.8 %collective-permute-start.44 = (bf16[96,1536]{1,0:T(8,128)(2,1)S(1)}, bf16[96,1536]{1,0:T(8,128)(2,1)S(1)}, u32[]{:S(2)}, u32[]{:S(2)}) collective-permute-start(bf16[96,1536]{1,0:T(8,128)(2,1)S(1)} %get-tuple-element.58), channel_id=1, source_target_pairs={{0,4},{2,6},{8,0},{10,2},{16,8},{18,10},{24,16},{26,18},{28,24},{3... | collective-permute-start | bytes 884744 | tf_op jit(solution)/shard_map/ppermute | solution.py:102
  259.6 15.6 %collective-permute-start.38 = (bf16[96,1536]{1,0:T(8,128)(2,1)S(1)}, bf16[96,1536]{1,0:T(8,128)(2,1)S(1)}, u32[]{:S(2)}, u32[]{:S(2)}) collective-permute-start(bf16[96,1536]{1,0:T(8,128)(2,1)S(1)} %get-tuple-element.55), channel_id=1, source_target_pairs={{0,8},{2,10},{8,16},{10,18},{16,24},{18,26},{24,28},{26,30},{28,20... | collective-permute-start | bytes 884744 | tf_op jit(solution)/shard_map/ppermute | solution.py:102
  260.2 15.4 %collective-permute-start.45 = (bf16[96,1536]{1,0:T(8,128)(2,1)S(1)}, bf16[96,1536]{1,0:T(8,128)(2,1)S(1)}, u32[]{:S(2)}, u32[]{:S(2)}) collective-permute-start(bf16[96,1536]{1,0:T(8,128)(2,1)S(1)} %get-tuple-element.56), channel_id=1, source_target_pairs={{0,4},{2,6},{8,0},{10,2},{16,8},{18,10},{24,16},{26,18},{28,24},{3... | collective-permute-start | bytes 884744 | tf_op jit(solution)/shard_map/ppermute | solution.py:102
  276.8 15.3 %collective-permute-start.39 = (bf16[96,1536]{1,0:T(8,128)(2,1)S(1)}, bf16[96,1536]{1,0:T(8,128)(2,1)S(1)}, u32[]{:S(2)}, u32[]{:S(2)}) collective-permute-start(bf16[96,1536]{1,0:T(8,128)(2,1)S(1)} %get-tuple-element.53), channel_id=1, source_target_pairs={{0,8},{2,10},{8,16},{10,18},{16,24},{18,26},{24,28},{26,30},{28,20... | collective-permute-start | bytes 884744 | tf_op jit(solution)/shard_map/ppermute | solution.py:102
  277.4 15.1 %collective-permute-start.46 = (bf16[96,1536]{1,0:T(8,128)(2,1)S(1)}, bf16[96,1536]{1,0:T(8,128)(2,1)S(1)}, u32[]{:S(2)}, u32[]{:S(2)}) collective-permute-start(bf16[96,1536]{1,0:T(8,128)(2,1)S(1)} %get-tuple-element.54), channel_id=1, source_target_pairs={{0,4},{2,6},{8,0},{10,2},{16,8},{18,10},{24,16},{26,18},{28,24},{3... | collective-permute-start | bytes 884744 | tf_op jit(solution)/shard_map/ppermute | solution.py:102
  278.9 49.8 %copy-start.4 = (f32[192,768]{1,0:T(8,128)S(1)}, f32[192,768]{1,0:T(8,128)}, u32[]{:S(2)}) copy-start(f32[192,768]{1,0:T(8,128)} %copy-done.3) | copy-start | bytes 1769476
  278.9 49.8 %copy-start.6 = (f32[192,768]{1,0:T(8,128)S(1)}, f32[192,768]{1,0:T(8,128)}, u32[]{:S(2)}) copy-start(f32[192,768]{1,0:T(8,128)} %copy-done.5) | copy-start | bytes 1769476
  278.9 49.8 %copy-start.8 = (f32[192,768]{1,0:T(8,128)S(1)}, f32[192,768]{1,0:T(8,128)}, u32[]{:S(2)}) copy-start(f32[192,768]{1,0:T(8,128)} %copy-done.7) | copy-start | bytes 1769476
  278.9 49.8 %copy-start.10 = (f32[192,768]{1,0:T(8,128)S(1)}, f32[192,768]{1,0:T(8,128)}, u32[]{:S(2)}) copy-start(f32[192,768]{1,0:T(8,128)} %copy-done.9) | copy-start | bytes 1769476
  293.6 12.2 %collective-permute-start.40 = (bf16[96,1536]{1,0:T(8,128)(2,1)S(1)}, bf16[96,1536]{1,0:T(8,128)(2,1)S(1)}, u32[]{:S(2)}, u32[]{:S(2)}) collective-permute-start(bf16[96,1536]{1,0:T(8,128)(2,1)S(1)} %get-tuple-element.51), channel_id=1, source_target_pairs={{0,8},{2,10},{8,16},{10,18},{16,24},{18,26},{24,28},{26,30},{28,20... | collective-permute-start | bytes 884744 | tf_op jit(solution)/shard_map/ppermute | solution.py:102
  294.7 11.2 %collective-permute-start.47 = (bf16[96,1536]{1,0:T(8,128)(2,1)S(1)}, bf16[96,1536]{1,0:T(8,128)(2,1)S(1)}, u32[]{:S(2)}, u32[]{:S(2)}) collective-permute-start(bf16[96,1536]{1,0:T(8,128)(2,1)S(1)} %get-tuple-element.52), channel_id=1, source_target_pairs={{0,4},{2,6},{8,0},{10,2},{16,8},{18,10},{24,16},{26,18},{28,24},{3... | collective-permute-start | bytes 884744 | tf_op jit(solution)/shard_map/ppermute | solution.py:102
  307.0 7.8 %collective-permute-start.41 = (bf16[96,1536]{1,0:T(8,128)(2,1)S(1)}, bf16[96,1536]{1,0:T(8,128)(2,1)S(1)}, u32[]{:S(2)}, u32[]{:S(2)}) collective-permute-start(bf16[96,1536]{1,0:T(8,128)(2,1)S(1)} %get-tuple-element.49), channel_id=1, source_target_pairs={{0,8},{2,10},{8,16},{10,18},{16,24},{18,26},{24,28},{26,30},{28,20... | collective-permute-start | bytes 884744 | tf_op jit(solution)/shard_map/ppermute | solution.py:102
  308.6 7.4 %collective-permute-start.48 = (bf16[96,1536]{1,0:T(8,128)(2,1)S(1)}, bf16[96,1536]{1,0:T(8,128)(2,1)S(1)}, u32[]{:S(2)}, u32[]{:S(2)}) collective-permute-start(bf16[96,1536]{1,0:T(8,128)(2,1)S(1)} %get-tuple-element.50), channel_id=1, source_target_pairs={{0,4},{2,6},{8,0},{10,2},{16,8},{18,10},{24,16},{26,18},{28,24},{3... | collective-permute-start | bytes 884744 | tf_op jit(solution)/shard_map/ppermute | solution.py:102
  317.1 6.8 %collective-permute-start.42 = (bf16[96,1536]{1,0:T(8,128)(2,1)S(1)}, bf16[96,1536]{1,0:T(8,128)(2,1)S(1)}, u32[]{:S(2)}, u32[]{:S(2)}) collective-permute-start(bf16[96,1536]{1,0:T(8,128)(2,1)S(1)} %get-tuple-element.47), channel_id=1, source_target_pairs={{0,8},{2,10},{8,16},{10,18},{16,24},{18,26},{24,28},{26,30},{28,20... | collective-permute-start | bytes 884744 | tf_op jit(solution)/shard_map/ppermute | solution.py:102
  318.7 6.7 %collective-permute-start.49 = (bf16[96,1536]{1,0:T(8,128)(2,1)S(1)}, bf16[96,1536]{1,0:T(8,128)(2,1)S(1)}, u32[]{:S(2)}, u32[]{:S(2)}) collective-permute-start(bf16[96,1536]{1,0:T(8,128)(2,1)S(1)} %get-tuple-element.48), channel_id=1, source_target_pairs={{0,4},{2,6},{8,0},{10,2},{16,8},{18,10},{24,16},{26,18},{28,24},{3... | collective-permute-start | bytes 884744 | tf_op jit(solution)/shard_map/ppermute | solution.py:102
  326.6 6.8 %collective-permute-start.43 = (bf16[96,1536]{1,0:T(8,128)(2,1)S(1)}, bf16[96,1536]{1,0:T(8,128)(2,1)S(1)}, u32[]{:S(2)}, u32[]{:S(2)}) collective-permute-start(bf16[96,1536]{1,0:T(8,128)(2,1)S(1)} %get-tuple-element.45), channel_id=1, source_target_pairs={{0,8},{2,10},{8,16},{10,18},{16,24},{18,26},{24,28},{26,30},{28,20... | collective-permute-start | bytes 884744 | tf_op jit(solution)/shard_map/ppermute | solution.py:102
  328.1 6.7 %collective-permute-start.50 = (bf16[96,1536]{1,0:T(8,128)(2,1)S(1)}, bf16[96,1536]{1,0:T(8,128)(2,1)S(1)}, u32[]{:S(2)}, u32[]{:S(2)}) collective-permute-start(bf16[96,1536]{1,0:T(8,128)(2,1)S(1)} %get-tuple-element.46), channel_id=1, source_target_pairs={{0,4},{2,6},{8,0},{10,2},{16,8},{18,10},{24,16},{26,18},{28,24},{3... | collective-permute-start | bytes 884744 | tf_op jit(solution)/shard_map/ppermute | solution.py:102
  331.6 7.8 %collective-permute-start.30 = (f32[2]{0:T(128)S(1)}, f32[2]{0:T(128)S(1)}, u32[]{:S(2)}, u32[]{:S(2)}) collective-permute-start(f32[2]{0:T(128)S(1)} %pad_maximum_fusion.4), channel_id=1, source_target_pairs={{0,2},{2,0},{4,6},{6,4},{8,10},{10,8},{12,14},{14,12},{16,18},{18,... | collective-permute-start | bytes 32 | tf_op jit(solution)/shard_map/ppermute | solution.py:109
  336.0 21.8 %collective-permute-start.51 = (bf16[96,3072]{1,0:T(8,128)(2,1)S(1)}, bf16[96,3072]{1,0:T(8,128)(2,1)S(1)}, u32[]{:S(2)}, u32[]{:S(2)}) collective-permute-start(bf16[96,3072]{1,0:T(8,128)(2,1)S(1)} %pad_maximum_fusion.3), channel_id=1, source_target_pairs={{0,1},{2,3},{4,5},{6,7},{8,9},{10,11},{12,13},{14,15},{16,17},{18,... | collective-permute-start | bytes 1769480 | tf_op jit(solution)/shard_map/ppermute | solution.py:144
  340.7 3.5 collective-permute-start.31
  345.6 3.5 collective-permute-start.32
  349.2 4.4 collective-permute-start.33
  442.6 30.5 %collective-permute-start.52 = (bf16[3072,192]{0,1:T(8,128)(2,1)S(1)}, bf16[3072,192]{0,1:T(8,128)(2,1)S(1)}, u32[]{:S(2)}, u32[]{:S(2)}) collective-permute-start(bf16[3072,192]{0,1:T(8,128)(2,1)S(1)} %all_to_all.17), channel_id=1, source_target_pairs={{1,0},{3,2},{5,4},{7,6},{9,8},{11,10},{13,12},{15,14},{17,16},{19,... | collective-permute-start | bytes 3538952 | tf_op jit(solution)/shard_map/ppermute | solution.py:161
  530.2 22.2 %collective-permute-start.53 = (bf16[192,1536]{1,0:T(8,128)(2,1)S(1)}, bf16[192,1536]{1,0:T(8,128)(2,1)S(1)}, u32[]{:S(2)}, u32[]{:S(2)}) collective-permute-start(bf16[192,1536]{1,0:T(8,128)(2,1)S(1)} %dynamic_slice.274), channel_id=1, source_target_pairs={{0,1},{2,3},{4,5},{6,7},{8,9},{10,11},{12,13},{14,15},{16,17},{18,... | collective-permute-start | bytes 1769480 | tf_op jit(solution)/shard_map/ppermute | solution.py:169
  532.9 1.2 collective-permute-start.54
  535.4 3.6 collective-permute-start.55
  539.7 3.6 collective-permute-start.56
  543.9 4.5 collective-permute-start.57
  549.0 2.6 collective-permute-start.58
  (11 other events, 53.5 us)
Sparse Core Ops, SparseCore 0:
  184.7 121.6 all-gather.1

commit v4 on v3

--- a/solution.py
+++ b/solution.py
@@ -78,7 +78,7 @@
     chip = dp_index // 2
     place = jnp.where(chip % 2 == 0, chip // 2, chips - 1 - chip // 2)
 
-    def ring_reduce(x, lanes):
+    def ring_reduce(x, lanes, beside=()):
         width = x.shape[1] // (2 * lanes)
         count = x.shape[0] // chips
 
@@ -88,6 +88,7 @@
             piece = lax.dynamic_slice(x, (owner * count, lane * width), (count, width))
             return piece.astype(f32)
 
+        made = None
         totals = [None] * (2 * lanes)
         for lane in range(2 * lanes):
             totals[lane] = block(lane, place + (1 if lane % 2 else -1))
@@ -101,7 +102,11 @@
                 ]
                 got = lax.ppermute(totals[lane].astype(bf16), "dp", moves)
                 totals[lane] = got.astype(f32) + block(lane, place - way * (step + 2))
-        return jnp.concatenate(totals, axis=1)
+            for due, make in beside:
+                if due == step:
+                    made = make(made)
+                    totals, made = lax.optimization_barrier((totals, made))
+        return jnp.concatenate(totals, axis=1), made
 
     def sum_dp(x):
         hop = 1
@@ -129,30 +134,46 @@
     cov_part, cotangents = lax.optimization_barrier(
         (dot_rows(my_half, mine).astype(bf16), cotangents)
     )
-    cov_rows = ring_reduce(cov_part, 2)
-
-    if c == 2:
-        rest = lax.ppermute(cotangents, "grp", [(1, 0)])
-        all_grads = jnp.concatenate([cotangents, rest], axis=1)
-    all_grads = jnp.concatenate([all_grads, other_core(all_grads)], axis=0)
-    if c == 2:
-        all_grads = jnp.where(on_g, mine, all_grads)
-    acts = jnp.concatenate([activations, other_core(activations)], axis=0)
-    acts = lax.dynamic_slice_in_dim(acts, core * (cols // 2), cols // 2, 1)
-    grad_rows = ring_reduce(dot_rows(acts, all_grads).astype(bf16), 1).astype(bf16)
+
+    def fetch_grads(unused):
+        if c == 2:
+            return lax.ppermute(cotangents, "grp", [(1, 0)])
+        return all_grads
+
+    def share_grads(fetched):
+        if c == 2:
+            fetched = jnp.concatenate([cotangents, fetched], axis=1)
+        return fetched, other_core(fetched)
+
+    def grad_product(shared):
+        whole = jnp.concatenate(shared, axis=0)
+        if c == 2:
+            whole = jnp.where(on_g, mine, whole)
+        acts = jnp.concatenate([activations, other_core(activations)], axis=0)
+        acts = lax.dynamic_slice_in_dim(acts, core * (cols // 2), cols // 2, 1)
+        return dot_rows(acts, whole).astype(bf16)
+
+    cov_rows, grad_part = ring_reduce(
+        cov_part,
+        2,
+        ((chips // 2 - 1, fetch_grads), (chips - 4, share_grads), (chips - 3, grad_product)),
+    )
+
+    cov = lax.all_gather(cov_rows.astype(bf16), "dp", axis=0, tiled=True)
+
+    def diag_mask(start, count):
+        return start + lax.iota(jnp.int32, count)[:, None] == lax.iota(jnp.int32, D)[None, :]
+
+    trace_part = jnp.sum(jnp.where(diag_mask(dp_index * rows, rows), cov_rows, 0.0))
+    parts = jnp.stack([trace_part, jnp.sum(cov_rows * cov_rows)])
+    grad_rows, sums = ring_reduce(grad_part, 1, ((chips - 3, lambda unused: sum_dp(parts)),))
+    grad_rows = grad_rows.astype(bf16)
     if c == 2:
         first = lax.ppermute(grad_rows, "grp", [(0, 1)])
         grad_rows = jnp.concatenate([first, grad_rows], axis=0)
     else:
         grad_rows = lax.all_gather(grad_rows, "grp", axis=0, tiled=True)
-
-    cov = lax.all_gather(cov_rows.astype(bf16), "dp", axis=0, tiled=True)
-
-    def diag_mask(start, count):
-        return start + lax.iota(jnp.int32, count)[:, None] == lax.iota(jnp.int32, D)[None, :]
-
-    trace_part = jnp.sum(jnp.where(diag_mask(dp_index * rows, rows), cov_rows, 0.0))
-    trace, square = sum_dp(jnp.stack([trace_part, jnp.sum(cov_rows * cov_rows)]))
+    trace, square = sums
     damp = damping * trace / D
     scale = lax.rsqrt(square + 2.0 * damp * trace + D * damp * damp)
 

time: 561 us -> 541 us (0.964)
  waiting for transfers between devices: 254 us -> 232 us
    ppermute x1, waiting for transfers between devices: 29.1 us -> 0.01 us  [fetch_grads(): return lax.ppermute(cotangents, 'grp', [(1, 0)])]
    ppermute x3, waiting for transfers between devices: 14.1 us -> 5.87 us  [other_core(): return lax.ppermute(x, 'dp', pairs)]
    ppermute x8, waiting for transfers between devices: 11.5 us -> 19.1 us  [sum_dp(): x = x + lax.ppermute(x, 'dp', [(i, i ^ hop) for i in range(n)])]
    add x1 -> x5, other arithmetic: 1.47 us -> 8.74 us  [ring_reduce(): totals[lane] = got.astype(f32) + block(lane, place - way * (step + 2))]
    unnamed x32 -> x12, local copies, waits for them, and re-layouts: 12.5 us -> 8.76 us
    convert_element_type x12 -> x8, other arithmetic: 16.2 us -> 13.7 us  [ring_reduce(): got = lax.ppermute(totals[lane].astype(bf16), 'dp', moves)]
  transfers between devices with their start and end apart: 60 -> 60, of which waited for: 54 -> 46; matrix products, arithmetic and copies ran while one was open for 6% -> 7% of each run, Pallas kernels for 0% -> 0%
where the time goes in v4:
time: 541 us; the launch traced here: 540 us
  waiting for transfers between devices  232 us (43%)
  Pallas kernels  82.4 us (15%)
  starting transfers between devices  69.9 us (13%)
  other arithmetic  41.6 us (8%)
  blocking collectives  40.8 us (8%)
  local copies, waits for them, and re-layouts  29.8 us (6%)
  matrix products  21.9 us (4%)
  between operations  21.8 us (4%)
    ppermute x42, waiting for transfers between devices, ring_reduce(): got = lax.ppermute(totals[lane].astype(bf16), 'dp', moves)  140 us
    pallas_call x2, Pallas kernels, series(): pl.pallas_call(kernel, out_shape=jax.ShapeDtypeStruct((rows, D), f32), in...  82.4 us
    ppermute x42, starting transfers between devices, ring_reduce(): got = lax.ppermute(totals[lane].astype(bf16), 'dp', moves)  44.5 us
    all_to_all x1, blocking collectives, shards(): left = lax.all_to_all(left, 'dp', split_axis=1, concat_axis=0, tiled=True)  40.8 us
    ppermute x1, waiting for transfers between devices, shards(): lax.ppermute(jnp.where(on_g, activations, cotangents), 'grp', [(0, 1), (1...  34.4 us
    ppermute x1, waiting for transfers between devices, shards(): left = lax.ppermute(left, 'grp', [(part + j, j) for j in range(part)])  29.1 us
    dot_general x2, matrix products, dot_rows(): lax.dot_general(left, right, (((0,), (0,)), ((), ())), preferred_element_...  21.9 us
    ppermute x8, waiting for transfers between devices, sum_dp(): x = x + lax.ppermute(x, 'dp', [(i, i ^ hop) for i in range(n)])  19.1 us
  transfers between devices with their start and end apart: 60, of which 46 were waited for; matrix products, arithmetic and copies ran while one was open for 7% of the time, Pallas kernels for 0%

profile of v4, /device:TPU:0, one launch (start us, length us, event | category | flops | bytes accessed | tf_op | source)
XLA Modules:
  0.0 540.4 jit_solution(12125654117379260382)
XLA Ops:
  6.5 1.7 copy.12
  8.3 1.7 copy.11
  10.2 3.0 collective-permute-start
  13.2 34.4 %collective-permute-done = bf16[512,1536]{0,1:T(8,128)(2,1)S(1)} collective-permute-done((bf16[512,1536]{0,1:T(8,128)(2,1)S(1)}, bf16[512,1536]{0,1:T(8,128)(2,1)S(1)}, u32[]{:S(2)}, u32[]{:S(2)}) %collective-permute-start) | collective-permute-done | bytes 1572896 | tf_op jit(solution)/shard_map/ppermute | solution.py:119
  47.6 2.2 maximum_select_fusion.4
  49.8 5.9 %collective-permute-done.1 = bf16[512,3072]{0,1:T(8,128)(2,1)S(1)} collective-permute-done((bf16[512,3072]{0,1:T(8,128)(2,1)}, bf16[512,3072]{0,1:T(8,128)(2,1)S(1)}, u32[]{:S(2)}, u32[]{:S(2)}) %collective-permute-start.1) | collective-permute-done | bytes 3145760 | tf_op jit(solution)/shard_map/ppermute | solution.py:75
  55.7 4.0 pad_maximum_fusion
  60.0 12.1 %convolution_convert_fusion = bf16[1536,3072]{1,0:T(8,128)(2,1)S(1)} fusion(bf16[1024,1536]{0,1:T(8,128)(2,1)S(1)} %bitcast.26, bf16[512,3072]{0,1:T(8,128)(2,1)} %copy-done.3, bf16[512,3072]{0,1:T(8,128)(2,1)} %maximum_select_fusion.4), kind=kOutput, calls=%fused_computation | convolution fusion | flops 9680977920 | bytes 18874368 | tf_op jit(solution)/shard_map/dot_general | solution.py:18
  72.2 3.7 copy-done.1
  76.6 1.8 collective-permute-start.14
  78.7 1.8 collective-permute-start.6
  80.7 6.0 %collective-permute-done.14 = bf16[192,768]{1,0:T(8,128)(2,1)S(1)} collective-permute-done((bf16[192,768]{1,0:T(8,128)(2,1)}, bf16[192,768]{1,0:T(8,128)(2,1)S(1)}, u32[]{:S(2)}, u32[]{:S(2)}) %collective-permute-start.14) | collective-permute-done | bytes 294944 | tf_op jit(solution)/shard_map/ppermute | solution.py:103
  88.3 4.0 collective-permute-done.6
  93.6 2.4 add_convert_fusion.14
  102.1 4.1 collective-permute-done.15
  107.8 2.7 collective-permute-done.7
  111.8 2.7 add_convert_fusion.13
  118.6 6.1 %collective-permute-done.16 = bf16[192,768]{1,0:T(8,128)(2,1)} collective-permute-done((bf16[192,768]{1,0:T(8,128)(2,1)}, bf16[192,768]{1,0:T(8,128)(2,1)}, u32[]{:S(2)}, u32[]{:S(2)}) %collective-permute-start.16) | collective-permute-done | bytes 294944 | tf_op jit(solution)/shard_map/ppermute | solution.py:103
  126.0 1.9 collective-permute-done.8
  129.1 2.7 add_convert_fusion.12
  135.9 4.9 collective-permute-done.17
  142.1 1.9 collective-permute-done.9
  145.2 2.7 convert_add_fusion.14
  147.9 1.8 pad_maximum_fusion.1
  153.7 6.5 %collective-permute-done.22 = bf16[192,768]{1,0:T(8,128)(2,1)} collective-permute-done((bf16[192,768]{1,0:T(8,128)(2,1)S(1)}, bf16[192,768]{1,0:T(8,128)(2,1)}, u32[]{:S(2)}, u32[]{:S(2)}) %collective-permute-start.22) | collective-permute-done | bytes 294944 | tf_op jit(solution)/shard_map/ppermute | solution.py:103
  160.7 4.9 collective-permute-done.20
  165.6 1.8 collective-permute-done.19
  167.4 1.9 convert_add_fusion.10
  169.3 1.7 collective-permute-start.27
  173.6 9.7 %fusion.4 = bf16[768,3072]{1,0:T(8,128)(2,1)} fusion(bf16[512,3072]{0,1:T(8,128)(2,1)} %collective-permute-done.23, bf16[512,3072]{0,1:T(8,128)(2,1)} %pad_maximum_fusion.1, pred[]{:T(512)S(6)} %ge.3, s32[]{:T(128)S(6)} %select_n.448, bf16[512,1536]{1,0:T(8,128)(2,1)} %param.2, bf16[512,1536]{1,0:T(8,128)(2,1)} %collective-permute-done.28, ...), kind=kOutput, calls=%fused_computation.7 | convolution fusion | flops 4865654784 | bytes 20447236 | tf_op jit(solution)/shard_map/dot_general | solution.py:18
  189.0 4.2 collective-permute-done.41
  193.4 3.0 collective-permute-done.43
  202.5 7.1 %collective-permute-done.35 = bf16[96,1536]{1,0:T(8,128)(2,1)S(1)} collective-permute-done((bf16[96,1536]{1,0:T(8,128)(2,1)S(1)}, bf16[96,1536]{1,0:T(8,128)(2,1)S(1)}, u32[]{:S(2)}, u32[]{:S(2)}) %collective-permute-start.35) | collective-permute-done | bytes 294944 | tf_op jit(solution)/shard_map/ppermute | solution.py:103
  209.6 3.3 collective-permute-done.29
  214.2 3.2 collective-permute-start.36
  217.4 13.0 %collective-permute-done.36 = bf16[96,1536]{1,0:T(8,128)(2,1)S(1)} collective-permute-done((bf16[96,1536]{1,0:T(8,128)(2,1)S(1)}, bf16[96,1536]{1,0:T(8,128)(2,1)S(1)}, u32[]{:S(2)}, u32[]{:S(2)}) %collective-permute-start.36) | collective-permute-done | bytes 294944 | tf_op jit(solution)/shard_map/ppermute | solution.py:103
  230.4 2.6 collective-permute-done.30
  234.3 2.0 collective-permute-start.31
  236.3 13.8 %collective-permute-done.37 = bf16[96,1536]{1,0:T(8,128)(2,1)S(1)} collective-permute-done((bf16[96,1536]{1,0:T(8,128)(2,1)S(1)}, bf16[96,1536]{1,0:T(8,128)(2,1)S(1)}, u32[]{:S(2)}, u32[]{:S(2)}) %collective-permute-start.37) | collective-permute-done | bytes 294944 | tf_op jit(solution)/shard_map/ppermute | solution.py:103
  251.4 2.1 collective-permute-start.32
  253.6 14.0 %collective-permute-done.38 = bf16[96,1536]{1,0:T(8,128)(2,1)S(1)} collective-permute-done((bf16[96,1536]{1,0:T(8,128)(2,1)S(1)}, bf16[96,1536]{1,0:T(8,128)(2,1)S(1)}, u32[]{:S(2)}, u32[]{:S(2)}) %collective-permute-start.38) | collective-permute-done | bytes 294944 | tf_op jit(solution)/shard_map/ppermute | solution.py:103
  273.9 9.2 %collective-permute-done.39 = bf16[96,1536]{1,0:T(8,128)(2,1)S(1)} collective-permute-done((bf16[96,1536]{1,0:T(8,128)(2,1)S(1)}, bf16[96,1536]{1,0:T(8,128)(2,1)S(1)}, u32[]{:S(2)}, u32[]{:S(2)}) %collective-permute-start.39) | collective-permute-done | bytes 294944 | tf_op jit(solution)/shard_map/ppermute | solution.py:103
  285.2 1.9 collective-permute-start.34
  288.6 9.9 %collective-permute-done.46 = f32[2]{0:T(128)S(1)} collective-permute-done((f32[2]{0:T(128)S(1)}, f32[2]{0:T(128)S(1)}, u32[]{:S(2)}, u32[]{:S(2)}) %collective-permute-start.46) | collective-permute-done | bytes 40 | tf_op jit(solution)/shard_map/ppermute | solution.py:114
  299.8 3.5 collective-permute-done.47
  303.4 2.5 collective-permute-start.48
  305.9 1.9 collective-permute-done.48
  309.0 1.6 collective-permute-start.49
  311.1 11.0 %collective-permute-done.49 = bf16[96,1536]{1,0:T(8,128)(2,1)S(1)} collective-permute-done((bf16[96,1536]{1,0:T(8,128)(2,1)S(1)}, bf16[96,1536]{1,0:T(8,128)(2,1)S(1)}, u32[]{:S(2)}, u32[]{:S(2)}) %collective-permute-start.49) | collective-permute-done | bytes 294944 | tf_op jit(solution)/shard_map/ppermute | solution.py:103
  324.9 3.5 collective-permute-start.51
  333.0 2.8 collective-permute-done.51
  336.9 41.2 %series.2 = f32[192,3072]{1,0:T(8,128)S(1)} custom-call(f32[2]{0:T(128)S(1)} %pad_maximum_fusion.5.scalar_ref, f32[192,3072]{1,0:T(8,128)S(1)} %maximum_convert_fusion.start_ref, bf16[3072,3072]{1,0:T(8,128)(2,1)} %all-gather.2.cloned.1.call-done.cov_ref), custom_call_target="tpu_custom_call" | custom-call | flops 25367150592 | bytes 23592960 | tf_op jit(solution)/shard_map/series/pallas_call | solution.py:43
  378.9 40.8 %all_to_all.19 = bf16[192,16,192]{0,2,1:T(8,128)(2,1)S(1)} all-to-all(bf16[192,16,192]{0,2,1:T(8,128)(2,1)S(1)} %bitcast.25), channel_id=1, replica_groups=mesh['dp'=16,'grp'=2] {'dp'}, dimensions={1} | all-to-all | bytes 2359296 | tf_op jit(solution)/shard_map/all_to_all | solution.py:181
  420.6 1.7 all_to_all.17
  423.8 29.1 %collective-permute-done.52 = bf16[3072,192]{0,1:T(8,128)(2,1)S(1)} collective-permute-done((bf16[3072,192]{0,1:T(8,128)(2,1)S(1)}, bf16[3072,192]{0,1:T(8,128)(2,1)S(1)}, u32[]{:S(2)}, u32[]{:S(2)}) %collective-permute-start.52) | collective-permute-done | bytes 1179680 | tf_op jit(solution)/shard_map/ppermute | solution.py:182
  453.0 5.7 %reshape.24 = f32[8,2,2,96,192]{3,2,1,0,4:T(2,128)} reshape(bf16[3072,192]{0,1:T(8,128)(2,1)S(1)} %collective-permute-done.52) | data formatting | bytes 3538944 | tf_op jit(solution)/shard_map/convert_element_type | solution.py:184
  458.7 3.9 copy.19
  462.6 4.6 reshape.23
  467.2 1.7 copy-done
  468.8 41.2 %series.3 = f32[192,3072]{1,0:T(8,128)S(1)} custom-call(f32[2]{0:T(128)S(1)} %pad_maximum_fusion.5.scalar_ref, f32[192,3072]{1,0:T(8,128)S(1)} %bitcast.21, bf16[3072,3072]{1,0:T(8,128)(2,1)} %all-gather.2.cloned.1.call-done.cov_ref), custom_call_target="tpu_custom_call" | custom-call | flops 25367150592 | bytes 23592960 | tf_op jit(solution)/shard_map/series/pallas_call | solution.py:43
  515.4 2.6 collective-permute-start.55
  519.6 3.2 collective-permute-start.56
  523.9 3.2 collective-permute-start.57
  529.0 2.6 collective-permute-start.58
  (118 shorter events, 78.1 us)
Async XLA Ops:
  6.5 330.3 %all-gather.2.cloned.1.call-start = ((), (), s32[]{:S(2)}) async-start(), calls=%async_computation.1 | async-start | bytes 20054016 | tf_op jit(solution)/shard_map/all_gather | solution.py:162
  10.2 37.4 %collective-permute-start = (bf16[512,1536]{0,1:T(8,128)(2,1)S(1)}, bf16[512,1536]{0,1:T(8,128)(2,1)S(1)}, u32[]{:S(2)}, u32[]{:S(2)}) collective-permute-start(bf16[512,1536]{0,1:T(8,128)(2,1)S(1)} %broadcast_select_fusion), channel_id=1, source_target_pairs={{0,1},{1,0},{2,3},{3,2},{4,5},{5,4},{6,7},{7,6},{8,9},{9,8},{10,11... | collective-permute-start | bytes 4718600 | tf_op jit(solution)/shard_map/ppermute | solution.py:119
  49.8 5.9 %collective-permute-start.1 = (bf16[512,3072]{0,1:T(8,128)(2,1)}, bf16[512,3072]{0,1:T(8,128)(2,1)S(1)}, u32[]{:S(2)}, u32[]{:S(2)}) collective-permute-start(bf16[512,3072]{0,1:T(8,128)(2,1)} %maximum_select_fusion.4), channel_id=1, source_target_pairs={{0,2},{2,0},{4,6},{6,4},{8,10},{10,8},{12,14},{14,12},{16,18},{18,... | collective-permute-start | bytes 9437192 | tf_op jit(solution)/shard_map/ppermute | solution.py:75
  55.7 4.0 copy-start.3
  72.2 3.7 copy-start.1
  75.8 24.2 %copy-start.2 = (bf16[512,1536]{1,0:T(8,128)(2,1)S(1)}, bf16[512,1536]{1,0:T(8,128)(2,1)}, u32[]{:S(2)}) copy-start(bf16[512,1536]{1,0:T(8,128)(2,1)} %param.3) | copy-start | bytes 4718596
  76.6 10.1 %collective-permute-start.14 = (bf16[192,768]{1,0:T(8,128)(2,1)}, bf16[192,768]{1,0:T(8,128)(2,1)S(1)}, u32[]{:S(2)}, u32[]{:S(2)}) collective-permute-start(bf16[192,768]{1,0:T(8,128)(2,1)} %get-tuple-element.77), channel_id=1, source_target_pairs={{0,4},{2,6},{8,0},{10,2},{16,8},{18,10},{24,16},{26,18},{28,24},{3... | collective-permute-start | bytes 884744 | tf_op jit(solution)/shard_map/ppermute | solution.py:103
  78.4 9.9 %collective-permute-start.10 = (bf16[192,768]{1,0:T(8,128)(2,1)S(1)}, bf16[192,768]{1,0:T(8,128)(2,1)S(1)}, u32[]{:S(2)}, u32[]{:S(2)}) collective-permute-start(bf16[192,768]{1,0:T(8,128)(2,1)S(1)} %get-tuple-element.78), channel_id=1, source_target_pairs={{0,8},{2,10},{8,16},{10,18},{16,24},{18,26},{24,28},{26,30},{28,20... | collective-permute-start | bytes 884744 | tf_op jit(solution)/shard_map/ppermute | solution.py:103
  78.7 13.6 %collective-permute-start.6 = (bf16[192,768]{1,0:T(8,128)(2,1)S(1)}, bf16[192,768]{1,0:T(8,128)(2,1)S(1)}, u32[]{:S(2)}, u32[]{:S(2)}) collective-permute-start(bf16[192,768]{1,0:T(8,128)(2,1)S(1)} %get-tuple-element.79), channel_id=1, source_target_pairs={{0,4},{2,6},{8,0},{10,2},{16,8},{18,10},{24,16},{26,18},{28,24},{3... | collective-permute-start | bytes 884744 | tf_op jit(solution)/shard_map/ppermute | solution.py:103
  80.4 13.2 %collective-permute-start.2 = (bf16[192,768]{1,0:T(8,128)(2,1)S(1)}, bf16[192,768]{1,0:T(8,128)(2,1)}, u32[]{:S(2)}, u32[]{:S(2)}) collective-permute-start(bf16[192,768]{1,0:T(8,128)(2,1)S(1)} %get-tuple-element.80), channel_id=1, source_target_pairs={{0,8},{2,10},{8,16},{10,18},{16,24},{18,26},{24,28},{26,30},{28,20... | collective-permute-start | bytes 884744 | tf_op jit(solution)/shard_map/ppermute | solution.py:103
  96.0 10.3 %collective-permute-start.15 = (bf16[192,768]{1,0:T(8,128)(2,1)}, bf16[192,768]{1,0:T(8,128)(2,1)}, u32[]{:S(2)}, u32[]{:S(2)}) collective-permute-start(bf16[192,768]{1,0:T(8,128)(2,1)} %get-tuple-element.73), channel_id=1, source_target_pairs={{0,4},{2,6},{8,0},{10,2},{16,8},{18,10},{24,16},{26,18},{28,24},{3... | collective-permute-start | bytes 884744 | tf_op jit(solution)/shard_map/ppermute | solution.py:103
  97.6 10.3 %collective-permute-start.11 = (bf16[192,768]{1,0:T(8,128)(2,1)}, bf16[192,768]{1,0:T(8,128)(2,1)}, u32[]{:S(2)}, u32[]{:S(2)}) collective-permute-start(bf16[192,768]{1,0:T(8,128)(2,1)} %get-tuple-element.74), channel_id=1, source_target_pairs={{0,8},{2,10},{8,16},{10,18},{16,24},{18,26},{24,28},{26,30},{28,20... | collective-permute-start | bytes 884744 | tf_op jit(solution)/shard_map/ppermute | solution.py:103
  98.0 12.5 %collective-permute-start.7 = (bf16[192,768]{1,0:T(8,128)(2,1)}, bf16[192,768]{1,0:T(8,128)(2,1)}, u32[]{:S(2)}, u32[]{:S(2)}) collective-permute-start(bf16[192,768]{1,0:T(8,128)(2,1)} %get-tuple-element.75), channel_id=1, source_target_pairs={{0,4},{2,6},{8,0},{10,2},{16,8},{18,10},{24,16},{26,18},{28,24},{3... | collective-permute-start | bytes 884744 | tf_op jit(solution)/shard_map/ppermute | solution.py:103
  99.6 12.2 %collective-permute-start.3 = (bf16[192,768]{1,0:T(8,128)(2,1)S(1)}, bf16[192,768]{1,0:T(8,128)(2,1)}, u32[]{:S(2)}, u32[]{:S(2)}) collective-permute-start(bf16[192,768]{1,0:T(8,128)(2,1)S(1)} %get-tuple-element.76), channel_id=1, source_target_pairs={{0,8},{2,10},{8,16},{10,18},{16,24},{18,26},{24,28},{26,30},{28,20... | collective-permute-start | bytes 884744 | tf_op jit(solution)/shard_map/ppermute | solution.py:103
  100.8 47.1 %collective-permute-start.18 = (bf16[512,1536]{0,1:T(8,128)(2,1)S(1)}, bf16[512,1536]{0,1:T(8,128)(2,1)S(1)}, u32[]{:S(2)}, u32[]{:S(2)}) collective-permute-start(bf16[512,1536]{0,1:T(8,128)(2,1)S(1)} %copy.15), channel_id=1, source_target_pairs={{1,0},{3,2},{5,4},{7,6},{9,8},{11,10},{13,12},{15,14},{17,16},{19,... | collective-permute-start | bytes 4718600 | tf_op jit(solution)/shard_map/ppermute | solution.py:140
  114.5 10.2 %collective-permute-start.16 = (bf16[192,768]{1,0:T(8,128)(2,1)}, bf16[192,768]{1,0:T(8,128)(2,1)}, u32[]{:S(2)}, u32[]{:S(2)}) collective-permute-start(bf16[192,768]{1,0:T(8,128)(2,1)} %get-tuple-element.69), channel_id=1, source_target_pairs={{0,4},{2,6},{8,0},{10,2},{16,8},{18,10},{24,16},{26,18},{28,24},{3... | collective-permute-start | bytes 884744 | tf_op jit(solution)/shard_map/ppermute | solution.py:103
  116.1 9.9 %collective-permute-start.12 = (bf16[192,768]{1,0:T(8,128)(2,1)}, bf16[192,768]{1,0:T(8,128)(2,1)}, u32[]{:S(2)}, u32[]{:S(2)}) collective-permute-start(bf16[192,768]{1,0:T(8,128)(2,1)} %get-tuple-element.70), channel_id=1, source_target_pairs={{0,8},{2,10},{8,16},{10,18},{16,24},{18,26},{24,28},{26,30},{28,20... | collective-permute-start | bytes 884744 | tf_op jit(solution)/shard_map/ppermute | solution.py:103
  116.5 11.3 %collective-permute-start.8 = (bf16[192,768]{1,0:T(8,128)(2,1)}, bf16[192,768]{1,0:T(8,128)(2,1)}, u32[]{:S(2)}, u32[]{:S(2)}) collective-permute-start(bf16[192,768]{1,0:T(8,128)(2,1)} %get-tuple-element.71), channel_id=1, source_target_pairs={{0,4},{2,6},{8,0},{10,2},{16,8},{18,10},{24,16},{26,18},{28,24},{3... | collective-permute-start | bytes 884744 | tf_op jit(solution)/shard_map/ppermute | solution.py:103
  118.1 11.0 %collective-permute-start.4 = (bf16[192,768]{1,0:T(8,128)(2,1)S(1)}, bf16[192,768]{1,0:T(8,128)(2,1)}, u32[]{:S(2)}, u32[]{:S(2)}) collective-permute-start(bf16[192,768]{1,0:T(8,128)(2,1)S(1)} %get-tuple-element.72), channel_id=1, source_target_pairs={{0,8},{2,10},{8,16},{10,18},{16,24},{18,26},{24,28},{26,30},{28,20... | collective-permute-start | bytes 884744 | tf_op jit(solution)/shard_map/ppermute | solution.py:103
  131.8 9.0 %collective-permute-start.17 = (bf16[192,768]{1,0:T(8,128)(2,1)}, bf16[192,768]{1,0:T(8,128)(2,1)}, u32[]{:S(2)}, u32[]{:S(2)}) collective-permute-start(bf16[192,768]{1,0:T(8,128)(2,1)} %get-tuple-element.65), channel_id=1, source_target_pairs={{0,4},{2,6},{8,0},{10,2},{16,8},{18,10},{24,16},{26,18},{28,24},{3... | collective-permute-start | bytes 884744 | tf_op jit(solution)/shard_map/ppermute | solution.py:103
  133.4 8.7 %collective-permute-start.13 = (bf16[192,768]{1,0:T(8,128)(2,1)}, bf16[192,768]{1,0:T(8,128)(2,1)}, u32[]{:S(2)}, u32[]{:S(2)}) collective-permute-start(bf16[192,768]{1,0:T(8,128)(2,1)} %get-tuple-element.66), channel_id=1, source_target_pairs={{0,8},{2,10},{8,16},{10,18},{16,24},{18,26},{24,28},{26,30},{28,20... | collective-permute-start | bytes 884744 | tf_op jit(solution)/shard_map/ppermute | solution.py:103
  133.8 10.1 %collective-permute-start.9 = (bf16[192,768]{1,0:T(8,128)(2,1)}, bf16[192,768]{1,0:T(8,128)(2,1)}, u32[]{:S(2)}, u32[]{:S(2)}) collective-permute-start(bf16[192,768]{1,0:T(8,128)(2,1)} %get-tuple-element.67), channel_id=1, source_target_pairs={{0,4},{2,6},{8,0},{10,2},{16,8},{18,10},{24,16},{26,18},{28,24},{3... | collective-permute-start | bytes 884744 | tf_op jit(solution)/shard_map/ppermute | solution.py:103
  135.4 9.8 %collective-permute-start.5 = (bf16[192,768]{1,0:T(8,128)(2,1)S(1)}, bf16[192,768]{1,0:T(8,128)(2,1)}, u32[]{:S(2)}, u32[]{:S(2)}) collective-permute-start(bf16[192,768]{1,0:T(8,128)(2,1)S(1)} %get-tuple-element.68), channel_id=1, source_target_pairs={{0,8},{2,10},{8,16},{10,18},{16,24},{18,26},{24,28},{26,30},{28,20... | collective-permute-start | bytes 884744 | tf_op jit(solution)/shard_map/ppermute | solution.py:103
  149.7 23.9 %copy-start.4 = (bf16[512,3072]{0,1:T(8,128)(2,1)S(1)}, bf16[512,3072]{0,1:T(8,128)(2,1)}, u32[]{:S(2)}) copy-start(bf16[512,3072]{0,1:T(8,128)(2,1)} %copy-done.3) | copy-start | bytes 9437188
  149.7 19.6 %collective-permute-start.23 = (bf16[512,3072]{0,1:T(8,128)(2,1)}, bf16[512,3072]{0,1:T(8,128)(2,1)}, u32[]{:S(2)}, u32[]{:S(2)}) collective-permute-start(bf16[512,3072]{0,1:T(8,128)(2,1)} %pad_maximum_fusion.1), channel_id=1, source_target_pairs={{0,2},{2,0},{4,6},{6,4},{8,10},{10,8},{12,14},{14,12},{16,18},{18,... | collective-permute-start | bytes 9437192 | tf_op jit(solution)/shard_map/ppermute | solution.py:75
  149.7 23.9 %collective-permute-start.28 = (bf16[512,1536]{1,0:T(8,128)(2,1)}, bf16[512,1536]{1,0:T(8,128)(2,1)}, u32[]{:S(2)}, u32[]{:S(2)}) collective-permute-start(bf16[512,1536]{1,0:T(8,128)(2,1)} %param.2), channel_id=1, source_target_pairs={{0,2},{2,0},{4,6},{6,4},{8,10},{10,8},{12,14},{14,12},{16,18},{18,... | collective-permute-start | bytes 4718600 | tf_op jit(solution)/shard_map/ppermute | solution.py:75
  150.2 10.0 %collective-permute-start.22 = (bf16[192,768]{1,0:T(8,128)(2,1)S(1)}, bf16[192,768]{1,0:T(8,128)(2,1)}, u32[]{:S(2)}, u32[]{:S(2)}) collective-permute-start(bf16[192,768]{1,0:T(8,128)(2,1)S(1)} %get-tuple-element.31), channel_id=1, source_target_pairs={{0,4},{2,6},{8,0},{10,2},{16,8},{18,10},{24,16},{26,18},{28,24},{3... | collective-permute-start | bytes 884744 | tf_op jit(solution)/shard_map/ppermute | solution.py:103
  151.7 9.0 %collective-permute-start.21 = (bf16[192,768]{1,0:T(8,128)(2,1)}, bf16[192,768]{1,0:T(8,128)(2,1)}, u32[]{:S(2)}, u32[]{:S(2)}) collective-permute-start(bf16[192,768]{1,0:T(8,128)(2,1)} %get-tuple-element.30), channel_id=1, source_target_pairs={{0,8},{2,10},{8,16},{10,18},{16,24},{18,26},{24,28},{26,30},{28,20... | collective-permute-start | bytes 884744 | tf_op jit(solution)/shard_map/ppermute | solution.py:103
  152.3 13.3 %collective-permute-start.20 = (bf16[192,768]{1,0:T(8,128)(2,1)}, bf16[192,768]{1,0:T(8,128)(2,1)}, u32[]{:S(2)}, u32[]{:S(2)}) collective-permute-start(bf16[192,768]{1,0:T(8,128)(2,1)} %get-tuple-element.29), channel_id=1, source_target_pairs={{0,4},{2,6},{8,0},{10,2},{16,8},{18,10},{24,16},{26,18},{28,24},{3... | collective-permute-start | bytes 884744 | tf_op jit(solution)/shard_map/ppermute | solution.py:103
  160.2 7.2 %collective-permute-start.19 = (bf16[192,768]{1,0:T(8,128)(2,1)S(1)}, bf16[192,768]{1,0:T(8,128)(2,1)}, u32[]{:S(2)}, u32[]{:S(2)}) collective-permute-start(bf16[192,768]{1,0:T(8,128)(2,1)S(1)} %get-tuple-element.28), channel_id=1, source_target_pairs={{0,8},{2,10},{8,16},{10,18},{16,24},{18,26},{24,28},{26,30},{28,20... | collective-permute-start | bytes 884744 | tf_op jit(solution)/shard_map/ppermute | solution.py:103
  169.3 14.0 %collective-permute-start.27 = (bf16[192,768]{1,0:T(8,128)(2,1)S(1)}, bf16[192,768]{1,0:T(8,128)(2,1)S(1)}, u32[]{:S(2)}, u32[]{:S(2)}) collective-permute-start(bf16[192,768]{1,0:T(8,128)(2,1)S(1)} %get-tuple-element.36), channel_id=1, source_target_pairs={{0,4},{2,6},{8,0},{10,2},{16,8},{18,10},{24,16},{26,18},{28,24},{3... | collective-permute-start | bytes 884744 | tf_op jit(solution)/shard_map/ppermute | solution.py:103
  171.0 12.4 %collective-permute-start.26 = (bf16[192,768]{1,0:T(8,128)(2,1)S(1)}, bf16[192,768]{1,0:T(8,128)(2,1)S(1)}, u32[]{:S(2)}, u32[]{:S(2)}) collective-permute-start(bf16[192,768]{1,0:T(8,128)(2,1)S(1)} %get-tuple-element.35), channel_id=1, source_target_pairs={{0,8},{2,10},{8,16},{10,18},{16,24},{18,26},{24,28},{26,30},{28,20... | collective-permute-start | bytes 884744 | tf_op jit(solution)/shard_map/ppermute | solution.py:103
  171.6 11.8 %collective-permute-start.25 = (bf16[192,768]{1,0:T(8,128)(2,1)S(1)}, bf16[192,768]{1,0:T(8,128)(2,1)S(1)}, u32[]{:S(2)}, u32[]{:S(2)}) collective-permute-start(bf16[192,768]{1,0:T(8,128)(2,1)S(1)} %get-tuple-element.34), channel_id=1, source_target_pairs={{0,4},{2,6},{8,0},{10,2},{16,8},{18,10},{24,16},{26,18},{28,24},{3... | collective-permute-start | bytes 884744 | tf_op jit(solution)/shard_map/ppermute | solution.py:103
  173.0 10.4 %collective-permute-start.24 = (bf16[192,768]{1,0:T(8,128)(2,1)S(1)}, bf16[192,768]{1,0:T(8,128)(2,1)S(1)}, u32[]{:S(2)}, u32[]{:S(2)}) collective-permute-start(bf16[192,768]{1,0:T(8,128)(2,1)S(1)} %get-tuple-element.33), channel_id=1, source_target_pairs={{0,8},{2,10},{8,16},{10,18},{16,24},{18,26},{24,28},{26,30},{28,20... | collective-permute-start | bytes 884744 | tf_op jit(solution)/shard_map/ppermute | solution.py:103
  184.9 8.3 %collective-permute-start.41 = (bf16[192,768]{1,0:T(8,128)(2,1)S(1)}, bf16[192,768]{1,0:T(8,128)(2,1)S(1)}, u32[]{:S(2)}, u32[]{:S(2)}) collective-permute-start(bf16[192,768]{1,0:T(8,128)(2,1)S(1)} %get-tuple-element.40), channel_id=1, source_target_pairs={{0,8},{2,10},{8,16},{10,18},{16,24},{18,26},{24,28},{26,30},{28,20... | collective-permute-start | bytes 884744 | tf_op jit(solution)/shard_map/ppermute | solution.py:103
  185.5 8.0 %collective-permute-start.44 = (bf16[192,768]{1,0:T(8,128)(2,1)S(1)}, bf16[192,768]{1,0:T(8,128)(2,1)S(1)}, u32[]{:S(2)}, u32[]{:S(2)}) collective-permute-start(bf16[192,768]{1,0:T(8,128)(2,1)S(1)} %get-tuple-element.43), channel_id=1, source_target_pairs={{0,4},{2,6},{8,0},{10,2},{16,8},{18,10},{24,16},{26,18},{28,24},{3... | collective-permute-start | bytes 884744 | tf_op jit(solution)/shard_map/ppermute | solution.py:103
  187.0 9.4 %collective-permute-start.43 = (bf16[192,768]{1,0:T(8,128)(2,1)S(1)}, bf16[192,768]{1,0:T(8,128)(2,1)S(1)}, u32[]{:S(2)}, u32[]{:S(2)}) collective-permute-start(bf16[192,768]{1,0:T(8,128)(2,1)S(1)} %get-tuple-element.42), channel_id=1, source_target_pairs={{0,8},{2,10},{8,16},{10,18},{16,24},{18,26},{24,28},{26,30},{28,20... | collective-permute-start | bytes 884744 | tf_op jit(solution)/shard_map/ppermute | solution.py:103
  187.5 9.1 %collective-permute-start.42 = (bf16[192,768]{1,0:T(8,128)(2,1)S(1)}, bf16[192,768]{1,0:T(8,128)(2,1)S(1)}, u32[]{:S(2)}, u32[]{:S(2)}) collective-permute-start(bf16[192,768]{1,0:T(8,128)(2,1)S(1)} %get-tuple-element.41), channel_id=1, source_target_pairs={{0,4},{2,6},{8,0},{10,2},{16,8},{18,10},{24,16},{26,18},{28,24},{3... | collective-permute-start | bytes 884744 | tf_op jit(solution)/shard_map/ppermute | solution.py:103
  200.4 9.2 %collective-permute-start.35 = (bf16[96,1536]{1,0:T(8,128)(2,1)S(1)}, bf16[96,1536]{1,0:T(8,128)(2,1)S(1)}, u32[]{:S(2)}, u32[]{:S(2)}) collective-permute-start(bf16[96,1536]{1,0:T(8,128)(2,1)S(1)} %get-tuple-element.95), channel_id=1, source_target_pairs={{0,4},{2,6},{8,0},{10,2},{16,8},{18,10},{24,16},{26,18},{28,24},{3... | collective-permute-start | bytes 884744 | tf_op jit(solution)/shard_map/ppermute | solution.py:103
  202.0 10.9 %collective-permute-start.29 = (bf16[96,1536]{1,0:T(8,128)(2,1)S(1)}, bf16[96,1536]{1,0:T(8,128)(2,1)S(1)}, u32[]{:S(2)}, u32[]{:S(2)}) collective-permute-start(bf16[96,1536]{1,0:T(8,128)(2,1)S(1)} %get-tuple-element.96), channel_id=1, source_target_pairs={{0,8},{2,10},{8,16},{10,18},{16,24},{18,26},{24,28},{26,30},{28,20... | collective-permute-start | bytes 884744 | tf_op jit(solution)/shard_map/ppermute | solution.py:103
  214.2 16.3 %collective-permute-start.36 = (bf16[96,1536]{1,0:T(8,128)(2,1)S(1)}, bf16[96,1536]{1,0:T(8,128)(2,1)S(1)}, u32[]{:S(2)}, u32[]{:S(2)}) collective-permute-start(bf16[96,1536]{1,0:T(8,128)(2,1)S(1)} %get-tuple-element.93), channel_id=1, source_target_pairs={{0,4},{2,6},{8,0},{10,2},{16,8},{18,10},{24,16},{26,18},{28,24},{3... | collective-permute-start | bytes 884744 | tf_op jit(solution)/shard_map/ppermute | solution.py:103
  217.4 15.6 %collective-permute-start.30 = (bf16[96,1536]{1,0:T(8,128)(2,1)S(1)}, bf16[96,1536]{1,0:T(8,128)(2,1)S(1)}, u32[]{:S(2)}, u32[]{:S(2)}) collective-permute-start(bf16[96,1536]{1,0:T(8,128)(2,1)S(1)} %get-tuple-element.94), channel_id=1, source_target_pairs={{0,8},{2,10},{8,16},{10,18},{16,24},{18,26},{24,28},{26,30},{28,20... | collective-permute-start | bytes 884744 | tf_op jit(solution)/shard_map/ppermute | solution.py:103
  234.2 15.9 %collective-permute-start.37 = (bf16[96,1536]{1,0:T(8,128)(2,1)S(1)}, bf16[96,1536]{1,0:T(8,128)(2,1)S(1)}, u32[]{:S(2)}, u32[]{:S(2)}) collective-permute-start(bf16[96,1536]{1,0:T(8,128)(2,1)S(1)} %get-tuple-element.91), channel_id=1, source_target_pairs={{0,4},{2,6},{8,0},{10,2},{16,8},{18,10},{24,16},{26,18},{28,24},{3... | collective-permute-start | bytes 884744 | tf_op jit(solution)/shard_map/ppermute | solution.py:103
  234.3 15.9 %collective-permute-start.31 = (bf16[96,1536]{1,0:T(8,128)(2,1)S(1)}, bf16[96,1536]{1,0:T(8,128)(2,1)S(1)}, u32[]{:S(2)}, u32[]{:S(2)}) collective-permute-start(bf16[96,1536]{1,0:T(8,128)(2,1)S(1)} %get-tuple-element.92), channel_id=1, source_target_pairs={{0,8},{2,10},{8,16},{10,18},{16,24},{18,26},{24,28},{26,30},{28,20... | collective-permute-start | bytes 884744 | tf_op jit(solution)/shard_map/ppermute | solution.py:103
  251.4 16.3 %collective-permute-start.38 = (bf16[96,1536]{1,0:T(8,128)(2,1)S(1)}, bf16[96,1536]{1,0:T(8,128)(2,1)S(1)}, u32[]{:S(2)}, u32[]{:S(2)}) collective-permute-start(bf16[96,1536]{1,0:T(8,128)(2,1)S(1)} %get-tuple-element.89), channel_id=1, source_target_pairs={{0,4},{2,6},{8,0},{10,2},{16,8},{18,10},{24,16},{26,18},{28,24},{3... | collective-permute-start | bytes 884744 | tf_op jit(solution)/shard_map/ppermute | solution.py:103
  251.4 16.2 %collective-permute-start.32 = (bf16[96,1536]{1,0:T(8,128)(2,1)S(1)}, bf16[96,1536]{1,0:T(8,128)(2,1)S(1)}, u32[]{:S(2)}, u32[]{:S(2)}) collective-permute-start(bf16[96,1536]{1,0:T(8,128)(2,1)S(1)} %get-tuple-element.90), channel_id=1, source_target_pairs={{0,8},{2,10},{8,16},{10,18},{16,24},{18,26},{24,28},{26,30},{28,20... | collective-permute-start | bytes 884744 | tf_op jit(solution)/shard_map/ppermute | solution.py:103
  268.8 14.3 %collective-permute-start.39 = (bf16[96,1536]{1,0:T(8,128)(2,1)S(1)}, bf16[96,1536]{1,0:T(8,128)(2,1)S(1)}, u32[]{:S(2)}, u32[]{:S(2)}) collective-permute-start(bf16[96,1536]{1,0:T(8,128)(2,1)S(1)} %get-tuple-element.87), channel_id=1, source_target_pairs={{0,4},{2,6},{8,0},{10,2},{16,8},{18,10},{24,16},{26,18},{28,24},{3... | collective-permute-start | bytes 884744 | tf_op jit(solution)/shard_map/ppermute | solution.py:103
  269.5 14.4 %collective-permute-start.33 = (bf16[96,1536]{1,0:T(8,128)(2,1)S(1)}, bf16[96,1536]{1,0:T(8,128)(2,1)S(1)}, u32[]{:S(2)}, u32[]{:S(2)}) collective-permute-start(bf16[96,1536]{1,0:T(8,128)(2,1)S(1)} %get-tuple-element.88), channel_id=1, source_target_pairs={{0,8},{2,10},{8,16},{10,18},{16,24},{18,26},{24,28},{26,30},{28,20... | collective-permute-start | bytes 884744 | tf_op jit(solution)/shard_map/ppermute | solution.py:103
  273.9 13.2 %collective-permute-start.45 = (f32[2]{0:T(128)S(1)}, f32[2]{0:T(128)S(1)}, u32[]{:S(2)}, u32[]{:S(2)}) collective-permute-start(f32[2]{0:T(128)S(1)} %pad_maximum_fusion.4), channel_id=1, source_target_pairs={{0,2},{2,0},{4,6},{6,4},{8,10},{10,8},{12,14},{14,12},{16,18},{18,... | collective-permute-start | bytes 32 | tf_op jit(solution)/shard_map/ppermute | solution.py:114
  285.0 22.8 %collective-permute-start.40 = (bf16[96,1536]{1,0:T(8,128)(2,1)S(1)}, bf16[96,1536]{1,0:T(8,128)(2,1)S(1)}, u32[]{:S(2)}, u32[]{:S(2)}) collective-permute-start(bf16[96,1536]{1,0:T(8,128)(2,1)S(1)} %get-tuple-element.85), channel_id=1, source_target_pairs={{0,4},{2,6},{8,0},{10,2},{16,8},{18,10},{24,16},{26,18},{28,24},{3... | collective-permute-start | bytes 884744 | tf_op jit(solution)/shard_map/ppermute | solution.py:103
  285.2 22.6 %collective-permute-start.34 = (bf16[96,1536]{1,0:T(8,128)(2,1)S(1)}, bf16[96,1536]{1,0:T(8,128)(2,1)S(1)}, u32[]{:S(2)}, u32[]{:S(2)}) collective-permute-start(bf16[96,1536]{1,0:T(8,128)(2,1)S(1)} %get-tuple-element.86), channel_id=1, source_target_pairs={{0,8},{2,10},{8,16},{10,18},{16,24},{18,26},{24,28},{26,30},{28,20... | collective-permute-start | bytes 884744 | tf_op jit(solution)/shard_map/ppermute | solution.py:103
  288.5 9.9 %collective-permute-start.46 = (f32[2]{0:T(128)S(1)}, f32[2]{0:T(128)S(1)}, u32[]{:S(2)}, u32[]{:S(2)}) collective-permute-start(f32[2]{0:T(128)S(1)} %fusion.13), channel_id=1, source_target_pairs={{0,4},{2,6},{4,0},{6,2},{8,12},{10,14},{12,8},{14,10},{16,20},{18,... | collective-permute-start | bytes 32 | tf_op jit(solution)/shard_map/ppermute | solution.py:114
  299.8 3.5 collective-permute-start.47
  303.4 4.4 collective-permute-start.48
  309.0 13.1 %collective-permute-start.49 = (bf16[96,1536]{1,0:T(8,128)(2,1)S(1)}, bf16[96,1536]{1,0:T(8,128)(2,1)S(1)}, u32[]{:S(2)}, u32[]{:S(2)}) collective-permute-start(bf16[96,1536]{1,0:T(8,128)(2,1)S(1)} %get-tuple-element.45), channel_id=1, source_target_pairs={{0,8},{2,10},{8,16},{10,18},{16,24},{18,26},{24,28},{26,30},{28,20... | collective-permute-start | bytes 884744 | tf_op jit(solution)/shard_map/ppermute | solution.py:103
  310.7 13.0 %collective-permute-start.50 = (bf16[96,1536]{1,0:T(8,128)(2,1)S(1)}, bf16[96,1536]{1,0:T(8,128)(2,1)S(1)}, u32[]{:S(2)}, u32[]{:S(2)}) collective-permute-start(bf16[96,1536]{1,0:T(8,128)(2,1)S(1)} %get-tuple-element.46), channel_id=1, source_target_pairs={{0,4},{2,6},{8,0},{10,2},{16,8},{18,10},{24,16},{26,18},{28,24},{3... | collective-permute-start | bytes 884744 | tf_op jit(solution)/shard_map/ppermute | solution.py:103
  324.9 10.8 %collective-permute-start.51 = (bf16[96,3072]{1,0:T(8,128)(2,1)S(1)}, bf16[96,3072]{1,0:T(8,128)(2,1)S(1)}, u32[]{:S(2)}, u32[]{:S(2)}) collective-permute-start(bf16[96,3072]{1,0:T(8,128)(2,1)S(1)} %pad_maximum_fusion.3), channel_id=1, source_target_pairs={{0,1},{2,3},{4,5},{6,7},{8,9},{10,11},{12,13},{14,15},{16,17},{18,... | collective-permute-start | bytes 1769480 | tf_op jit(solution)/shard_map/ppermute | solution.py:172
  422.3 30.7 %collective-permute-start.52 = (bf16[3072,192]{0,1:T(8,128)(2,1)S(1)}, bf16[3072,192]{0,1:T(8,128)(2,1)S(1)}, u32[]{:S(2)}, u32[]{:S(2)}) collective-permute-start(bf16[3072,192]{0,1:T(8,128)(2,1)S(1)} %all_to_all.17), channel_id=1, source_target_pairs={{1,0},{3,2},{5,4},{7,6},{9,8},{11,10},{13,12},{15,14},{17,16},{19,... | collective-permute-start | bytes 3538952 | tf_op jit(solution)/shard_map/ppermute | solution.py:182
  510.1 22.2 %collective-permute-start.53 = (bf16[192,1536]{1,0:T(8,128)(2,1)S(1)}, bf16[192,1536]{1,0:T(8,128)(2,1)S(1)}, u32[]{:S(2)}, u32[]{:S(2)}) collective-permute-start(bf16[192,1536]{1,0:T(8,128)(2,1)S(1)} %dynamic_slice.274), channel_id=1, source_target_pairs={{0,1},{2,3},{4,5},{6,7},{8,9},{10,11},{12,13},{14,15},{16,17},{18,... | collective-permute-start | bytes 1769480 | tf_op jit(solution)/shard_map/ppermute | solution.py:190
  512.8 1.2 collective-permute-start.54
  515.4 3.6 collective-permute-start.55
  519.6 3.6 collective-permute-start.56
  523.9 4.5 collective-permute-start.57
  529.0 2.6 collective-permute-start.58
  (1 other events, 1.7 us)
Sparse Core Ops, SparseCore 0:
  199.4 137.4 all-gather.1

commit v5 on v4

--- a/solution.py
+++ b/solution.py
@@ -178,8 +178,15 @@
     scale = lax.rsqrt(square + 2.0 * damp * trace + D * damp * damp)
 
     left = series(grad_rows.astype(f32), cov, scale, damp).astype(bf16)
-    left = lax.all_to_all(left, "dp", split_axis=1, concat_axis=0, tiled=True)
-    left = lax.ppermute(left, "grp", [(part + j, j) for j in range(part)])
+    blocks = left.reshape(rows, n, rows).transpose(1, 0, 2)
+    got = []
+    for turn in range(n):
+        piece = lax.dynamic_index_in_dim(blocks, (dp_index + turn) % n, 0, keepdims=False)
+        moves = [
+            (i * c + part + j, (i + turn) % n * c + j) for i in range(n) for j in range(part)
+        ]
+        got.append(lax.ppermute(piece, ("dp", "grp"), moves))
+    left = lax.dynamic_slice_in_dim(jnp.stack(2 * got[::-1]), n - 1 - dp_index, n, 0)
     left = left.reshape(chips, 2, c, D // c // n, rows).transpose(2, 1, 0, 3, 4).reshape(D, rows)
     precond = series(left.T.astype(f32), cov, scale, damp)
 

time: 541 us -> 522 us (0.965)
  blocking collectives: 40.8 us -> 0 us
  starting transfers between devices: 69.9 us -> 86.3 us
    all_to_all x1 -> x0, blocking collectives: 40.8 us -> none  [shards(): left = lax.all_to_all(left, 'dp', split_axis=1, concat_axis=0, tiled=True)]
    ppermute x1 -> x16, starting transfers between devices: 1.51 us -> 20.6 us  [shards(): got.append(lax.ppermute(piece, ('dp', 'grp'), moves))]
    convert_element_type x3 -> x2, local copies, waits for them, and re-layouts: 14.2 us -> 7.71 us  [shards(): precond = series(left.T.astype(f32), cov, scale, damp)]
    unnamed x12 -> x59, local copies, waits for them, and re-layouts: 8.76 us -> 14.6 us
    ppermute x1 -> x16, waiting for transfers between devices: 29.1 us -> 26.8 us  [shards(): got.append(lax.ppermute(piece, ('dp', 'grp'), moves))]
  transfers between devices with their start and end apart: 60 -> 75, of which waited for: 46 -> 52; matrix products, arithmetic and copies ran while one was open for 7% -> 8% of each run, Pallas kernels for 0% -> 0%
where the time goes in v5:
time: 522 us; the launch traced here: 520 us
  waiting for transfers between devices  233 us (45%)
  starting transfers between devices  86.3 us (17%)
  Pallas kernels  82.7 us (16%)
  other arithmetic  41.8 us (8%)
  local copies, waits for them, and re-layouts  32.1 us (6%)
  between operations  22.1 us (4%)
  matrix products  21.8 us (4%)
    ppermute x42, waiting for transfers between devices, ring_reduce(): got = lax.ppermute(totals[lane].astype(bf16), 'dp', moves)  140 us
    pallas_call x2, Pallas kernels, series(): pl.pallas_call(kernel, out_shape=jax.ShapeDtypeStruct((rows, D), f32), in...  82.7 us
    ppermute x42, starting transfers between devices, ring_reduce(): got = lax.ppermute(totals[lane].astype(bf16), 'dp', moves)  44.4 us
    ppermute x1, waiting for transfers between devices, shards(): lax.ppermute(jnp.where(on_g, activations, cotangents), 'grp', [(0, 1), (1...  34.4 us
    ppermute x16, waiting for transfers between devices, shards(): got.append(lax.ppermute(piece, ('dp', 'grp'), moves))  26.8 us
    ppermute x8, waiting for transfers between devices, sum_dp(): x = x + lax.ppermute(x, 'dp', [(i, i ^ hop) for i in range(n)])  22.8 us
    dot_general x2, matrix products, dot_rows(): lax.dot_general(left, right, (((0,), (0,)), ((), ())), preferred_element_...  21.8 us
    ppermute x16, starting transfers between devices, shards(): got.append(lax.ppermute(piece, ('dp', 'grp'), moves))  20.6 us
  transfers between devices with their start and end apart: 75, of which 52 were waited for; matrix products, arithmetic and copies ran while one was open for 8% of the time, Pallas kernels for 0%

profile of v5, /device:TPU:0, one launch (start us, length us, event | category | flops | bytes accessed | tf_op | source)
XLA Modules:
  0.0 520.2 jit_solution(4347723893527458766)
XLA Ops:
  6.5 1.7 copy.4
  8.3 1.7 copy.3
  10.2 3.0 collective-permute-start
  13.2 34.4 %collective-permute-done = bf16[512,1536]{0,1:T(8,128)(2,1)S(1)} collective-permute-done((bf16[512,1536]{0,1:T(8,128)(2,1)S(1)}, bf16[512,1536]{0,1:T(8,128)(2,1)S(1)}, u32[]{:S(2)}, u32[]{:S(2)}) %collective-permute-start) | collective-permute-done | bytes 1572896 | tf_op jit(solution)/shard_map/ppermute | solution.py:119
  47.6 2.2 maximum_select_fusion.4
  49.8 5.9 %collective-permute-done.1 = bf16[512,3072]{0,1:T(8,128)(2,1)S(1)} collective-permute-done((bf16[512,3072]{0,1:T(8,128)(2,1)}, bf16[512,3072]{0,1:T(8,128)(2,1)S(1)}, u32[]{:S(2)}, u32[]{:S(2)}) %collective-permute-start.1) | collective-permute-done | bytes 3145760 | tf_op jit(solution)/shard_map/ppermute | solution.py:75
  55.7 4.0 pad_maximum_fusion
  60.0 12.1 %convolution_convert_fusion = bf16[1536,3072]{1,0:T(8,128)(2,1)S(1)} fusion(bf16[1024,1536]{0,1:T(8,128)(2,1)S(1)} %bitcast.117, bf16[512,3072]{0,1:T(8,128)(2,1)} %copy-done.3, bf16[512,3072]{0,1:T(8,128)(2,1)} %maximum_select_fusion.4), kind=kOutput, calls=%fused_computation | convolution fusion | flops 9680977920 | bytes 18874368 | tf_op jit(solution)/shard_map/dot_general | solution.py:18
  72.2 3.7 copy-done.1
  76.7 1.8 collective-permute-start.14
  78.7 1.8 collective-permute-start.6
  80.7 6.0 %collective-permute-done.14 = bf16[192,768]{1,0:T(8,128)(2,1)S(1)} collective-permute-done((bf16[192,768]{1,0:T(8,128)(2,1)}, bf16[192,768]{1,0:T(8,128)(2,1)S(1)}, u32[]{:S(2)}, u32[]{:S(2)}) %collective-permute-start.14) | collective-permute-done | bytes 294944 | tf_op jit(solution)/shard_map/ppermute | solution.py:103
  88.3 4.0 collective-permute-done.6
  93.6 2.4 add_convert_fusion.14
  102.2 4.1 collective-permute-done.15
  107.9 2.7 collective-permute-done.7
  111.9 2.7 add_convert_fusion.13
  118.6 6.1 %collective-permute-done.16 = bf16[192,768]{1,0:T(8,128)(2,1)} collective-permute-done((bf16[192,768]{1,0:T(8,128)(2,1)}, bf16[192,768]{1,0:T(8,128)(2,1)}, u32[]{:S(2)}, u32[]{:S(2)}) %collective-permute-start.16) | collective-permute-done | bytes 294944 | tf_op jit(solution)/shard_map/ppermute | solution.py:103
  126.0 1.9 collective-permute-done.8
  129.2 2.7 add_convert_fusion.12
  135.9 4.9 collective-permute-done.17
  142.1 1.9 collective-permute-done.9
  145.3 2.7 convert_add_fusion.14
  148.0 1.8 pad_maximum_fusion.1
  153.8 6.5 %collective-permute-done.22 = bf16[192,768]{1,0:T(8,128)(2,1)} collective-permute-done((bf16[192,768]{1,0:T(8,128)(2,1)S(1)}, bf16[192,768]{1,0:T(8,128)(2,1)}, u32[]{:S(2)}, u32[]{:S(2)}) %collective-permute-start.22) | collective-permute-done | bytes 294944 | tf_op jit(solution)/shard_map/ppermute | solution.py:103
  160.8 4.9 collective-permute-done.20
  165.7 1.8 collective-permute-done.19
  167.5 1.9 convert_add_fusion.10
  173.7 9.7 %fusion.4 = bf16[768,3072]{1,0:T(8,128)(2,1)} fusion(bf16[512,3072]{0,1:T(8,128)(2,1)} %collective-permute-done.23, bf16[512,3072]{0,1:T(8,128)(2,1)} %pad_maximum_fusion.1, pred[]{:T(512)S(6)} %ge.3, s32[]{:T(128)S(6)} %select_n.564, bf16[512,1536]{1,0:T(8,128)(2,1)} %param.2, bf16[512,1536]{1,0:T(8,128)(2,1)} %collective-permute-done.28, ...), kind=kOutput, calls=%fused_computation.7 | convolution fusion | flops 4865654784 | bytes 20447236 | tf_op jit(solution)/shard_map/dot_general | solution.py:18
  189.0 4.2 collective-permute-done.41
  193.4 3.0 collective-permute-done.43
  202.5 7.1 %collective-permute-done.35 = bf16[96,1536]{1,0:T(8,128)(2,1)S(1)} collective-permute-done((bf16[96,1536]{1,0:T(8,128)(2,1)S(1)}, bf16[96,1536]{1,0:T(8,128)(2,1)S(1)}, u32[]{:S(2)}, u32[]{:S(2)}) %collective-permute-start.35) | collective-permute-done | bytes 294944 | tf_op jit(solution)/shard_map/ppermute | solution.py:103
  209.6 3.3 collective-permute-done.29
  214.2 3.2 collective-permute-start.36
  217.4 13.1 %collective-permute-done.36 = bf16[96,1536]{1,0:T(8,128)(2,1)S(1)} collective-permute-done((bf16[96,1536]{1,0:T(8,128)(2,1)S(1)}, bf16[96,1536]{1,0:T(8,128)(2,1)S(1)}, u32[]{:S(2)}, u32[]{:S(2)}) %collective-permute-start.36) | collective-permute-done | bytes 294944 | tf_op jit(solution)/shard_map/ppermute | solution.py:103
  230.4 2.6 collective-permute-done.30
  234.3 2.0 collective-permute-start.31
  236.3 13.9 %collective-permute-done.37 = bf16[96,1536]{1,0:T(8,128)(2,1)S(1)} collective-permute-done((bf16[96,1536]{1,0:T(8,128)(2,1)S(1)}, bf16[96,1536]{1,0:T(8,128)(2,1)S(1)}, u32[]{:S(2)}, u32[]{:S(2)}) %collective-permute-start.37) | collective-permute-done | bytes 294944 | tf_op jit(solution)/shard_map/ppermute | solution.py:103
  251.5 2.2 collective-permute-start.32
  253.6 14.1 %collective-permute-done.38 = bf16[96,1536]{1,0:T(8,128)(2,1)S(1)} collective-permute-done((bf16[96,1536]{1,0:T(8,128)(2,1)S(1)}, bf16[96,1536]{1,0:T(8,128)(2,1)S(1)}, u32[]{:S(2)}, u32[]{:S(2)}) %collective-permute-start.38) | collective-permute-done | bytes 294944 | tf_op jit(solution)/shard_map/ppermute | solution.py:103
  273.8 9.4 %collective-permute-done.39 = bf16[96,1536]{1,0:T(8,128)(2,1)S(1)} collective-permute-done((bf16[96,1536]{1,0:T(8,128)(2,1)S(1)}, bf16[96,1536]{1,0:T(8,128)(2,1)S(1)}, u32[]{:S(2)}, u32[]{:S(2)}) %collective-permute-start.39) | collective-permute-done | bytes 294944 | tf_op jit(solution)/shard_map/ppermute | solution.py:103
  285.4 1.8 collective-permute-start.34
  288.7 9.9 %collective-permute-done.46 = f32[2]{0:T(128)S(1)} collective-permute-done((f32[2]{0:T(128)S(1)}, f32[2]{0:T(128)S(1)}, u32[]{:S(2)}, u32[]{:S(2)}) %collective-permute-start.46) | collective-permute-done | bytes 40 | tf_op jit(solution)/shard_map/ppermute | solution.py:114
  299.9 3.5 collective-permute-done.47
  303.4 2.4 collective-permute-start.48
  305.8 2.0 collective-permute-done.48
  311.2 11.0 %collective-permute-done.49 = bf16[96,1536]{1,0:T(8,128)(2,1)S(1)} collective-permute-done((bf16[96,1536]{1,0:T(8,128)(2,1)S(1)}, bf16[96,1536]{1,0:T(8,128)(2,1)S(1)}, u32[]{:S(2)}, u32[]{:S(2)}) %collective-permute-start.49) | collective-permute-done | bytes 294944 | tf_op jit(solution)/shard_map/ppermute | solution.py:103
  324.9 3.7 collective-permute-start.51
  333.2 2.6 collective-permute-done.51
  336.9 41.4 %series.2 = f32[192,3072]{1,0:T(8,128)S(1)} custom-call(f32[2]{0:T(128)S(1)} %pad_maximum_fusion.5.scalar_ref, f32[192,3072]{1,0:T(8,128)S(1)} %maximum_convert_fusion.start_ref, bf16[3072,3072]{1,0:T(8,128)(2,1)} %all-gather.2.cloned.1.call-done.cov_ref), custom_call_target="tpu_custom_call" | custom-call | flops 25367150592 | bytes 23592960 | tf_op jit(solution)/shard_map/series/pallas_call | solution.py:43
  378.4 1.8 reshape.55
  380.2 4.3 constant_dynamic-slice_fusion.1
  403.3 2.6 collective-permute-done.57
  408.5 14.9 %collective-permute-done.59 = bf16[192,192]{1,0:T(8,128)(2,1)S(1)} collective-permute-done((bf16[192,192]{1,0:T(8,128)(2,1)S(1)}, bf16[192,192]{1,0:T(8,128)(2,1)S(1)}, u32[]{:S(2)}, u32[]{:S(2)}) %collective-permute-start.59) | collective-permute-done | bytes 73760 | tf_op jit(solution)/shard_map/ppermute | solution.py:188
  428.7 3.4 collective-permute-done.64
  432.1 3.6 collective-permute-done.65
  436.3 1.7 collective-permute-done.67
  438.7 3.2 copy.25
  441.9 4.5 reshape.56
  448.1 41.4 %series.3 = f32[192,3072]{1,0:T(8,128)S(1)} custom-call(f32[2]{0:T(128)S(1)} %pad_maximum_fusion.5.scalar_ref, f32[192,3072]{1,0:T(8,128)S(1)} %bitcast.114, bf16[3072,3072]{1,0:T(8,128)(2,1)} %all-gather.2.cloned.1.call-done.cov_ref), custom_call_target="tpu_custom_call" | custom-call | flops 25367150592 | bytes 23592960 | tf_op jit(solution)/shard_map/series/pallas_call | solution.py:43
  494.9 3.3 collective-permute-start.70
  500.7 2.3 collective-permute-done.71
  505.0 3.2 collective-permute-done.72
  508.9 2.6 collective-permute-start.73
  (195 shorter events, 108.1 us)
Async XLA Ops:
  6.5 330.3 %all-gather.2.cloned.1.call-start = ((), (), s32[]{:S(2)}) async-start(), calls=%async_computation | async-start | bytes 20054016 | tf_op jit(solution)/shard_map/all_gather | solution.py:162
  10.2 37.4 %collective-permute-start = (bf16[512,1536]{0,1:T(8,128)(2,1)S(1)}, bf16[512,1536]{0,1:T(8,128)(2,1)S(1)}, u32[]{:S(2)}, u32[]{:S(2)}) collective-permute-start(bf16[512,1536]{0,1:T(8,128)(2,1)S(1)} %broadcast_select_fusion), channel_id=1, source_target_pairs={{0,1},{1,0},{2,3},{3,2},{4,5},{5,4},{6,7},{7,6},{8,9},{9,8},{10,11... | collective-permute-start | bytes 4718600 | tf_op jit(solution)/shard_map/ppermute | solution.py:119
  76.7 10.1 %collective-permute-start.14 = (bf16[192,768]{1,0:T(8,128)(2,1)}, bf16[192,768]{1,0:T(8,128)(2,1)S(1)}, u32[]{:S(2)}, u32[]{:S(2)}) collective-permute-start(bf16[192,768]{1,0:T(8,128)(2,1)} %get-tuple-element.77), channel_id=1, source_target_pairs={{0,4},{2,6},{8,0},{10,2},{16,8},{18,10},{24,16},{26,18},{28,24},{3... | collective-permute-start | bytes 884744 | tf_op jit(solution)/shard_map/ppermute | solution.py:103
  78.4 9.9 %collective-permute-start.10 = (bf16[192,768]{1,0:T(8,128)(2,1)S(1)}, bf16[192,768]{1,0:T(8,128)(2,1)S(1)}, u32[]{:S(2)}, u32[]{:S(2)}) collective-permute-start(bf16[192,768]{1,0:T(8,128)(2,1)S(1)} %get-tuple-element.78), channel_id=1, source_target_pairs={{0,8},{2,10},{8,16},{10,18},{16,24},{18,26},{24,28},{26,30},{28,20... | collective-permute-start | bytes 884744 | tf_op jit(solution)/shard_map/ppermute | solution.py:103
  78.7 13.6 %collective-permute-start.6 = (bf16[192,768]{1,0:T(8,128)(2,1)S(1)}, bf16[192,768]{1,0:T(8,128)(2,1)S(1)}, u32[]{:S(2)}, u32[]{:S(2)}) collective-permute-start(bf16[192,768]{1,0:T(8,128)(2,1)S(1)} %get-tuple-element.79), channel_id=1, source_target_pairs={{0,4},{2,6},{8,0},{10,2},{16,8},{18,10},{24,16},{26,18},{28,24},{3... | collective-permute-start | bytes 884744 | tf_op jit(solution)/shard_map/ppermute | solution.py:103
  80.5 13.2 %collective-permute-start.2 = (bf16[192,768]{1,0:T(8,128)(2,1)S(1)}, bf16[192,768]{1,0:T(8,128)(2,1)}, u32[]{:S(2)}, u32[]{:S(2)}) collective-permute-start(bf16[192,768]{1,0:T(8,128)(2,1)S(1)} %get-tuple-element.80), channel_id=1, source_target_pairs={{0,8},{2,10},{8,16},{10,18},{16,24},{18,26},{24,28},{26,30},{28,20... | collective-permute-start | bytes 884744 | tf_op jit(solution)/shard_map/ppermute | solution.py:103
  96.0 10.3 %collective-permute-start.15 = (bf16[192,768]{1,0:T(8,128)(2,1)}, bf16[192,768]{1,0:T(8,128)(2,1)}, u32[]{:S(2)}, u32[]{:S(2)}) collective-permute-start(bf16[192,768]{1,0:T(8,128)(2,1)} %get-tuple-element.73), channel_id=1, source_target_pairs={{0,4},{2,6},{8,0},{10,2},{16,8},{18,10},{24,16},{26,18},{28,24},{3... | collective-permute-start | bytes 884744 | tf_op jit(solution)/shard_map/ppermute | solution.py:103
  97.6 10.3 %collective-permute-start.11 = (bf16[192,768]{1,0:T(8,128)(2,1)}, bf16[192,768]{1,0:T(8,128)(2,1)}, u32[]{:S(2)}, u32[]{:S(2)}) collective-permute-start(bf16[192,768]{1,0:T(8,128)(2,1)} %get-tuple-element.74), channel_id=1, source_target_pairs={{0,8},{2,10},{8,16},{10,18},{16,24},{18,26},{24,28},{26,30},{28,20... | collective-permute-start | bytes 884744 | tf_op jit(solution)/shard_map/ppermute | solution.py:103
  98.1 12.5 %collective-permute-start.7 = (bf16[192,768]{1,0:T(8,128)(2,1)}, bf16[192,768]{1,0:T(8,128)(2,1)}, u32[]{:S(2)}, u32[]{:S(2)}) collective-permute-start(bf16[192,768]{1,0:T(8,128)(2,1)} %get-tuple-element.75), channel_id=1, source_target_pairs={{0,4},{2,6},{8,0},{10,2},{16,8},{18,10},{24,16},{26,18},{28,24},{3... | collective-permute-start | bytes 884744 | tf_op jit(solution)/shard_map/ppermute | solution.py:103
  99.6 12.2 %collective-permute-start.3 = (bf16[192,768]{1,0:T(8,128)(2,1)S(1)}, bf16[192,768]{1,0:T(8,128)(2,1)}, u32[]{:S(2)}, u32[]{:S(2)}) collective-permute-start(bf16[192,768]{1,0:T(8,128)(2,1)S(1)} %get-tuple-element.76), channel_id=1, source_target_pairs={{0,8},{2,10},{8,16},{10,18},{16,24},{18,26},{24,28},{26,30},{28,20... | collective-permute-start | bytes 884744 | tf_op jit(solution)/shard_map/ppermute | solution.py:103
  100.8 47.2 %collective-permute-start.18 = (bf16[512,1536]{0,1:T(8,128)(2,1)S(1)}, bf16[512,1536]{0,1:T(8,128)(2,1)S(1)}, u32[]{:S(2)}, u32[]{:S(2)}) collective-permute-start(bf16[512,1536]{0,1:T(8,128)(2,1)S(1)} %copy.7), channel_id=1, source_target_pairs={{1,0},{3,2},{5,4},{7,6},{9,8},{11,10},{13,12},{15,14},{17,16},{19,... | collective-permute-start | bytes 4718600 | tf_op jit(solution)/shard_map/ppermute | solution.py:140
  114.6 10.2 %collective-permute-start.16 = (bf16[192,768]{1,0:T(8,128)(2,1)}, bf16[192,768]{1,0:T(8,128)(2,1)}, u32[]{:S(2)}, u32[]{:S(2)}) collective-permute-start(bf16[192,768]{1,0:T(8,128)(2,1)} %get-tuple-element.69), channel_id=1, source_target_pairs={{0,4},{2,6},{8,0},{10,2},{16,8},{18,10},{24,16},{26,18},{28,24},{3... | collective-permute-start | bytes 884744 | tf_op jit(solution)/shard_map/ppermute | solution.py:103
  116.1 9.9 %collective-permute-start.12 = (bf16[192,768]{1,0:T(8,128)(2,1)}, bf16[192,768]{1,0:T(8,128)(2,1)}, u32[]{:S(2)}, u32[]{:S(2)}) collective-permute-start(bf16[192,768]{1,0:T(8,128)(2,1)} %get-tuple-element.70), channel_id=1, source_target_pairs={{0,8},{2,10},{8,16},{10,18},{16,24},{18,26},{24,28},{26,30},{28,20... | collective-permute-start | bytes 884744 | tf_op jit(solution)/shard_map/ppermute | solution.py:103
  116.6 11.3 %collective-permute-start.8 = (bf16[192,768]{1,0:T(8,128)(2,1)}, bf16[192,768]{1,0:T(8,128)(2,1)}, u32[]{:S(2)}, u32[]{:S(2)}) collective-permute-start(bf16[192,768]{1,0:T(8,128)(2,1)} %get-tuple-element.71), channel_id=1, source_target_pairs={{0,4},{2,6},{8,0},{10,2},{16,8},{18,10},{24,16},{26,18},{28,24},{3... | collective-permute-start | bytes 884744 | tf_op jit(solution)/shard_map/ppermute | solution.py:103
  118.2 11.0 %collective-permute-start.4 = (bf16[192,768]{1,0:T(8,128)(2,1)S(1)}, bf16[192,768]{1,0:T(8,128)(2,1)}, u32[]{:S(2)}, u32[]{:S(2)}) collective-permute-start(bf16[192,768]{1,0:T(8,128)(2,1)S(1)} %get-tuple-element.72), channel_id=1, source_target_pairs={{0,8},{2,10},{8,16},{10,18},{16,24},{18,26},{24,28},{26,30},{28,20... | collective-permute-start | bytes 884744 | tf_op jit(solution)/shard_map/ppermute | solution.py:103
  131.9 9.0 %collective-permute-start.17 = (bf16[192,768]{1,0:T(8,128)(2,1)}, bf16[192,768]{1,0:T(8,128)(2,1)}, u32[]{:S(2)}, u32[]{:S(2)}) collective-permute-start(bf16[192,768]{1,0:T(8,128)(2,1)} %get-tuple-element.65), channel_id=1, source_target_pairs={{0,4},{2,6},{8,0},{10,2},{16,8},{18,10},{24,16},{26,18},{28,24},{3... | collective-permute-start | bytes 884744 | tf_op jit(solution)/shard_map/ppermute | solution.py:103
  133.4 8.7 %collective-permute-start.13 = (bf16[192,768]{1,0:T(8,128)(2,1)}, bf16[192,768]{1,0:T(8,128)(2,1)}, u32[]{:S(2)}, u32[]{:S(2)}) collective-permute-start(bf16[192,768]{1,0:T(8,128)(2,1)} %get-tuple-element.66), channel_id=1, source_target_pairs={{0,8},{2,10},{8,16},{10,18},{16,24},{18,26},{24,28},{26,30},{28,20... | collective-permute-start | bytes 884744 | tf_op jit(solution)/shard_map/ppermute | solution.py:103
  133.9 10.1 %collective-permute-start.9 = (bf16[192,768]{1,0:T(8,128)(2,1)}, bf16[192,768]{1,0:T(8,128)(2,1)}, u32[]{:S(2)}, u32[]{:S(2)}) collective-permute-start(bf16[192,768]{1,0:T(8,128)(2,1)} %get-tuple-element.67), channel_id=1, source_target_pairs={{0,4},{2,6},{8,0},{10,2},{16,8},{18,10},{24,16},{26,18},{28,24},{3... | collective-permute-start | bytes 884744 | tf_op jit(solution)/shard_map/ppermute | solution.py:103
  135.5 9.8 %collective-permute-start.5 = (bf16[192,768]{1,0:T(8,128)(2,1)S(1)}, bf16[192,768]{1,0:T(8,128)(2,1)}, u32[]{:S(2)}, u32[]{:S(2)}) collective-permute-start(bf16[192,768]{1,0:T(8,128)(2,1)S(1)} %get-tuple-element.68), channel_id=1, source_target_pairs={{0,8},{2,10},{8,16},{10,18},{16,24},{18,26},{24,28},{26,30},{28,20... | collective-permute-start | bytes 884744 | tf_op jit(solution)/shard_map/ppermute | solution.py:103
  149.8 19.6 %collective-permute-start.23 = (bf16[512,3072]{0,1:T(8,128)(2,1)}, bf16[512,3072]{0,1:T(8,128)(2,1)}, u32[]{:S(2)}, u32[]{:S(2)}) collective-permute-start(bf16[512,3072]{0,1:T(8,128)(2,1)} %pad_maximum_fusion.1), channel_id=1, source_target_pairs={{0,2},{2,0},{4,6},{6,4},{8,10},{10,8},{12,14},{14,12},{16,18},{18,... | collective-permute-start | bytes 9437192 | tf_op jit(solution)/shard_map/ppermute | solution.py:75
  149.8 23.9 %collective-permute-start.28 = (bf16[512,1536]{1,0:T(8,128)(2,1)}, bf16[512,1536]{1,0:T(8,128)(2,1)}, u32[]{:S(2)}, u32[]{:S(2)}) collective-permute-start(bf16[512,1536]{1,0:T(8,128)(2,1)} %param.2), channel_id=1, source_target_pairs={{0,2},{2,0},{4,6},{6,4},{8,10},{10,8},{12,14},{14,12},{16,18},{18,... | collective-permute-start | bytes 4718600 | tf_op jit(solution)/shard_map/ppermute | solution.py:75
  150.3 10.0 %collective-permute-start.22 = (bf16[192,768]{1,0:T(8,128)(2,1)S(1)}, bf16[192,768]{1,0:T(8,128)(2,1)}, u32[]{:S(2)}, u32[]{:S(2)}) collective-permute-start(bf16[192,768]{1,0:T(8,128)(2,1)S(1)} %get-tuple-element.31), channel_id=1, source_target_pairs={{0,4},{2,6},{8,0},{10,2},{16,8},{18,10},{24,16},{26,18},{28,24},{3... | collective-permute-start | bytes 884744 | tf_op jit(solution)/shard_map/ppermute | solution.py:103
  151.7 9.0 %collective-permute-start.21 = (bf16[192,768]{1,0:T(8,128)(2,1)}, bf16[192,768]{1,0:T(8,128)(2,1)}, u32[]{:S(2)}, u32[]{:S(2)}) collective-permute-start(bf16[192,768]{1,0:T(8,128)(2,1)} %get-tuple-element.30), channel_id=1, source_target_pairs={{0,8},{2,10},{8,16},{10,18},{16,24},{18,26},{24,28},{26,30},{28,20... | collective-permute-start | bytes 884744 | tf_op jit(solution)/shard_map/ppermute | solution.py:103
  152.3 13.3 %collective-permute-start.20 = (bf16[192,768]{1,0:T(8,128)(2,1)}, bf16[192,768]{1,0:T(8,128)(2,1)}, u32[]{:S(2)}, u32[]{:S(2)}) collective-permute-start(bf16[192,768]{1,0:T(8,128)(2,1)} %get-tuple-element.29), channel_id=1, source_target_pairs={{0,4},{2,6},{8,0},{10,2},{16,8},{18,10},{24,16},{26,18},{28,24},{3... | collective-permute-start | bytes 884744 | tf_op jit(solution)/shard_map/ppermute | solution.py:103
  169.4 14.0 %collective-permute-start.27 = (bf16[192,768]{1,0:T(8,128)(2,1)S(1)}, bf16[192,768]{1,0:T(8,128)(2,1)S(1)}, u32[]{:S(2)}, u32[]{:S(2)}) collective-permute-start(bf16[192,768]{1,0:T(8,128)(2,1)S(1)} %get-tuple-element.36), channel_id=1, source_target_pairs={{0,4},{2,6},{8,0},{10,2},{16,8},{18,10},{24,16},{26,18},{28,24},{3... | collective-permute-start | bytes 884744 | tf_op jit(solution)/shard_map/ppermute | solution.py:103
  171.0 12.3 %collective-permute-start.26 = (bf16[192,768]{1,0:T(8,128)(2,1)S(1)}, bf16[192,768]{1,0:T(8,128)(2,1)S(1)}, u32[]{:S(2)}, u32[]{:S(2)}) collective-permute-start(bf16[192,768]{1,0:T(8,128)(2,1)S(1)} %get-tuple-element.35), channel_id=1, source_target_pairs={{0,8},{2,10},{8,16},{10,18},{16,24},{18,26},{24,28},{26,30},{28,20... | collective-permute-start | bytes 884744 | tf_op jit(solution)/shard_map/ppermute | solution.py:103
  171.6 11.7 %collective-permute-start.25 = (bf16[192,768]{1,0:T(8,128)(2,1)S(1)}, bf16[192,768]{1,0:T(8,128)(2,1)S(1)}, u32[]{:S(2)}, u32[]{:S(2)}) collective-permute-start(bf16[192,768]{1,0:T(8,128)(2,1)S(1)} %get-tuple-element.34), channel_id=1, source_target_pairs={{0,4},{2,6},{8,0},{10,2},{16,8},{18,10},{24,16},{26,18},{28,24},{3... | collective-permute-start | bytes 884744 | tf_op jit(solution)/shard_map/ppermute | solution.py:103
  173.1 10.3 %collective-permute-start.24 = (bf16[192,768]{1,0:T(8,128)(2,1)S(1)}, bf16[192,768]{1,0:T(8,128)(2,1)S(1)}, u32[]{:S(2)}, u32[]{:S(2)}) collective-permute-start(bf16[192,768]{1,0:T(8,128)(2,1)S(1)} %get-tuple-element.33), channel_id=1, source_target_pairs={{0,8},{2,10},{8,16},{10,18},{16,24},{18,26},{24,28},{26,30},{28,20... | collective-permute-start | bytes 884744 | tf_op jit(solution)/shard_map/ppermute | solution.py:103
  184.9 8.3 %collective-permute-start.41 = (bf16[192,768]{1,0:T(8,128)(2,1)S(1)}, bf16[192,768]{1,0:T(8,128)(2,1)S(1)}, u32[]{:S(2)}, u32[]{:S(2)}) collective-permute-start(bf16[192,768]{1,0:T(8,128)(2,1)S(1)} %get-tuple-element.40), channel_id=1, source_target_pairs={{0,8},{2,10},{8,16},{10,18},{16,24},{18,26},{24,28},{26,30},{28,20... | collective-permute-start | bytes 884744 | tf_op jit(solution)/shard_map/ppermute | solution.py:103
  187.0 9.4 %collective-permute-start.43 = (bf16[192,768]{1,0:T(8,128)(2,1)S(1)}, bf16[192,768]{1,0:T(8,128)(2,1)S(1)}, u32[]{:S(2)}, u32[]{:S(2)}) collective-permute-start(bf16[192,768]{1,0:T(8,128)(2,1)S(1)} %get-tuple-element.42), channel_id=1, source_target_pairs={{0,8},{2,10},{8,16},{10,18},{16,24},{18,26},{24,28},{26,30},{28,20... | collective-permute-start | bytes 884744 | tf_op jit(solution)/shard_map/ppermute | solution.py:103
  187.5 9.1 %collective-permute-start.42 = (bf16[192,768]{1,0:T(8,128)(2,1)S(1)}, bf16[192,768]{1,0:T(8,128)(2,1)S(1)}, u32[]{:S(2)}, u32[]{:S(2)}) collective-permute-start(bf16[192,768]{1,0:T(8,128)(2,1)S(1)} %get-tuple-element.41), channel_id=1, source_target_pairs={{0,4},{2,6},{8,0},{10,2},{16,8},{18,10},{24,16},{26,18},{28,24},{3... | collective-permute-start | bytes 884744 | tf_op jit(solution)/shard_map/ppermute | solution.py:103
  200.4 9.2 %collective-permute-start.35 = (bf16[96,1536]{1,0:T(8,128)(2,1)S(1)}, bf16[96,1536]{1,0:T(8,128)(2,1)S(1)}, u32[]{:S(2)}, u32[]{:S(2)}) collective-permute-start(bf16[96,1536]{1,0:T(8,128)(2,1)S(1)} %get-tuple-element.95), channel_id=1, source_target_pairs={{0,4},{2,6},{8,0},{10,2},{16,8},{18,10},{24,16},{26,18},{28,24},{3... | collective-permute-start | bytes 884744 | tf_op jit(solution)/shard_map/ppermute | solution.py:103
  202.0 10.9 %collective-permute-start.29 = (bf16[96,1536]{1,0:T(8,128)(2,1)S(1)}, bf16[96,1536]{1,0:T(8,128)(2,1)S(1)}, u32[]{:S(2)}, u32[]{:S(2)}) collective-permute-start(bf16[96,1536]{1,0:T(8,128)(2,1)S(1)} %get-tuple-element.96), channel_id=1, source_target_pairs={{0,8},{2,10},{8,16},{10,18},{16,24},{18,26},{24,28},{26,30},{28,20... | collective-permute-start | bytes 884744 | tf_op jit(solution)/shard_map/ppermute | solution.py:103
  214.2 16.3 %collective-permute-start.36 = (bf16[96,1536]{1,0:T(8,128)(2,1)S(1)}, bf16[96,1536]{1,0:T(8,128)(2,1)S(1)}, u32[]{:S(2)}, u32[]{:S(2)}) collective-permute-start(bf16[96,1536]{1,0:T(8,128)(2,1)S(1)} %get-tuple-element.93), channel_id=1, source_target_pairs={{0,4},{2,6},{8,0},{10,2},{16,8},{18,10},{24,16},{26,18},{28,24},{3... | collective-permute-start | bytes 884744 | tf_op jit(solution)/shard_map/ppermute | solution.py:103
  217.4 15.6 %collective-permute-start.30 = (bf16[96,1536]{1,0:T(8,128)(2,1)S(1)}, bf16[96,1536]{1,0:T(8,128)(2,1)S(1)}, u32[]{:S(2)}, u32[]{:S(2)}) collective-permute-start(bf16[96,1536]{1,0:T(8,128)(2,1)S(1)} %get-tuple-element.94), channel_id=1, source_target_pairs={{0,8},{2,10},{8,16},{10,18},{16,24},{18,26},{24,28},{26,30},{28,20... | collective-permute-start | bytes 884744 | tf_op jit(solution)/shard_map/ppermute | solution.py:103
  234.2 15.9 %collective-permute-start.37 = (bf16[96,1536]{1,0:T(8,128)(2,1)S(1)}, bf16[96,1536]{1,0:T(8,128)(2,1)S(1)}, u32[]{:S(2)}, u32[]{:S(2)}) collective-permute-start(bf16[96,1536]{1,0:T(8,128)(2,1)S(1)} %get-tuple-element.91), channel_id=1, source_target_pairs={{0,4},{2,6},{8,0},{10,2},{16,8},{18,10},{24,16},{26,18},{28,24},{3... | collective-permute-start | bytes 884744 | tf_op jit(solution)/shard_map/ppermute | solution.py:103
  234.3 15.9 %collective-permute-start.31 = (bf16[96,1536]{1,0:T(8,128)(2,1)S(1)}, bf16[96,1536]{1,0:T(8,128)(2,1)S(1)}, u32[]{:S(2)}, u32[]{:S(2)}) collective-permute-start(bf16[96,1536]{1,0:T(8,128)(2,1)S(1)} %get-tuple-element.92), channel_id=1, source_target_pairs={{0,8},{2,10},{8,16},{10,18},{16,24},{18,26},{24,28},{26,30},{28,20... | collective-permute-start | bytes 884744 | tf_op jit(solution)/shard_map/ppermute | solution.py:103
  251.4 16.3 %collective-permute-start.38 = (bf16[96,1536]{1,0:T(8,128)(2,1)S(1)}, bf16[96,1536]{1,0:T(8,128)(2,1)S(1)}, u32[]{:S(2)}, u32[]{:S(2)}) collective-permute-start(bf16[96,1536]{1,0:T(8,128)(2,1)S(1)} %get-tuple-element.89), channel_id=1, source_target_pairs={{0,4},{2,6},{8,0},{10,2},{16,8},{18,10},{24,16},{26,18},{28,24},{3... | collective-permute-start | bytes 884744 | tf_op jit(solution)/shard_map/ppermute | solution.py:103
  251.5 16.2 %collective-permute-start.32 = (bf16[96,1536]{1,0:T(8,128)(2,1)S(1)}, bf16[96,1536]{1,0:T(8,128)(2,1)S(1)}, u32[]{:S(2)}, u32[]{:S(2)}) collective-permute-start(bf16[96,1536]{1,0:T(8,128)(2,1)S(1)} %get-tuple-element.90), channel_id=1, source_target_pairs={{0,8},{2,10},{8,16},{10,18},{16,24},{18,26},{24,28},{26,30},{28,20... | collective-permute-start | bytes 884744 | tf_op jit(solution)/shard_map/ppermute | solution.py:103
  268.9 14.3 %collective-permute-start.39 = (bf16[96,1536]{1,0:T(8,128)(2,1)S(1)}, bf16[96,1536]{1,0:T(8,128)(2,1)S(1)}, u32[]{:S(2)}, u32[]{:S(2)}) collective-permute-start(bf16[96,1536]{1,0:T(8,128)(2,1)S(1)} %get-tuple-element.87), channel_id=1, source_target_pairs={{0,4},{2,6},{8,0},{10,2},{16,8},{18,10},{24,16},{26,18},{28,24},{3... | collective-permute-start | bytes 884744 | tf_op jit(solution)/shard_map/ppermute | solution.py:103
  269.6 14.4 %collective-permute-start.33 = (bf16[96,1536]{1,0:T(8,128)(2,1)S(1)}, bf16[96,1536]{1,0:T(8,128)(2,1)S(1)}, u32[]{:S(2)}, u32[]{:S(2)}) collective-permute-start(bf16[96,1536]{1,0:T(8,128)(2,1)S(1)} %get-tuple-element.88), channel_id=1, source_target_pairs={{0,8},{2,10},{8,16},{10,18},{16,24},{18,26},{24,28},{26,30},{28,20... | collective-permute-start | bytes 884744 | tf_op jit(solution)/shard_map/ppermute | solution.py:103
  273.8 13.4 %collective-permute-start.45 = (f32[2]{0:T(128)S(1)}, f32[2]{0:T(128)S(1)}, u32[]{:S(2)}, u32[]{:S(2)}) collective-permute-start(f32[2]{0:T(128)S(1)} %pad_maximum_fusion.4), channel_id=1, source_target_pairs={{0,2},{2,0},{4,6},{6,4},{8,10},{10,8},{12,14},{14,12},{16,18},{18,... | collective-permute-start | bytes 32 | tf_op jit(solution)/shard_map/ppermute | solution.py:114
  285.1 22.7 %collective-permute-start.40 = (bf16[96,1536]{1,0:T(8,128)(2,1)S(1)}, bf16[96,1536]{1,0:T(8,128)(2,1)S(1)}, u32[]{:S(2)}, u32[]{:S(2)}) collective-permute-start(bf16[96,1536]{1,0:T(8,128)(2,1)S(1)} %get-tuple-element.85), channel_id=1, source_target_pairs={{0,4},{2,6},{8,0},{10,2},{16,8},{18,10},{24,16},{26,18},{28,24},{3... | collective-permute-start | bytes 884744 | tf_op jit(solution)/shard_map/ppermute | solution.py:103
  285.4 22.5 %collective-permute-start.34 = (bf16[96,1536]{1,0:T(8,128)(2,1)S(1)}, bf16[96,1536]{1,0:T(8,128)(2,1)S(1)}, u32[]{:S(2)}, u32[]{:S(2)}) collective-permute-start(bf16[96,1536]{1,0:T(8,128)(2,1)S(1)} %get-tuple-element.86), channel_id=1, source_target_pairs={{0,8},{2,10},{8,16},{10,18},{16,24},{18,26},{24,28},{26,30},{28,20... | collective-permute-start | bytes 884744 | tf_op jit(solution)/shard_map/ppermute | solution.py:103
  288.5 10.1 %collective-permute-start.46 = (f32[2]{0:T(128)S(1)}, f32[2]{0:T(128)S(1)}, u32[]{:S(2)}, u32[]{:S(2)}) collective-permute-start(f32[2]{0:T(128)S(1)} %fusion.13), channel_id=1, source_target_pairs={{0,4},{2,6},{4,0},{6,2},{8,12},{10,14},{12,8},{14,10},{16,20},{18,... | collective-permute-start | bytes 32 | tf_op jit(solution)/shard_map/ppermute | solution.py:114
  309.1 13.1 %collective-permute-start.49 = (bf16[96,1536]{1,0:T(8,128)(2,1)S(1)}, bf16[96,1536]{1,0:T(8,128)(2,1)S(1)}, u32[]{:S(2)}, u32[]{:S(2)}) collective-permute-start(bf16[96,1536]{1,0:T(8,128)(2,1)S(1)} %get-tuple-element.45), channel_id=1, source_target_pairs={{0,8},{2,10},{8,16},{10,18},{16,24},{18,26},{24,28},{26,30},{28,20... | collective-permute-start | bytes 884744 | tf_op jit(solution)/shard_map/ppermute | solution.py:103
  310.6 13.0 %collective-permute-start.50 = (bf16[96,1536]{1,0:T(8,128)(2,1)S(1)}, bf16[96,1536]{1,0:T(8,128)(2,1)S(1)}, u32[]{:S(2)}, u32[]{:S(2)}) collective-permute-start(bf16[96,1536]{1,0:T(8,128)(2,1)S(1)} %get-tuple-element.46), channel_id=1, source_target_pairs={{0,4},{2,6},{8,0},{10,2},{16,8},{18,10},{24,16},{26,18},{28,24},{3... | collective-permute-start | bytes 884744 | tf_op jit(solution)/shard_map/ppermute | solution.py:103
  324.9 10.9 %collective-permute-start.51 = (bf16[96,3072]{1,0:T(8,128)(2,1)S(1)}, bf16[96,3072]{1,0:T(8,128)(2,1)S(1)}, u32[]{:S(2)}, u32[]{:S(2)}) collective-permute-start(bf16[96,3072]{1,0:T(8,128)(2,1)S(1)} %pad_maximum_fusion.3), channel_id=1, source_target_pairs={{0,1},{2,3},{4,5},{6,7},{8,9},{10,11},{12,13},{14,15},{16,17},{18,... | collective-permute-start | bytes 1769480 | tf_op jit(solution)/shard_map/ppermute | solution.py:172
  385.1 11.4 %collective-permute-start.52 = (bf16[192,192]{1,0:T(8,128)(2,1)}, bf16[192,192]{1,0:T(8,128)(2,1)S(1)}, u32[]{:S(2)}, u32[]{:S(2)}) collective-permute-start(bf16[192,192]{1,0:T(8,128)(2,1)} %bitcast.113), channel_id=1, source_target_pairs={{1,30},{3,0},{5,2},{7,4},{9,6},{11,8},{13,10},{15,12},{17,14},{19,... | collective-permute-start | bytes 221192 | tf_op jit(solution)/shard_map/ppermute | solution.py:188
  387.3 10.5 %collective-permute-start.53 = (bf16[192,192]{1,0:T(8,128)(2,1)S(1)}, bf16[192,192]{1,0:T(8,128)(2,1)S(1)}, u32[]{:S(2)}, u32[]{:S(2)}) collective-permute-start(bf16[192,192]{1,0:T(8,128)(2,1)S(1)} %bitcast.132), channel_id=1, source_target_pairs={{1,28},{3,30},{5,0},{7,2},{9,4},{11,6},{13,8},{15,10},{17,12},{19,... | collective-permute-start | bytes 221192 | tf_op jit(solution)/shard_map/ppermute | solution.py:188
  389.6 9.6 %collective-permute-start.54 = (bf16[192,192]{1,0:T(8,128)(2,1)S(1)}, bf16[192,192]{1,0:T(8,128)(2,1)S(1)}, u32[]{:S(2)}, u32[]{:S(2)}) collective-permute-start(bf16[192,192]{1,0:T(8,128)(2,1)S(1)} %bitcast.131), channel_id=1, source_target_pairs={{1,26},{3,28},{5,30},{7,0},{9,2},{11,4},{13,6},{15,8},{17,10},{19,... | collective-permute-start | bytes 221192 | tf_op jit(solution)/shard_map/ppermute | solution.py:188
  391.8 8.8 %collective-permute-start.55 = (bf16[192,192]{1,0:T(8,128)(2,1)S(1)}, bf16[192,192]{1,0:T(8,128)(2,1)S(1)}, u32[]{:S(2)}, u32[]{:S(2)}) collective-permute-start(bf16[192,192]{1,0:T(8,128)(2,1)S(1)} %bitcast.130), channel_id=1, source_target_pairs={{1,24},{3,26},{5,28},{7,30},{9,0},{11,2},{13,4},{15,6},{17,8},{19,... | collective-permute-start | bytes 221192 | tf_op jit(solution)/shard_map/ppermute | solution.py:188
  396.5 9.3 %collective-permute-start.57 = (bf16[192,192]{1,0:T(8,128)(2,1)S(1)}, bf16[192,192]{1,0:T(8,128)(2,1)S(1)}, u32[]{:S(2)}, u32[]{:S(2)}) collective-permute-start(bf16[192,192]{1,0:T(8,128)(2,1)S(1)} %bitcast.128), channel_id=1, source_target_pairs={{1,20},{3,22},{5,24},{7,26},{9,28},{11,30},{13,0},{15,2},{17,4},{1... | collective-permute-start | bytes 221192 | tf_op jit(solution)/shard_map/ppermute | solution.py:188
  397.9 9.3 %collective-permute-start.58 = (bf16[192,192]{1,0:T(8,128)(2,1)S(1)}, bf16[192,192]{1,0:T(8,128)(2,1)S(1)}, u32[]{:S(2)}, u32[]{:S(2)}) collective-permute-start(bf16[192,192]{1,0:T(8,128)(2,1)S(1)} %bitcast.127), channel_id=1, source_target_pairs={{1,18},{3,20},{5,22},{7,24},{9,26},{11,28},{13,30},{15,0},{17,2},{... | collective-permute-start | bytes 221192 | tf_op jit(solution)/shard_map/ppermute | solution.py:188
  399.2 24.2 %collective-permute-start.59 = (bf16[192,192]{1,0:T(8,128)(2,1)S(1)}, bf16[192,192]{1,0:T(8,128)(2,1)S(1)}, u32[]{:S(2)}, u32[]{:S(2)}) collective-permute-start(bf16[192,192]{1,0:T(8,128)(2,1)S(1)} %bitcast.126), channel_id=1, source_target_pairs={{1,16},{3,18},{5,20},{7,22},{9,24},{11,26},{13,28},{15,30},{17,0},... | collective-permute-start | bytes 221192 | tf_op jit(solution)/shard_map/ppermute | solution.py:188
  400.6 24.1 %collective-permute-start.60 = (bf16[192,192]{1,0:T(8,128)(2,1)S(1)}, bf16[192,192]{1,0:T(8,128)(2,1)S(1)}, u32[]{:S(2)}, u32[]{:S(2)}) collective-permute-start(bf16[192,192]{1,0:T(8,128)(2,1)S(1)} %bitcast.125), channel_id=1, source_target_pairs={{1,14},{3,16},{5,18},{7,20},{9,22},{11,24},{13,26},{15,28},{17,30}... | collective-permute-start | bytes 221192 | tf_op jit(solution)/shard_map/ppermute | solution.py:188
  401.9 24.1 %collective-permute-start.61 = (bf16[192,192]{1,0:T(8,128)(2,1)S(1)}, bf16[192,192]{1,0:T(8,128)(2,1)S(1)}, u32[]{:S(2)}, u32[]{:S(2)}) collective-permute-start(bf16[192,192]{1,0:T(8,128)(2,1)S(1)} %bitcast.124), channel_id=1, source_target_pairs={{1,12},{3,14},{5,16},{7,18},{9,20},{11,22},{13,24},{15,26},{17,28}... | collective-permute-start | bytes 221192 | tf_op jit(solution)/shard_map/ppermute | solution.py:188
  405.9 21.5 %collective-permute-start.62 = (bf16[192,192]{1,0:T(8,128)(2,1)S(1)}, bf16[192,192]{1,0:T(8,128)(2,1)S(1)}, u32[]{:S(2)}, u32[]{:S(2)}) collective-permute-start(bf16[192,192]{1,0:T(8,128)(2,1)S(1)} %bitcast.123), channel_id=1, source_target_pairs={{1,10},{3,12},{5,14},{7,16},{9,18},{11,20},{13,22},{15,24},{17,26}... | collective-permute-start | bytes 221192 | tf_op jit(solution)/shard_map/ppermute | solution.py:188
  407.2 21.5 %collective-permute-start.63 = (bf16[192,192]{1,0:T(8,128)(2,1)S(1)}, bf16[192,192]{1,0:T(8,128)(2,1)S(1)}, u32[]{:S(2)}, u32[]{:S(2)}) collective-permute-start(bf16[192,192]{1,0:T(8,128)(2,1)S(1)} %bitcast.122), channel_id=1, source_target_pairs={{1,8},{3,10},{5,12},{7,14},{9,16},{11,18},{13,20},{15,22},{17,24},... | collective-permute-start | bytes 221192 | tf_op jit(solution)/shard_map/ppermute | solution.py:188
  423.4 8.7 %collective-permute-start.64 = (bf16[192,192]{1,0:T(8,128)(2,1)S(1)}, bf16[192,192]{1,0:T(8,128)(2,1)S(1)}, u32[]{:S(2)}, u32[]{:S(2)}) collective-permute-start(bf16[192,192]{1,0:T(8,128)(2,1)S(1)} %bitcast.121), channel_id=1, source_target_pairs={{1,6},{3,8},{5,10},{7,12},{9,14},{11,16},{13,18},{15,20},{17,22},{... | collective-permute-start | bytes 221192 | tf_op jit(solution)/shard_map/ppermute | solution.py:188
  424.7 11.1 %collective-permute-start.65 = (bf16[192,192]{1,0:T(8,128)(2,1)S(1)}, bf16[192,192]{1,0:T(8,128)(2,1)S(1)}, u32[]{:S(2)}, u32[]{:S(2)}) collective-permute-start(bf16[192,192]{1,0:T(8,128)(2,1)S(1)} %bitcast.120), channel_id=1, source_target_pairs={{1,4},{3,6},{5,8},{7,10},{9,12},{11,14},{13,16},{15,18},{17,20},{1... | collective-permute-start | bytes 221192 | tf_op jit(solution)/shard_map/ppermute | solution.py:188
  426.1 10.2 %collective-permute-start.66 = (bf16[192,192]{1,0:T(8,128)(2,1)S(1)}, bf16[192,192]{1,0:T(8,128)(2,1)S(1)}, u32[]{:S(2)}, u32[]{:S(2)}) collective-permute-start(bf16[192,192]{1,0:T(8,128)(2,1)S(1)} %bitcast.119), channel_id=1, source_target_pairs={{1,2},{3,4},{5,6},{7,8},{9,10},{11,12},{13,14},{15,16},{17,18},{19... | collective-permute-start | bytes 221192 | tf_op jit(solution)/shard_map/ppermute | solution.py:188
  427.4 10.5 %collective-permute-start.67 = (bf16[192,192]{1,0:T(8,128)(2,1)S(1)}, bf16[192,192]{1,0:T(8,128)(2,1)S(1)}, u32[]{:S(2)}, u32[]{:S(2)}) collective-permute-start(bf16[192,192]{1,0:T(8,128)(2,1)S(1)} %bitcast.118), channel_id=1, source_target_pairs={{1,0},{3,2},{5,4},{7,6},{9,8},{11,10},{13,12},{15,14},{17,16},{19,... | collective-permute-start | bytes 221192 | tf_op jit(solution)/shard_map/ppermute | solution.py:188
  489.6 22.6 %collective-permute-start.68 = (bf16[192,1536]{1,0:T(8,128)(2,1)S(1)}, bf16[192,1536]{1,0:T(8,128)(2,1)S(1)}, u32[]{:S(2)}, u32[]{:S(2)}) collective-permute-start(bf16[192,1536]{1,0:T(8,128)(2,1)S(1)} %dynamic_slice.296), channel_id=1, source_target_pairs={{0,1},{2,3},{4,5},{6,7},{8,9},{10,11},{12,13},{14,15},{16,17},{18,... | collective-permute-start | bytes 1769480 | tf_op jit(solution)/shard_map/ppermute | solution.py:197
  (16 other events, 110.4 us)
Sparse Core Ops, SparseCore 0:
  199.4 137.4 all-gather.1
